TPU v7x, 32 devices: a whole 2x2x4 slice. The times are simulated.
32 devices in a mesh: dp: 16 (over z, y, x), section: 2 (over core).
Axes of the slice: x: 2, y: 2, z: 4, core: 2. Of those that a mesh axis runs over, the one named last changes fastest.
Arguments:
- tokens: bfloat16 [32, 1024, 1024], P('dp'), may hold values from -6 to 6
- seq_length: int32 [32], P('dp'), may hold values from 256 to 1024, as said below
- cotangent: bfloat16 [32, 1024, 1024], P('dp'), may hold values from -6 to 6
- ln_gain: bfloat16 [2, 2, 1024], P('section'), may hold values from 0.25 to 1.75
- ln_bias: bfloat16 [2, 2, 1024], P('section'), may hold values from -1.796875 to 1.796875
- w_qkv: bfloat16 [2, 1024, 3072], P('section', 'dp'), may hold values from -0.1875 to 0.1875
- w_out: bfloat16 [2, 1024, 1024], P('section', 'dp'), may hold values from -2 to 2
- w_fc: bfloat16 [2, 1024, 4096], P('section', 'dp'), may hold values from -0.1875 to 0.1875
- w_proj: bfloat16 [2, 4096, 1024], P('section', 'dp'), may hold values from -0.09375 to 0.09375
- prefix_table: bfloat16 [10, 1024], replicated, may hold values from -6 to 6
- reparam_w1: bfloat16 [1024, 512], replicated, may hold values from -0.1875 to 0.1875
- reparam_b1: bfloat16 [512], replicated, may hold values from -3 to 3
- reparam_w2: bfloat16 [2, 512, 2048], P('section'), may hold values from -0.25 to 0.25
- reparam_b2: bfloat16 [2, 2048], P('section'), may hold values from -3 to 3
Outputs:
- activations: bfloat16 [2, 32, 1024, 1024], P('section', 'dp')
- input_grads: bfloat16 [2, 32, 1024, 1024], P('section', 'dp')
- grad_table: float32 [10, 1024], replicated
- grad_w1: float32 [1024, 512], replicated
- grad_b1: float32 [512], replicated
- grad_w2: float32 [2, 512, 2048], P('section')
- grad_b2: float32 [2, 2048], P('section')
Inputs may be any that keep to these rules, and one draw needn't show every extreme that they name: `seq_length`: each row holds either one sequence of 1024 positions or four sequences of 256; both kinds occur in every draw.
All inputs are finite; a program needn't handle non-finite values.
Results may differ from a plain program's by a relative error of at most 0.015.
Values may be sent and summed in bfloat16 or wider, within the bound.
No kernel may reach another device: no remote copies, remote signals or barrier semaphores. Data moves between devices by JAX's collectives and lax.ppermute only.
A program may use at most 320 MiB of HBM per device.

v0:
```python
import jax
import jax.numpy as jnp
from jax import lax
from jax.sharding import PartitionSpec as P

D = 1024
HEADS = 16
HEAD_DIM = 64
PREFIX = 10


eps_norm = 1e-05
neg_big = -1e30
highest_mode = lax.Precision.HIGHEST


def passed_along(shard, axis, by):
    size = lax.axis_size(axis)
    pairs = [(i, i + by) for i in range(size) if 0 <= i + by < size]
    return lax.ppermute(shard, axis, pairs)


def layer_norm(values, gain, offset):
    centre = jnp.mean(values, axis=-1, keepdims=True)
    spread = values - centre
    variance = jnp.mean(spread * spread, axis=-1, keepdims=True)
    return spread * lax.rsqrt(variance + eps_norm) * gain + offset


def norm_back(values, gain, offset, upstream):
    return jax.vjp(lambda inputs: layer_norm(inputs, gain, offset), values)[1](upstream)[0]


def gelu_tanh(values):
    return jax.nn.gelu(values, approximate=True)


def split_heads(matrix):
    return matrix.reshape(matrix.shape[0], HEADS, HEAD_DIM)


def block_scores(query_block, key_rows, prefix_keys, block_start, segment):
    block_size = query_block.shape[0]
    block_stop = block_start + block_size
    scale_factor = HEAD_DIM ** (-0.5)
    row_part = jnp.einsum(
        "qhd,khd->hqk", query_block, key_rows[:block_stop], preferred_element_type=jnp.float32
    )
    prefix_part = jnp.einsum(
        "qhd,khd->hqk", query_block, prefix_keys, preferred_element_type=jnp.float32
    )
    query_pos = block_start + jnp.arange(block_size, dtype=jnp.int32)
    key_pos = jnp.arange(block_stop, dtype=jnp.int32)
    allowed = (key_pos[None, :] <= query_pos[:, None]) & (
        segment[:block_stop][None, :] == segment[block_start:block_stop][:, None]
    )
    return (jnp.where(allowed[None], row_part * scale_factor, neg_big), prefix_part * scale_factor)


def split_projected(projected):
    return tuple(
        (
            split_heads(projected[:, column_part * D : (column_part + 1) * D])
            for column_part in range(3)
        )
    )


def attend(projected, prefix_pair, segment):
    length = projected.shape[0]
    block_size = min(512, length)
    queries, key_rows, value_rows = split_projected(projected)
    prefix_keys, prefix_values = prefix_pair
    outputs = []
    log_sums = []
    for block_index in range(length // block_size):
        block_start = block_index * block_size
        block_stop = block_start + block_size
        row_scores, prefix_scores = block_scores(
            queries[block_start:block_stop], key_rows, prefix_keys, block_start, segment
        )
        row_max = jnp.maximum(
            jnp.max(row_scores, axis=-1, keepdims=True),
            jnp.max(prefix_scores, axis=-1, keepdims=True),
        )
        row_exp = jnp.exp(row_scores - row_max)
        prefix_exp = jnp.exp(prefix_scores - row_max)
        denominator = jnp.sum(row_exp, axis=-1, keepdims=True) + jnp.sum(
            prefix_exp, axis=-1, keepdims=True
        )
        block_out = jnp.einsum(
            "hqk,khd->qhd",
            (row_exp / denominator).astype(jnp.bfloat16),
            value_rows[:block_stop],
            preferred_element_type=jnp.float32,
        )
        block_out = block_out + jnp.einsum(
            "hqk,khd->qhd",
            (prefix_exp / denominator).astype(jnp.bfloat16),
            prefix_values,
            preferred_element_type=jnp.float32,
        )
        outputs.append(block_out)
        log_sums.append(row_max + jnp.log(denominator))
    attended = jnp.concatenate(outputs, axis=0).reshape(length, D).astype(jnp.bfloat16)
    return (attended, log_sums)


def attend_back(projected, prefix_pair, segment, log_sums, grad_attended):
    length = projected.shape[0]
    block_size = min(512, length)
    scale_factor = HEAD_DIM ** (-0.5)
    queries, key_rows, value_rows = split_projected(projected)
    prefix_keys, prefix_values = prefix_pair
    grad_out = split_heads(grad_attended)
    grad_query_blocks = []
    grad_keys = jnp.zeros(key_rows.shape, jnp.float32)
    grad_values = jnp.zeros(value_rows.shape, jnp.float32)
    grad_prefix_keys = jnp.zeros(prefix_keys.shape, jnp.float32)
    grad_prefix_values = jnp.zeros(prefix_values.shape, jnp.float32)
    for block_index in range(length // block_size):
        block_start = block_index * block_size
        block_stop = block_start + block_size
        query_block = queries[block_start:block_stop]
        grad_block = grad_out[block_start:block_stop]
        row_scores, prefix_scores = block_scores(
            query_block, key_rows, prefix_keys, block_start, segment
        )
        row_probs = jnp.exp(row_scores - log_sums[block_index])
        prefix_probs = jnp.exp(prefix_scores - log_sums[block_index])
        row_dprob = jnp.einsum(
            "qhd,khd->hqk", grad_block, value_rows[:block_stop], preferred_element_type=jnp.float32
        )
        prefix_dprob = jnp.einsum(
            "qhd,khd->hqk", grad_block, prefix_values, preferred_element_type=jnp.float32
        )
        centre = jnp.sum(row_probs * row_dprob, axis=-1, keepdims=True) + jnp.sum(
            prefix_probs * prefix_dprob, axis=-1, keepdims=True
        )
        row_grad = (row_probs * (row_dprob - centre) * scale_factor).astype(jnp.bfloat16)
        prefix_grad = (prefix_probs * (prefix_dprob - centre) * scale_factor).astype(jnp.bfloat16)
        grad_query_blocks.append(
            jnp.einsum(
                "hqk,khd->qhd", row_grad, key_rows[:block_stop], preferred_element_type=jnp.float32
            )
            + jnp.einsum(
                "hqk,khd->qhd", prefix_grad, prefix_keys, preferred_element_type=jnp.float32
            )
        )
        grad_keys = grad_keys.at[:block_stop].add(
            jnp.einsum("hqk,qhd->khd", row_grad, query_block, preferred_element_type=jnp.float32)
        )
        grad_values = grad_values.at[:block_stop].add(
            jnp.einsum(
                "hqk,qhd->khd",
                row_probs.astype(jnp.bfloat16),
                grad_block,
                preferred_element_type=jnp.float32,
            )
        )
        grad_prefix_keys = grad_prefix_keys + jnp.einsum(
            "hqk,qhd->khd", prefix_grad, query_block, preferred_element_type=jnp.float32
        )
        grad_prefix_values = grad_prefix_values + jnp.einsum(
            "hqk,qhd->khd",
            prefix_probs.astype(jnp.bfloat16),
            grad_block,
            preferred_element_type=jnp.float32,
        )
    grad_projected = jnp.concatenate(
        [
            jnp.concatenate(grad_query_blocks, axis=0).reshape(length, D),
            grad_keys.reshape(length, D),
            grad_values.reshape(length, D),
        ],
        axis=1,
    ).astype(jnp.bfloat16)
    grad_prefix = jnp.concatenate(
        [grad_prefix_keys.reshape(PREFIX, D), grad_prefix_values.reshape(PREFIX, D)], axis=1
    )
    return (grad_projected, grad_prefix)


def forward_parts(hidden_in, segment, weights, prefix_pair):
    gain_pair, offset_pair, w_qkv, w_out, w_fc, w_proj = weights
    start_values = hidden_in.astype(jnp.float32)
    normed = layer_norm(start_values, gain_pair[0], offset_pair[0]).astype(jnp.bfloat16)
    projected = jnp.dot(normed, w_qkv, preferred_element_type=jnp.float32).astype(jnp.bfloat16)
    attended, log_sums = attend(projected, prefix_pair, segment)
    middle = start_values + jnp.dot(attended, w_out, preferred_element_type=jnp.float32)
    normed_two = layer_norm(middle, gain_pair[1], offset_pair[1]).astype(jnp.bfloat16)
    inner_act = jnp.dot(normed_two, w_fc, preferred_element_type=jnp.float32)
    activated = gelu_tanh(inner_act).astype(jnp.bfloat16)
    layer_out = (middle + jnp.dot(activated, w_proj, preferred_element_type=jnp.float32)).astype(
        jnp.bfloat16
    )
    return (layer_out, (start_values, projected, log_sums, middle, inner_act))


def layer_forward(hidden_in, segment, weights, prefix_pair):
    return forward_parts(hidden_in, segment, weights, prefix_pair)[0]


def layer_backward(hidden_in, upstream, segment, weights, prefix_pair):
    gain_pair, offset_pair, w_qkv, w_out, w_fc, w_proj = weights
    layer_out, kept_values = forward_parts(hidden_in, segment, weights, prefix_pair)
    start_values, projected, log_sums, middle, inner_act = kept_values
    grad_act = jnp.dot(upstream, w_proj.T, preferred_element_type=jnp.float32)
    grad_inner = jax.vjp(gelu_tanh, inner_act)[1](grad_act)[0].astype(jnp.bfloat16)
    grad_normed_two = jnp.dot(grad_inner, w_fc.T, preferred_element_type=jnp.float32)
    grad_middle = upstream.astype(jnp.float32) + norm_back(
        middle, gain_pair[1], offset_pair[1], grad_normed_two
    )
    grad_attended = jnp.dot(
        grad_middle.astype(jnp.bfloat16), w_out.T, preferred_element_type=jnp.float32
    ).astype(jnp.bfloat16)
    grad_projected, grad_prefix = attend_back(
        projected, prefix_pair, segment, log_sums, grad_attended
    )
    grad_normed = jnp.dot(grad_projected, w_qkv.T, preferred_element_type=jnp.float32)
    grad_in = grad_middle + norm_back(start_values, gain_pair[0], offset_pair[0], grad_normed)
    return (grad_in.astype(jnp.bfloat16), grad_prefix)


def reparam_hidden(table, w_first, b_first):
    return jnp.tanh(jnp.dot(table, w_first, precision=highest_mode) + b_first)


def reparam_out(hidden_units, w_second, b_second):
    return jnp.dot(hidden_units, w_second, precision=highest_mode) + b_second


def per_device(
    tokens,
    seq_length,
    cotangent,
    ln_gain,
    ln_bias,
    w_qkv,
    w_out,
    w_fc,
    w_proj,
    prefix_table,
    reparam_w1,
    reparam_b1,
    reparam_w2,
    reparam_b2,
):
    section_index = lax.axis_index("section")
    last_section = lax.axis_size("section") - 1
    micro_count = tokens.shape[0]
    row_length = tokens.shape[1]
    tick_count = micro_count + last_section
    norm_pair = (ln_gain[0].astype(jnp.float32), ln_bias[0].astype(jnp.float32))
    gathered = (
        lax.all_gather(w_qkv, "dp", axis=1, tiled=True),
        lax.all_gather(w_out, "dp", axis=1, tiled=True),
        lax.all_gather(w_fc, "dp", axis=1, tiled=True),
        lax.all_gather(w_proj, "dp", axis=1, tiled=True),
    )
    forward_weights = norm_pair + tuple((matrix[0] for matrix in gathered))
    table_values = prefix_table.astype(jnp.float32)
    first_weight = reparam_w1.astype(jnp.float32)
    first_bias = reparam_b1.astype(jnp.float32)
    second_weight = reparam_w2[0].astype(jnp.float32)
    second_bias = reparam_b2[0].astype(jnp.float32)
    hidden_units = reparam_hidden(table_values, first_weight, first_bias)
    prefix_kv = reparam_out(hidden_units, second_weight, second_bias).astype(jnp.bfloat16)
    prefix_pair = (split_heads(prefix_kv[:, :D]), split_heads(prefix_kv[:, D:]))
    positions = jnp.arange(row_length, dtype=jnp.int32)
    empty_rows = jnp.zeros(tokens.shape, jnp.bfloat16)
    start_rows = jnp.zeros(tokens.shape[1:], jnp.bfloat16)
    prefix_zero = jnp.zeros((PREFIX, 2 * D), jnp.float32)

    def forward_tick(time_step, state_pack):
        received, stored, produced = state_pack
        micro_index = time_step - section_index
        active_flag = (micro_index >= 0) & (micro_index < micro_count)
        micro_slot = jnp.clip(micro_index, 0, micro_count - 1)
        own_rows = lax.dynamic_index_in_dim(
            tokens, jnp.minimum(time_step, micro_count - 1), 0, keepdims=False
        )
        layer_in = jnp.where(section_index == 0, own_rows, received)
        segment = positions // lax.dynamic_index_in_dim(seq_length, micro_slot, 0, keepdims=False)
        layer_out = lax.cond(
            active_flag,
            lambda inputs: layer_forward(inputs, segment, forward_weights, prefix_pair),
            jnp.zeros_like,
            layer_in,
        )
        stored_old = lax.dynamic_index_in_dim(stored, micro_slot, 0, keepdims=False)
        stored = lax.dynamic_update_index_in_dim(
            stored, jnp.where(active_flag, layer_in, stored_old), micro_slot, 0
        )
        produced_old = lax.dynamic_index_in_dim(produced, micro_slot, 0, keepdims=False)
        produced = lax.dynamic_update_index_in_dim(
            produced, jnp.where(active_flag, layer_out, produced_old), micro_slot, 0
        )
        received = passed_along(layer_out, "section", 1)
        return (received, stored, produced)

    received, stored, produced = lax.fori_loop(
        0, tick_count, forward_tick, (start_rows, empty_rows, empty_rows)
    )

    def backward_tick(time_step, state_pack):
        received, returned, prefix_local, prefix_total = state_pack
        micro_index = time_step - last_section + section_index
        active_flag = (micro_index >= 0) & (micro_index < micro_count)
        micro_slot = jnp.clip(micro_index, 0, micro_count - 1)
        own_rows = lax.dynamic_index_in_dim(
            cotangent, jnp.minimum(time_step, micro_count - 1), 0, keepdims=False
        )
        upstream = jnp.where(section_index == last_section, own_rows, received)
        segment = positions // lax.dynamic_index_in_dim(seq_length, micro_slot, 0, keepdims=False)
        layer_in = lax.dynamic_index_in_dim(stored, micro_slot, 0, keepdims=False)
        grad_in, grad_prefix = lax.cond(
            active_flag,
            lambda operands: layer_backward(
                operands[0], operands[1], segment, forward_weights, prefix_pair
            ),
            lambda operands: (jnp.zeros_like(operands[0]), prefix_zero),
            (layer_in, upstream),
        )
        returned_old = lax.dynamic_index_in_dim(returned, micro_slot, 0, keepdims=False)
        returned = lax.dynamic_update_index_in_dim(
            returned, jnp.where(active_flag, grad_in, returned_old), micro_slot, 0
        )
        prefix_total = prefix_total + lax.psum(grad_prefix, "dp")
        received = passed_along(grad_in, "section", -1)
        return (received, returned, prefix_local, prefix_total)

    received, returned, prefix_local, prefix_total = lax.fori_loop(
        0, tick_count, backward_tick, (start_rows, empty_rows, prefix_zero, prefix_zero)
    )
    grad_hidden, grad_w2, grad_b2 = jax.vjp(reparam_out, hidden_units, second_weight, second_bias)[
        1
    ](prefix_total)
    grad_hidden = lax.psum(grad_hidden, "section")
    grad_table, grad_w1, grad_b1 = jax.vjp(reparam_hidden, table_values, first_weight, first_bias)[
        1
    ](grad_hidden)
    return (
        produced[None],
        returned[None],
        grad_table,
        grad_w1,
        grad_b1,
        grad_w2[None],
        grad_b2[None],
    )


def solution(mesh):
    in_specs = (
        P("dp", None, None),
        P("dp"),
        P("dp", None, None),
        P("section", None, None),
        P("section", None, None),
        P("section", "dp", None),
        P("section", "dp", None),
        P("section", "dp", None),
        P("section", "dp", None),
        P(),
        P(),
        P(),
        P("section", None, None),
        P("section", None),
    )
    out_specs = (
        P("section", "dp", None, None),
        P("section", "dp", None, None),
        P(),
        P(),
        P(),
        P("section", None, None),
        P("section", None),
    )
    return jax.shard_map(
        per_device, mesh=mesh, in_specs=in_specs, out_specs=out_specs, check_vma=False
    )
```

profile of v0, /device:TPU:0, one launch (start us, length us, event | category | flops | bytes accessed | tf_op | source)
XLA Modules:
  0.0 2406.1 jit_solution(6338666877473098938)
XLA Ops:
  22.8 51.4 %all-gather.7.cloned.1.call-done = bf16[1,1024,1024]{2,1,0:T(8,128)(2,1)} async-done(((bf16[1,64,1024]{2,1,0:T(8,128)(2,1)}), bf16[1,1024,1024]{2,1,0:T(8,128)(2,1)}) %all-gather.7.cloned.1.call-update) | async-done | bytes 2097168 | tf_op jit(solution)/shard_map/all_gather | solution.py:257
  74.2 95.6 %all-gather.5.cloned.1.call-done = bf16[1,1024,3072]{2,1,0:T(8,128)(2,1)} async-done(((bf16[1,64,3072]{2,1,0:T(8,128)(2,1)}), bf16[1,1024,3072]{2,1,0:T(8,128)(2,1)}) %all-gather.5.cloned.1.call-update) | async-done | bytes 6291472 | tf_op jit(solution)/shard_map/all_gather | solution.py:256
  169.8 113.9 %all-gather.9.cloned.1.call-done = bf16[1,1024,4096]{2,1,0:T(8,128)(2,1)} async-done(((bf16[1,64,4096]{2,1,0:T(8,128)(2,1)}), bf16[1,1024,4096]{2,1,0:T(8,128)(2,1)}) %all-gather.9.cloned.1.call-update) | async-done | bytes 8388624 | tf_op jit(solution)/shard_map/all_gather | solution.py:258
  283.7 113.7 %all-gather.11.cloned.1.call-done = bf16[1,4096,1024]{2,1,0:T(8,128)(2,1)} async-done(((bf16[1,256,1024]{2,1,0:T(8,128)(2,1)}), bf16[1,4096,1024]{2,1,0:T(8,128)(2,1)}) %all-gather.11.cloned.1.call-update) | async-done | bytes 8388624 | tf_op jit(solution)/shard_map/all_gather | solution.py:259
  404.1 580.3 %while.49 = (s32[]{:T(128)}, bf16[1024,1024]{0,1:T(8,128)(2,1)}, bf16[2,1024,1024]{1,2,0:T(8,128)(2,1)}, bf16[2,1024,1024]{2,1,0:T(8,128)(2,1)}, s32[]{:T(128)},...) while((s32[]{:T(128)}, bf16[1024,1024]{0,1:T(8,128)(2,1)}, ...), condition=%wide.region_15.16_spmd.clone.clone, body=%wide.region_0.15_spmd.clone.clone.sunk | while | flops 29263998976 | bytes 399132960 | solution.py:302
  440.7 156.1 %conditional.8 = (bf16[1024,1024]{0,1:T(8,128)(2,1)}) conditional(s32[]{:T(128)} %convert_element_type.423, () %tuple.209, (bf16[1024,1024]{0,1:T(8,128)(2,1)}, f32[2,1024]{1,0:T(2,128)}, f32[2,1024]{1,0:T(2,128)}, bf16[1024,3072]{1,0:T(8,128)(2,1)}, s32[2]{0:T(128)}, /*index=5*/s32[]{:T(128)}, s32[1024]{0:T(1024)S(1)}, s32[1024]{0:T(1024)S(1)}, ...), branch_computations={%region_1.1_spmd, %region_2.14_spmd} | conditional | flops 29260853248 | bytes 336212320 | solution.py:285
  566.5 30.3 %add_convert_fusion = bf16[1024,1024]{0,1:T(8,128)(2,1)} fusion(f32[1024,1024]{0,1:T(8,128)} %copy-done.32, bf16[4096,1024]{1,0:T(8,128)(2,1)} %get-tuple-element.1302, bf16[1024,4096]{1,0:T(8,128)(2,1)} %get-tuple-element.1301, f32[1024]{0:T(1024)S(1)} %bitcast.296, f32[1024]{0:T(1024)S(1)} %bitcast.295, f32[1024]{0:T(1024)S(1)} %add_rsqrt_fusion, ...), kind=kOutput, calls=%fused_computation.36 | convolution fusion | flops 17224957952 | bytes 23085056 | tf_op jit(solution)/shard_map/while/body/eval_jaxpr/cond/branch_1_fun/dot_general | solution.py:194
  630.1 156.1 %conditional.8 = (bf16[1024,1024]{0,1:T(8,128)(2,1)}) conditional(s32[]{:T(128)} %convert_element_type.423, () %tuple.209, (bf16[1024,1024]{0,1:T(8,128)(2,1)}, f32[2,1024]{1,0:T(2,128)}, f32[2,1024]{1,0:T(2,128)}, bf16[1024,3072]{1,0:T(8,128)(2,1)}, s32[2]{0:T(128)}, /*index=5*/s32[]{:T(128)}, s32[1024]{0:T(1024)S(1)}, s32[1024]{0:T(1024)S(1)}, ...), branch_computations={%region_1.1_spmd, %region_2.14_spmd} | conditional | flops 29260853248 | bytes 336212320 | solution.py:285
  755.9 30.3 %add_convert_fusion = bf16[1024,1024]{0,1:T(8,128)(2,1)} fusion(f32[1024,1024]{0,1:T(8,128)} %copy-done.32, bf16[4096,1024]{1,0:T(8,128)(2,1)} %get-tuple-element.1302, bf16[1024,4096]{1,0:T(8,128)(2,1)} %get-tuple-element.1301, f32[1024]{0:T(1024)S(1)} %bitcast.296, f32[1024]{0:T(1024)S(1)} %bitcast.295, f32[1024]{0:T(1024)S(1)} %add_rsqrt_fusion, ...), kind=kOutput, calls=%fused_computation.36 | convolution fusion | flops 17224957952 | bytes 23085056 | tf_op jit(solution)/shard_map/while/body/eval_jaxpr/cond/branch_1_fun/dot_general | solution.py:194
  821.2 144.9 %collective-permute-start = (bf16[1024,1024]{0,1:T(8,128)(2,1)}, bf16[1024,1024]{0,1:T(8,128)(2,1)}, u32[]{:S(2)}, u32[]{:S(2)}) collective-permute-start(bf16[1024,1024]{0,1:T(8,128)(2,1)} %get-tuple-element.2114), channel_id=1, source_target_pairs={{0,1},{2,3},{4,5},{6,7},{8,9},{10,11},{12,13},{14,15},{16,17},{18,... | collective-permute-start | bytes 6291464 | tf_op jit(solution)/shard_map/while/body/eval_jaxpr/ppermute | solution.py:20
  988.6 1388.3 %while.50 = (s32[]{:T(128)}, bf16[1024,1024]{0,1:T(8,128)(2,1)}, bf16[2,1024,1024]{2,1,0:T(8,128)(2,1)}, f32[10,2048]{1,0:T(8,128)}, s32[]{:T(128)}, /*index=5*/...) while((s32[]{:T(128)}, bf16[1024,1024]{0,1:T(8,128)(2,1)}, ...), condition=%wide.region_40.41_spmd.clone.clone, body=%wide.region_16.40_spmd.clone.clone.sunk | while | flops 53163843584 | bytes 1047763264 | solution.py:333
  1017.5 428.4 %all-reduce.4.cloned.1.call-done = f32[10,2048]{1,0:T(8,128)} async-done(((f32[10,2048]{1,0:T(8,128)}), f32[10,2048]{1,0:T(8,128)}) %all-reduce.4.cloned.1.call-update) | async-done | bytes 81936 | tf_op jit(solution)/shard_map/while/body/eval_jaxpr/psum | solution.py:329
  1447.5 354.2 %conditional.9 = (bf16[1024,1024]{0,1:T(8,128)(2,1)}, f32[10,2048]{1,0:T(8,128)}) conditional(s32[]{:T(128)} %convert_element_type.424, () %tuple.212, (pred[]{:T(512)}, s32[]{:T(128)}, bf16[2,1024,1024]{1,2,0:T(8,128)(2,1)}, bf16[1024,1024]{0,1:T(8,128)(2,1)}, bf16[4096,1024]{1,0:T(8,128)(2,1)}, /*index=5*/bf16[2,1024,1024]{1,2,0:T(8,128)(2,1)}, ...), branch_computations={%region_17.17_spmd, %region_18.38_spmd} | conditional | flops 53162733568 | bytes 1014809920 | solution.py:317
  1495.3 16.2 fusion.197
  1589.0 27.5 %fusion.86.clone.4 = bf16[1024,4096]{1,0:T(8,128)(2,1)} fusion(f32[1024,4096]{1,0:T(8,128)} %fusion.197, bf16[1024,4096]{1,0:T(8,128)(2,1)} %get-tuple-element.1340, f32[1024,1024]{0,1:T(8,128)} %copy-done.17, f32[1024]{0:T(1024)S(1)} %bitcast.297, f32[1024]{0:T(1024)S(1)} %bitcast.292, f32[1024]{0:T(1024)S(1)} %fusion.158, ...), kind=kOutput, calls=%fused_computation.103.clone.clone.clone.clone.1 | convolution fusion | flops 8679063552 | bytes 37765120 | tf_op jit(solution)/shard_map/while/body/eval_jaxpr/cond/branch_1_fun/dot_general | solution.py:192
  1700.9 22.3 multiply_reduce_fusion.1
  1723.2 28.1 %multiply_convert_fusion = bf16[16,512,1024]{2,1,0:T(8,128)(2,1)} fusion(f32[16,512,1024]{2,1,0:T(8,128)} %get-tuple-element.1770, f32[16,512,1024]{2,1,0:T(8,128)} %get-tuple-element.1754, f32[16,512]{1,0:T(8,128)S(1)} %add.560, f32[16,512]{1,0:T(8,128)S(1)} %get-tuple-element.1706), kind=kLoop, calls=%fused_computation.87 | loop fusion | flops 41943040 | bytes 83951616 | tf_op jit(solution)/shard_map/while/body/eval_jaxpr/cond/branch_1_fun/convert_element_type | solution.py:140
  1821.0 87.6 %all-reduce.4.cloned.1.call-done = f32[10,2048]{1,0:T(8,128)} async-done(((f32[10,2048]{1,0:T(8,128)}), f32[10,2048]{1,0:T(8,128)}) %all-reduce.4.cloned.1.call-update) | async-done | bytes 81936 | tf_op jit(solution)/shard_map/while/body/eval_jaxpr/psum | solution.py:329
  1910.5 354.3 %conditional.9 = (bf16[1024,1024]{0,1:T(8,128)(2,1)}, f32[10,2048]{1,0:T(8,128)}) conditional(s32[]{:T(128)} %convert_element_type.424, () %tuple.212, (pred[]{:T(512)}, s32[]{:T(128)}, bf16[2,1024,1024]{1,2,0:T(8,128)(2,1)}, bf16[1024,1024]{0,1:T(8,128)(2,1)}, bf16[4096,1024]{1,0:T(8,128)(2,1)}, /*index=5*/bf16[2,1024,1024]{1,2,0:T(8,128)(2,1)}, ...), branch_computations={%region_17.17_spmd, %region_18.38_spmd} | conditional | flops 53162733568 | bytes 1014809920 | solution.py:317
  1958.5 16.2 fusion.197
  2051.9 27.5 %fusion.86.clone.4 = bf16[1024,4096]{1,0:T(8,128)(2,1)} fusion(f32[1024,4096]{1,0:T(8,128)} %fusion.197, bf16[1024,4096]{1,0:T(8,128)(2,1)} %get-tuple-element.1340, f32[1024,1024]{0,1:T(8,128)} %copy-done.17, f32[1024]{0:T(1024)S(1)} %bitcast.297, f32[1024]{0:T(1024)S(1)} %bitcast.292, f32[1024]{0:T(1024)S(1)} %fusion.158, ...), kind=kOutput, calls=%fused_computation.103.clone.clone.clone.clone.1 | convolution fusion | flops 8679063552 | bytes 37765120 | tf_op jit(solution)/shard_map/while/body/eval_jaxpr/cond/branch_1_fun/dot_general | solution.py:192
  2163.8 22.3 multiply_reduce_fusion.1
  2186.1 28.1 %multiply_convert_fusion = bf16[16,512,1024]{2,1,0:T(8,128)(2,1)} fusion(f32[16,512,1024]{2,1,0:T(8,128)} %get-tuple-element.1770, f32[16,512,1024]{2,1,0:T(8,128)} %get-tuple-element.1754, f32[16,512]{1,0:T(8,128)S(1)} %add.560, f32[16,512]{1,0:T(8,128)S(1)} %get-tuple-element.1706), kind=kLoop, calls=%fused_computation.87 | loop fusion | flops 41943040 | bytes 83951616 | tf_op jit(solution)/shard_map/while/body/eval_jaxpr/cond/branch_1_fun/convert_element_type | solution.py:140
  2284.0 87.6 %all-reduce.4.cloned.1.call-done = f32[10,2048]{1,0:T(8,128)} async-done(((f32[10,2048]{1,0:T(8,128)}), f32[10,2048]{1,0:T(8,128)}) %all-reduce.4.cloned.1.call-update) | async-done | bytes 81936 | tf_op jit(solution)/shard_map/while/body/eval_jaxpr/psum | solution.py:329
  (590 shorter events, 989.3 us)
Async XLA Ops:
  7.2 67.0 %all-gather.7.cloned.1.call-start = ((), (), s32[]{:S(2)}) async-start(), calls=%async_computation.1 | async-start | bytes 2228224 | tf_op jit(solution)/shard_map/all_gather | solution.py:257
  7.9 161.9 %all-gather.5.cloned.1.call-start = ((), (), s32[]{:S(2)}) async-start(), calls=%async_computation | async-start | bytes 6684672 | tf_op jit(solution)/shard_map/all_gather | solution.py:256
  8.7 275.1 %all-gather.9.cloned.1.call-start = ((), (), s32[]{:S(2)}) async-start(), calls=%async_computation.2 | async-start | bytes 8912896 | tf_op jit(solution)/shard_map/all_gather | solution.py:258
  9.4 388.0 %all-gather.11.cloned.1.call-start = ((), (), s32[]{:S(2)}) async-start(), calls=%async_computation.3 | async-start | bytes 8912896 | tf_op jit(solution)/shard_map/all_gather | solution.py:259
  596.8 20.4 collective-permute-start
  786.2 20.4 collective-permute-start
  821.2 162.1 %collective-permute-start = (bf16[1024,1024]{0,1:T(8,128)(2,1)}, bf16[1024,1024]{0,1:T(8,128)(2,1)}, u32[]{:S(2)}, u32[]{:S(2)}) collective-permute-start(bf16[1024,1024]{0,1:T(8,128)(2,1)} %get-tuple-element.2114), channel_id=1, source_target_pairs={{0,1},{2,3},{4,5},{6,7},{8,9},{10,11},{12,13},{14,15},{16,17},{18,... | collective-permute-start | bytes 6291464 | tf_op jit(solution)/shard_map/while/body/eval_jaxpr/ppermute | solution.py:20
  988.8 457.2 %all-reduce.4.cloned.1.call-start = ((), (), s32[]{:S(2)}) async-start(), calls=%async_computation.4 | async-start | bytes 262144 | tf_op jit(solution)/shard_map/while/body/eval_jaxpr/psum | solution.py:329
  998.9 448.0 %collective-permute-start.1 = (bf16[1024,1024]{0,1:T(8,128)(2,1)}, bf16[1024,1024]{0,1:T(8,128)(2,1)}, u32[]{:S(2)}, u32[]{:S(2)}) collective-permute-start(bf16[1024,1024]{0,1:T(8,128)(2,1)} %get-tuple-element.1988), channel_id=1, source_target_pairs={{1,0},{3,2},{5,4},{7,6},{9,8},{11,10},{13,12},{15,14},{17,16},{19,... | collective-permute-start | bytes 6291464 | tf_op jit(solution)/shard_map/while/body/eval_jaxpr/ppermute | solution.py:20
  1010.5 435.5 %copy-start.39 = (f32[10,2048]{1,0:T(8,128)S(1)}, f32[10,2048]{1,0:T(8,128)}, u32[]{:S(2)}) copy-start(f32[10,2048]{1,0:T(8,128)} %get-tuple-element.2075) | copy-start | bytes 245764 | tf_op jit(solution)/shard_map/while
  1447.5 461.0 %all-reduce.4.cloned.1.call-start = ((), (), s32[]{:S(2)}) async-start(), calls=%async_computation.4 | async-start | bytes 262144 | tf_op jit(solution)/shard_map/while/body/eval_jaxpr/psum | solution.py:329
  1482.5 56.3 %copy-start.1 = (bf16[512,1024]{0,1:T(8,128)(2,1)}, bf16[512,1024]{0,1:T(8,128)(2,1)S(1)}, u32[]{:S(2)}) copy-start(bf16[512,1024]{0,1:T(8,128)(2,1)S(1)} %copy.73) | copy-start | bytes 3145732 | tf_op jit(solution)/shard_map/while/body/eval_jaxpr/cond
  1495.3 16.2 copy-start.6
  1495.3 16.2 copy-start.19
  1723.2 29.6 %copy-start.2 = (bf16[512,1024]{0,1:T(8,128)(2,1)S(1)}, bf16[512,1024]{0,1:T(8,128)(2,1)}, u32[]{:S(2)}) copy-start(bf16[512,1024]{0,1:T(8,128)(2,1)} %copy-done.1) | copy-start | bytes 3145732 | tf_op jit(solution)/shard_map/while/body/eval_jaxpr/cond
  1801.8 107.8 %collective-permute-start.1 = (bf16[1024,1024]{0,1:T(8,128)(2,1)}, bf16[1024,1024]{0,1:T(8,128)(2,1)}, u32[]{:S(2)}, u32[]{:S(2)}) collective-permute-start(bf16[1024,1024]{0,1:T(8,128)(2,1)} %get-tuple-element.1988), channel_id=1, source_target_pairs={{1,0},{3,2},{5,4},{7,6},{9,8},{11,10},{13,12},{15,14},{17,16},{19,... | collective-permute-start | bytes 6291464 | tf_op jit(solution)/shard_map/while/body/eval_jaxpr/ppermute | solution.py:20
  1813.9 94.6 %copy-start.39 = (f32[10,2048]{1,0:T(8,128)S(1)}, f32[10,2048]{1,0:T(8,128)}, u32[]{:S(2)}) copy-start(f32[10,2048]{1,0:T(8,128)} %get-tuple-element.2075) | copy-start | bytes 245764 | tf_op jit(solution)/shard_map/while
  1910.4 461.2 %all-reduce.4.cloned.1.call-start = ((), (), s32[]{:S(2)}) async-start(), calls=%async_computation.4 | async-start | bytes 262144 | tf_op jit(solution)/shard_map/while/body/eval_jaxpr/psum | solution.py:329
  1945.7 56.0 %copy-start.1 = (bf16[512,1024]{0,1:T(8,128)(2,1)}, bf16[512,1024]{0,1:T(8,128)(2,1)S(1)}, u32[]{:S(2)}) copy-start(bf16[512,1024]{0,1:T(8,128)(2,1)S(1)} %copy.73) | copy-start | bytes 3145732 | tf_op jit(solution)/shard_map/while/body/eval_jaxpr/cond
  1958.5 16.2 copy-start.6
  1958.5 16.2 copy-start.19
  2186.0 29.6 %copy-start.2 = (bf16[512,1024]{0,1:T(8,128)(2,1)S(1)}, bf16[512,1024]{0,1:T(8,128)(2,1)}, u32[]{:S(2)}) copy-start(bf16[512,1024]{0,1:T(8,128)(2,1)} %copy-done.1) | copy-start | bytes 3145732 | tf_op jit(solution)/shard_map/while/body/eval_jaxpr/cond
  2264.7 107.8 %collective-permute-start.1 = (bf16[1024,1024]{0,1:T(8,128)(2,1)}, bf16[1024,1024]{0,1:T(8,128)(2,1)}, u32[]{:S(2)}, u32[]{:S(2)}) collective-permute-start(bf16[1024,1024]{0,1:T(8,128)(2,1)} %get-tuple-element.1988), channel_id=1, source_target_pairs={{1,0},{3,2},{5,4},{7,6},{9,8},{11,10},{13,12},{15,14},{17,16},{19,... | collective-permute-start | bytes 6291464 | tf_op jit(solution)/shard_map/while/body/eval_jaxpr/ppermute | solution.py:20
  2276.9 94.6 %copy-start.39 = (f32[10,2048]{1,0:T(8,128)S(1)}, f32[10,2048]{1,0:T(8,128)}, u32[]{:S(2)}) copy-start(f32[10,2048]{1,0:T(8,128)} %get-tuple-element.2075) | copy-start | bytes 245764 | tf_op jit(solution)/shard_map/while
  (112 other events, 719.7 us)
Sparse Core Ops, SparseCore 0:
  10.8 63.3 all-gather.6
  77.0 92.7 all-gather.4
  172.6 111.0 all-gather.8
  286.4 111.0 all-gather.10
  1000.4 445.5 all-reduce.3
  1803.2 105.3 all-reduce.3
  2266.2 105.3 all-reduce.3
where the time goes:
time: 2410 us
  waiting for transfers between devices  981 us (41%)
  matrix products  686 us (28%)
  other arithmetic  278 us (12%)
  local copies, waits for them, and re-layouts  247 us (10%)
  starting transfers between devices  154 us (6%)
  loops' own time  42.1 us (2%)
    psum x3, waiting for transfers between devices, backward_tick(): prefix_total = prefix_total + lax.psum(grad_prefix, 'dp')  604 us
    ppermute x6, starting transfers between devices, passed_along(): return lax.ppermute(shard, axis, pairs)  154 us
    all_gather x1, waiting for transfers between devices, per_device(): lax.all_gather(w_fc, 'dp', axis=1, tiled=True)  114 us
    all_gather x1, waiting for transfers between devices, per_device(): lax.all_gather(w_proj, 'dp', axis=1, tiled=True)  114 us
    all_gather x1, waiting for transfers between devices, per_device(): lax.all_gather(w_qkv, 'dp', axis=1, tiled=True)  95.6 us
    reduce_sum x8, other arithmetic, attend(): jnp.sum(row_exp, axis=-1, keepdims=True)  94 us
    dot_general x8, matrix products, attend(): jnp.einsum('hqk,khd->qhd', (row_exp / denominator).astype(jnp.bfloat16),...  92.9 us
    dot_general x8, matrix products, block_scores(): jnp.einsum('qhd,khd->hqk', query_block, key_rows[:block_stop], preferred_...  90.8 us
  transfers between devices with their start and end apart: 13, of which 7 were waited for; matrix products, arithmetic and copies ran while one was open for 5% of the time, Pallas kernels for 0%

commit v1 on v0

v1 whole, which is shorter than its diff:
```python
import functools

import jax
import jax.numpy as jnp
from jax import lax
from jax.experimental import pallas as pl
from jax.experimental.pallas import tpu as pltpu
from jax.sharding import PartitionSpec as P

D = 1024
HEADS = 16
HEAD_DIM = 64
FF = 4096
PREFIX = 10
SLOTS = 16
PAIRS = 8
PAIR_DIM = 128
BLOCK = 256

eps_norm = 1e-05
neg_big = -1e30
highest_mode = lax.Precision.HIGHEST
VMEM_BYTES = 62 * 2**20
F32 = jnp.float32
BF16 = jnp.bfloat16


def dot(left, right, dims):
    return lax.dot_general(left, right, (dims, ((), ())), preferred_element_type=F32)


def dot_nn(left, right):
    return dot(left, right, ((1,), (0,)))


def dot_nt(left, right):
    return dot(left, right, ((1,), (1,)))


def dot_tn(left, right):
    return dot(left, right, ((0,), (0,)))


def normalised(values):
    centre = jnp.mean(values, axis=-1, keepdims=True)
    spread = values - centre
    variance = jnp.mean(spread * spread, axis=-1, keepdims=True)
    inverse = lax.rsqrt(variance + eps_norm)
    return spread * inverse, inverse


def layer_norm(values, gain, offset):
    return normalised(values)[0] * gain + offset


def norm_back(values, gain, upstream):
    unit, inverse = normalised(values)
    scaled = upstream * gain
    mean_scaled = jnp.mean(scaled, axis=-1, keepdims=True)
    mean_unit = jnp.mean(scaled * unit, axis=-1, keepdims=True)
    return (scaled - mean_scaled - unit * mean_unit) * inverse


SQRT_2_PI = 0.7978845608028654
CUBIC = 0.044715


def gelu_pair(values):
    cubic_part = (SQRT_2_PI * CUBIC) * (values * values)
    half_tanh = 0.5 + 0.5 * jnp.tanh(values * (SQRT_2_PI + cubic_part))
    out = values * half_tanh
    slope = half_tanh + out * ((2.0 - 2.0 * half_tanh) * (SQRT_2_PI + 3.0 * cubic_part))
    return out, slope


def matrix_of(ref):
    block = ref[...]
    return block.reshape(-1, block.shape[-1])


def params(**kwargs):
    return pltpu.CompilerParams(vmem_limit_bytes=VMEM_BYTES, **kwargs)


def row_tiles(length, size):
    return [slice(start, start + size) for start in range(0, length, size)]


def qkv_kernel(spot_ref, hidden_ref, norm_ref, weight_ref, out_ref, normed):
    step = pl.program_id(0)

    @pl.when(step == 0)
    def _():
        gain, offset = norm_ref[0:1], norm_ref[2:3]
        for rows in row_tiles(hidden_ref.shape[1], 256):
            values = hidden_ref[0, rows].astype(F32)
            normed[rows] = layer_norm(values, gain, offset).astype(BF16)

    scale = jnp.where(step == 0, HEAD_DIM**-0.5, 1.0)
    weight = matrix_of(weight_ref)
    for rows in row_tiles(out_ref.shape[0], 512):
        out_ref[rows] = (dot_nn(normed[rows], weight) * scale).astype(BF16)


def project(spot, hidden, norms, weights):
    length = hidden.shape[1]
    array, shape, index = weights
    return pl.pallas_call(
        qkv_kernel,
        grid_spec=pltpu.PrefetchScalarGridSpec(
            num_scalar_prefetch=1,
            grid=(3,),
            in_specs=[
                pl.BlockSpec((1, length, D), lambda j, s: (s[0], 0, 0)),
                pl.BlockSpec((8, D), lambda j, s: (0, 0)),
                pl.BlockSpec(shape, lambda j, s: index(j)),
            ],
            out_specs=pl.BlockSpec((length, D), lambda j, s: (0, j)),
            scratch_shapes=[pltpu.VMEM((length, D), BF16)],
        ),
        out_shape=jax.ShapeDtypeStruct((length, 3 * D), BF16),
        compiler_params=params(),
        name="norm_project",
    )(spot, hidden, norms, array)


def lane_halves(block):
    lanes = lax.broadcasted_iota(jnp.int32, block.shape, 1)
    zero = jnp.zeros_like(block)
    return jnp.where(lanes < HEAD_DIM, block, zero), jnp.where(lanes < HEAD_DIM, zero, block)


def masked_scores(prefix_scores, row_scores, lone):
    slots = lax.broadcasted_iota(jnp.int32, prefix_scores.shape, 0)
    prefix_scores = jnp.where(slots < PREFIX, prefix_scores, neg_big)
    diagonal = row_scores[-BLOCK:]
    keys = lax.broadcasted_iota(jnp.int32, diagonal.shape, 0)
    queries = lax.broadcasted_iota(jnp.int32, diagonal.shape, 1)
    diagonal = jnp.where(keys <= queries, diagonal, neg_big)
    if row_scores.shape[0] > BLOCK:
        row_scores = jnp.concatenate([row_scores[:-BLOCK], diagonal], axis=0)
    else:
        row_scores = diagonal
    return prefix_scores, row_scores


def strip_product(keys_ref, right, first, stop):
    if first == 0:
        whole = dot_nt(keys_ref[0 : SLOTS + stop], right)
        return whole[:SLOTS], whole[SLOTS:]
    return (
        dot_nt(keys_ref[0:SLOTS], right),
        dot_nt(keys_ref[SLOTS + first : SLOTS + stop], right),
    )


def attend_kernel(
    short_ref, q_ref, k_ref, v_ref, kp_ref, vp_ref, out_ref, log_ref, keys_a, keys_b, values_t, probs_p
):
    length = q_ref.shape[0]
    for rows, source in ((slice(0, SLOTS), kp_ref), (slice(SLOTS, SLOTS + length), k_ref)):
        keys_a[rows], keys_b[rows] = lane_halves(source[...])
    values_t[...] = v_ref[...].T
    prefix_values = jnp.concatenate(lane_halves(vp_ref[...]), axis=0)

    def run(short):
        for index in range(length // BLOCK):
            rows = slice(index * BLOCK, (index + 1) * BLOCK)
            first = rows.start if short else 0
            queries = q_ref[rows]
            parts = []
            for head, keys in enumerate((keys_a, keys_b)):
                prefix_scores, row_scores = masked_scores(
                    *strip_product(keys, queries, first, rows.stop), short
                )
                top = jnp.maximum(
                    jnp.max(row_scores, axis=0, keepdims=True),
                    jnp.max(prefix_scores, axis=0, keepdims=True),
                )
                row_exp = jnp.exp(row_scores - top)
                prefix_exp = jnp.exp(prefix_scores - top)
                total = jnp.sum(row_exp, axis=0, keepdims=True) + jnp.sum(
                    prefix_exp, axis=0, keepdims=True
                )
                log_ref[0, head : head + 1, rows] = top + jnp.log(total)
                inverse = 1.0 / total
                probs_p[head * SLOTS : (head + 1) * SLOTS, rows] = (prefix_exp * inverse).astype(BF16)
                span = slice(head * HEAD_DIM, (head + 1) * HEAD_DIM)
                parts.append(
                    dot_nn(values_t[span, first : rows.stop], row_exp.astype(BF16)) * inverse
                )
            both = jnp.concatenate(parts, axis=0) + dot_tn(prefix_values, probs_p[:, rows])
            out_ref[rows] = both.T.astype(BF16)

    is_short = short_ref[0] < length
    pl.when(is_short)(lambda: run(True))
    pl.when(jnp.logical_not(is_short))(lambda: run(False))


def pair_spec(length, part):
    return pl.BlockSpec((length, PAIR_DIM), lambda p, s: (0, part * PAIRS + p))


def attend(seq, projected, prefix_keys, prefix_values):
    length = projected.shape[0]
    return pl.pallas_call(
        attend_kernel,
        grid_spec=pltpu.PrefetchScalarGridSpec(
            num_scalar_prefetch=1,
            grid=(PAIRS,),
            in_specs=[
                pair_spec(length, 0),
                pair_spec(length, 1),
                pair_spec(length, 2),
                pair_spec(SLOTS, 0),
                pair_spec(SLOTS, 0),
            ],
            out_specs=[
                pair_spec(length, 0),
                pl.BlockSpec((1, 8, length), lambda p, s: (p, 0, 0)),
            ],
            scratch_shapes=[
                pltpu.VMEM((SLOTS + length, PAIR_DIM), BF16),
                pltpu.VMEM((SLOTS + length, PAIR_DIM), BF16),
                pltpu.VMEM((PAIR_DIM, length), BF16),
                pltpu.VMEM((2 * SLOTS, length), BF16),
            ],
        ),
        out_shape=[
            jax.ShapeDtypeStruct((length, D), BF16),
            jax.ShapeDtypeStruct((PAIRS, 8, length), F32),
        ],
        compiler_params=params(),
        name="attend",
    )(seq, projected, projected, projected, prefix_keys, prefix_values)


def attend_back_kernel(
    short_ref,
    q_ref,
    k_ref,
    v_ref,
    out_ref,
    grad_ref,
    kp_ref,
    vp_ref,
    log_ref,
    grads_ref,
    dkp_ref,
    dvp_ref,
    keys_a,
    keys_b,
    values_a,
    values_b,
    keys_t,
    dk,
    dv,
    dq_t,
    ds_p,
):
    length = q_ref.shape[0]
    for rows, source in ((slice(0, SLOTS), kp_ref), (slice(SLOTS, SLOTS + length), k_ref)):
        keys_a[rows], keys_b[rows] = lane_halves(source[...])
    for rows, source in ((slice(0, SLOTS), vp_ref), (slice(SLOTS, SLOTS + length), v_ref)):
        values_a[rows], values_b[rows] = lane_halves(source[...])
    keys_t[...] = k_ref[...].T
    prefix_keys = jnp.concatenate(lane_halves(kp_ref[...]), axis=0)
    dk[...] = jnp.zeros_like(dk)
    dv[...] = jnp.zeros_like(dv)

    def run(short):
        for index in range(length // BLOCK):
            rows = slice(index * BLOCK, (index + 1) * BLOCK)
            first = rows.start if short else 0
            queries, grads = q_ref[rows], grad_ref[rows]
            query_halves, grad_halves = lane_halves(queries), lane_halves(grads)
            weighted_t = (grads.astype(F32) * out_ref[rows].astype(F32)).T
            for head in range(2):
                keys, values = ((keys_a, values_a), (keys_b, values_b))[head]
                span = slice(head * HEAD_DIM, (head + 1) * HEAD_DIM)
                prefix_scores, row_scores = masked_scores(
                    *strip_product(keys, queries, first, rows.stop), short
                )
                log_sum = log_ref[0, head : head + 1, rows]
                row_probs = jnp.exp(row_scores - log_sum)
                prefix_probs = jnp.exp(prefix_scores - log_sum)
                centre = jnp.sum(weighted_t[span], axis=0, keepdims=True)
                prefix_dprob, row_dprob = strip_product(values, grads, first, rows.stop)
                row_ds = (row_probs * (row_dprob - centre)).astype(BF16)
                prefix_ds = (prefix_probs * (prefix_dprob - centre)).astype(BF16)
                row_probs = row_probs.astype(BF16)
                prefix_probs = prefix_probs.astype(BF16)
                ds_p[head * SLOTS : (head + 1) * SLOTS, rows] = prefix_ds
                for total, row_part, prefix_part, right in (
                    (dk, row_ds, prefix_ds, query_halves[head]),
                    (dv, row_probs, prefix_probs, grad_halves[head]),
                ):
                    if first == 0:
                        left = jnp.concatenate([prefix_part, row_part], axis=0)
                        total[0 : SLOTS + rows.stop] += dot_nn(left, right)
                    else:
                        total[0:SLOTS] += dot_nn(prefix_part, right)
                        total[SLOTS + first : SLOTS + rows.stop] += dot_nn(row_part, right)
                dq_t[span, rows] = dot_nn(keys_t[span, first : rows.stop], row_ds)
            both = dq_t[:, rows] + dot_tn(prefix_keys, ds_p[:, rows])
            grads_ref[0, rows] = (both.T * HEAD_DIM**-0.5).astype(BF16)

    is_short = short_ref[0] < length
    pl.when(is_short)(lambda: run(True))
    pl.when(jnp.logical_not(is_short))(lambda: run(False))
    grads_ref[1] = dk[SLOTS:].astype(BF16)
    grads_ref[2] = dv[SLOTS:].astype(BF16)
    dkp_ref[...] = dk[:SLOTS]
    dvp_ref[...] = dv[:SLOTS]


def attend_back(seq, projected, attended, grad_attended, prefix_keys, prefix_values, log_sums):
    length = projected.shape[0]
    ext = (SLOTS + length, PAIR_DIM)
    return pl.pallas_call(
        attend_back_kernel,
        grid_spec=pltpu.PrefetchScalarGridSpec(
            num_scalar_prefetch=1,
            grid=(PAIRS,),
            in_specs=[
                pair_spec(length, 0),
                pair_spec(length, 1),
                pair_spec(length, 2),
                pair_spec(length, 0),
                pair_spec(length, 0),
                pair_spec(SLOTS, 0),
                pair_spec(SLOTS, 0),
                pl.BlockSpec((1, 8, length), lambda p, s: (p, 0, 0)),
            ],
            out_specs=[
                pl.BlockSpec((3, length, PAIR_DIM), lambda p, s: (0, 0, p)),
                pair_spec(SLOTS, 0),
                pair_spec(SLOTS, 0),
            ],
            scratch_shapes=[
                pltpu.VMEM(ext, BF16),
                pltpu.VMEM(ext, BF16),
                pltpu.VMEM(ext, BF16),
                pltpu.VMEM(ext, BF16),
                pltpu.VMEM((PAIR_DIM, length), BF16),
                pltpu.VMEM(ext, F32),
                pltpu.VMEM(ext, F32),
                pltpu.VMEM((PAIR_DIM, length), F32),
                pltpu.VMEM((2 * SLOTS, length), BF16),
            ],
        ),
        out_shape=[
            jax.ShapeDtypeStruct((3, length, D), BF16),
            jax.ShapeDtypeStruct((SLOTS, D), F32),
            jax.ShapeDtypeStruct((SLOTS, D), F32),
        ],
        compiler_params=params(),
        name="attend_back",
    )(
        seq,
        projected,
        projected,
        projected,
        attended,
        grad_attended,
        prefix_keys,
        prefix_values,
        log_sums,
    )


def forward_kernel(
    spot_ref,
    attended_ref,
    hidden_ref,
    norm_ref,
    w_out_ref,
    w_fc_ref,
    w_proj_ref,
    middle_ref,
    slope_ref,
    out_ref,
    normed,
    total,
):
    step = pl.program_id(0)
    length = attended_ref.shape[0]

    @pl.when(step == 0)
    def _():
        gain, offset = norm_ref[1:2], norm_ref[3:4]
        w_out = matrix_of(w_out_ref)
        for rows in row_tiles(length, 256):
            middle = hidden_ref[0, rows].astype(F32) + dot_nn(attended_ref[rows], w_out)
            middle_ref[rows] = middle
            total[rows] = middle
            normed[rows] = layer_norm(middle, gain, offset).astype(BF16)

    w_fc, w_proj = matrix_of(w_fc_ref), matrix_of(w_proj_ref)
    for rows in row_tiles(length, 256):
        activated, slope = gelu_pair(dot_nn(normed[rows], w_fc))
        slope_ref[rows] = slope.astype(BF16)
        total[rows] += dot_nn(activated.astype(BF16), w_proj)

    @pl.when(step == pl.num_programs(0) - 1)
    def _():
        out_ref[0] = total[...].astype(BF16)


def once(shape, index):
    return pl.BlockSpec(shape, index, pipeline_mode=pl.Buffered(1))


def forward_block(spot, attended, hidden, norms, w_out, w_fc, w_proj):
    length = attended.shape[0]
    whole = lambda j, s: (0, 0)
    return pl.pallas_call(
        forward_kernel,
        grid_spec=pltpu.PrefetchScalarGridSpec(
            num_scalar_prefetch=1,
            grid=(FF // D,),
            in_specs=[
                once((length, D), whole),
                once((1, length, D), lambda j, s: (s[0], 0, 0)),
                once((8, D), whole),
                once(w_out[1], lambda j, s: w_out[2](0)),
                pl.BlockSpec(w_fc[1], lambda j, s: w_fc[2](j)),
                pl.BlockSpec(w_proj[1], lambda j, s: w_proj[2](j)),
            ],
            out_specs=[
                once((length, D), whole),
                pl.BlockSpec((length, D), lambda j, s: (0, j)),
                once((1, length, D), lambda j, s: (0, 0, 0)),
            ],
            scratch_shapes=[pltpu.VMEM((length, D), BF16), pltpu.VMEM((length, D), F32)],
        ),
        out_shape=[
            jax.ShapeDtypeStruct((length, D), F32),
            jax.ShapeDtypeStruct((length, FF), BF16),
            jax.ShapeDtypeStruct((1, length, D), BF16),
        ],
        compiler_params=params(),
        name="forward_block",
    )(spot, attended, hidden, norms, w_out[0], w_fc[0], w_proj[0])


def finish_backward(upstream_ref, middle_ref, grad_total, norm_ref, w_out_ref, grad_middle_ref, grad_attended_ref):
    gain = norm_ref[1:2]
    w_out = matrix_of(w_out_ref)
    for rows in row_tiles(middle_ref.shape[0], 256):
        grad_middle = upstream_ref[0, rows].astype(F32) + norm_back(
            middle_ref[rows], gain, grad_total[rows]
        )
        grad_middle_ref[rows] = grad_middle
        grad_attended_ref[rows] = dot_nt(grad_middle.astype(BF16), w_out).astype(BF16)


def turn_kernel(
    spot_ref,
    attended_ref,
    hidden_ref,
    upstream_ref,
    norm_ref,
    w_out_ref,
    w_fc_ref,
    w_proj_ref,
    out_ref,
    grad_middle_ref,
    grad_attended_ref,
    normed,
    middle,
    total,
    grad_total,
):
    step = pl.program_id(0)
    length = attended_ref.shape[0]

    @pl.when(step == 0)
    def _():
        gain, offset = norm_ref[1:2], norm_ref[3:4]
        w_out = matrix_of(w_out_ref)
        for rows in row_tiles(length, 256):
            values = hidden_ref[0, rows].astype(F32) + dot_nn(attended_ref[rows], w_out)
            middle[rows] = values
            total[rows] = values
            normed[rows] = layer_norm(values, gain, offset).astype(BF16)
        grad_total[...] = jnp.zeros_like(grad_total)

    w_fc, w_proj = matrix_of(w_fc_ref), matrix_of(w_proj_ref)
    for rows in row_tiles(length, 256):
        inner = dot_nn(normed[rows], w_fc)
        grad_act = dot_nt(upstream_ref[0, rows], w_proj)
        activated, slope = gelu_pair(inner)
        total[rows] += dot_nn(activated.astype(BF16), w_proj)
        grad_total[rows] += dot_nt((grad_act * slope).astype(BF16), w_fc)

    @pl.when(step == pl.num_programs(0) - 1)
    def _():
        out_ref[0] = total[...].astype(BF16)
        finish_backward(
            upstream_ref, middle, grad_total, norm_ref, w_out_ref, grad_middle_ref, grad_attended_ref
        )


def turn_block(spot, attended, hidden, upstream, norms, w_out, w_fc, w_proj):
    length = attended.shape[0]
    whole = lambda j, s: (0, 0)
    return pl.pallas_call(
        turn_kernel,
        grid_spec=pltpu.PrefetchScalarGridSpec(
            num_scalar_prefetch=1,
            grid=(FF // D,),
            in_specs=[
                once((length, D), whole),
                once((1, length, D), lambda j, s: (0, 0, 0)),
                once((1, length, D), lambda j, s: (s[0], 0, 0)),
                once((8, D), whole),
                once(w_out[1], lambda j, s: w_out[2](0)),
                pl.BlockSpec(w_fc[1], lambda j, s: w_fc[2](j)),
                pl.BlockSpec(w_proj[1], lambda j, s: w_proj[2](j)),
            ],
            out_specs=[
                once((1, length, D), lambda j, s: (0, 0, 0)),
                once((length, D), whole),
                once((length, D), whole),
            ],
            scratch_shapes=[
                pltpu.VMEM((length, D), BF16),
                pltpu.VMEM((length, D), F32),
                pltpu.VMEM((length, D), F32),
                pltpu.VMEM((length, D), F32),
            ],
        ),
        out_shape=[
            jax.ShapeDtypeStruct((1, length, D), BF16),
            jax.ShapeDtypeStruct((length, D), F32),
            jax.ShapeDtypeStruct((length, D), BF16),
        ],
        compiler_params=params(),
        name="turn_block",
    )(spot, attended, hidden, upstream, norms, w_out[0], w_fc[0], w_proj[0])


def backward_kernel(
    upstream_ref,
    slope_ref,
    middle_ref,
    norm_ref,
    w_out_ref,
    w_fc_ref,
    w_proj_ref,
    grad_middle_ref,
    grad_attended_ref,
    grad_total,
):
    step = pl.program_id(0)

    @pl.when(step == 0)
    def _():
        grad_total[...] = jnp.zeros_like(grad_total)

    w_fc, w_proj = matrix_of(w_fc_ref), matrix_of(w_proj_ref)
    for rows in row_tiles(middle_ref.shape[0], 256):
        grad_act = dot_nt(upstream_ref[0, rows], w_proj)
        grad_inner = (grad_act * slope_ref[rows].astype(F32)).astype(BF16)
        grad_total[rows] += dot_nt(grad_inner, w_fc)

    @pl.when(step == pl.num_programs(0) - 1)
    def _():
        finish_backward(
            upstream_ref, middle_ref, grad_total, norm_ref, w_out_ref, grad_middle_ref, grad_attended_ref
        )


def backward_block(upstream, slope, middle, norms, w_out, w_fc, w_proj):
    length = middle.shape[0]
    whole = lambda j: (0, 0)
    return pl.pallas_call(
        backward_kernel,
        grid=(FF // D,),
        in_specs=[
            once((1, length, D), lambda j: (0, 0, 0)),
            pl.BlockSpec((length, D), lambda j: (0, j)),
            once((length, D), whole),
            once((8, D), whole),
            once(w_out[1], lambda j: w_out[2](0)),
            pl.BlockSpec(w_fc[1], w_fc[2]),
            pl.BlockSpec(w_proj[1], w_proj[2]),
        ],
        out_specs=[once((length, D), whole), once((length, D), whole)],
        scratch_shapes=[pltpu.VMEM((length, D), F32)],
        out_shape=[
            jax.ShapeDtypeStruct((length, D), F32),
            jax.ShapeDtypeStruct((length, D), BF16),
        ],
        compiler_params=params(),
        name="backward_block",
    )(upstream, slope, middle, norms, w_out[0], w_fc[0], w_proj[0])


def unproject_kernel(spot_ref, grads_ref, hidden_ref, grad_middle_ref, norm_ref, weight_ref, out_ref, total):
    step = pl.program_id(0)
    weight = matrix_of(weight_ref)

    @pl.when(step == 0)
    def _():
        for rows in row_tiles(total.shape[0], 512):
            total[rows] = dot_nt(grads_ref[0, rows], weight)

    @pl.when(step == 1)
    def _():
        for rows in row_tiles(total.shape[0], 512):
            total[rows] += dot_nt(grads_ref[0, rows], weight)

    @pl.when(step == 2)
    def _():
        gain = norm_ref[0:1]
        for rows in row_tiles(total.shape[0], 256):
            grad_normed = total[rows] + dot_nt(grads_ref[0, rows], weight)
            values = hidden_ref[0, rows].astype(F32)
            grad = grad_middle_ref[rows] + norm_back(values, gain, grad_normed)
            out_ref[0, rows] = grad.astype(BF16)


def unproject(spot, grads, hidden, grad_middle, norms, weights):
    length = hidden.shape[1]
    array, shape, index = weights
    whole = lambda j, s: (0, 0)
    return pl.pallas_call(
        unproject_kernel,
        grid_spec=pltpu.PrefetchScalarGridSpec(
            num_scalar_prefetch=1,
            grid=(3,),
            in_specs=[
                pl.BlockSpec((1, length, D), lambda j, s: (j, 0, 0)),
                once((1, length, D), lambda j, s: (s[0], 0, 0)),
                once((length, D), whole),
                once((8, D), whole),
                pl.BlockSpec(shape, lambda j, s: index(j)),
            ],
            out_specs=once((1, length, D), lambda j, s: (0, 0, 0)),
            scratch_shapes=[pltpu.VMEM((length, D), F32)],
        ),
        out_shape=jax.ShapeDtypeStruct((1, length, D), BF16),
        compiler_params=params(),
        name="unproject",
    )(spot, grads, hidden, grad_middle, norms, array)


def swap_sections(values):
    return lax.ppermute(values, "section", [(0, 1), (1, 0)])


def per_section(section_index, own):
    other = swap_sections(own)
    is_first = section_index == 0
    return jnp.where(is_first, own, other), jnp.where(is_first, other, own)


def gather_weights(w_qkv, w_out, w_fc, w_proj):
    rows = w_qkv.shape[1]
    shards = D // rows
    columns = lambda matrix: jnp.moveaxis(matrix.reshape(rows, -1, D), 1, 0).reshape(-1, D)
    shard = jnp.concatenate(
        [columns(w_qkv[0]), columns(w_out[0]), columns(w_fc[0]), w_proj[0]], axis=0
    )
    every = lax.all_gather(shard, ("dp", "section"), axis=0)
    every = every.reshape(shards, 2, 12 * rows, D)
    layers = []
    for layer in range(2):
        if rows % 16 == 0:
            block = (shards, 1, rows, D)
            ff_shards = shards // 4

            def at(first, layer=layer):
                return lambda j: (0, layer, first + j, 0)

            layers.append(
                (
                    (every, block, at(0)),
                    (every, block, at(3)),
                    (every, block, at(4)),
                    (every, (ff_shards, 1, 4 * rows, D), lambda j, layer=layer: (j, layer, 2, 0)),
                )
            )
        else:
            mine = every[:, layer]
            straight = jnp.moveaxis(mine[:, : 8 * rows].reshape(shards, 8, rows, D), 1, 0)
            straight = straight.reshape(1, 8 * D, D)
            proj = mine[:, 8 * rows :].reshape(1, FF, D)

            def at(first):
                return lambda j: (0, first + j, 0)

            block = (1, D, D)
            layers.append(
                (
                    (straight, block, at(0)),
                    (straight, block, at(3)),
                    (straight, block, at(4)),
                    (proj, block, at(0)),
                )
            )
    return layers


def reparam_hidden(table, w_first, b_first):
    return jnp.tanh(jnp.dot(table, w_first, precision=highest_mode) + b_first)


def reparam_out(hidden_units, w_second, b_second):
    return jnp.dot(hidden_units, w_second, precision=highest_mode) + b_second


def sum_dp(values):
    count = lax.axis_size("dp")
    step = 1
    while step < count:
        pairs = [(i, i ^ step) for i in range(count)]
        values = values + lax.ppermute(values, "dp", pairs)
        step *= 2
    return values


def per_device(
    tokens,
    seq_length,
    cotangent,
    ln_gain,
    ln_bias,
    w_qkv,
    w_out,
    w_fc,
    w_proj,
    prefix_table,
    reparam_w1,
    reparam_b1,
    reparam_w2,
    reparam_b2,
):
    section_index = lax.axis_index("section")
    is_first = section_index == 0
    layers = gather_weights(w_qkv, w_out, w_fc, w_proj)

    table_values = prefix_table.astype(F32)
    first_weight = reparam_w1.astype(F32)
    first_bias = reparam_b1.astype(F32)
    second_weight = reparam_w2[0].astype(F32)
    second_bias = reparam_b2[0].astype(F32)
    hidden_units = reparam_hidden(table_values, first_weight, first_bias)
    prefix_kv = reparam_out(hidden_units, second_weight, second_bias).astype(BF16)
    pad = ((0, SLOTS - PREFIX), (0, 0))
    small = jnp.concatenate(
        [
            jnp.pad(prefix_kv[:, :D], pad),
            jnp.pad(prefix_kv[:, D:], pad),
            ln_gain[0],
            ln_bias[0],
            jnp.zeros((4, D), BF16),
        ],
        axis=0,
    )
    small_pair = per_section(section_index, small)
    prefix_pair = [(part[:SLOTS], part[SLOTS : 2 * SLOTS]) for part in small_pair]
    norm_pair = [part[2 * SLOTS :].astype(F32) for part in small_pair]

    spot = section_index.astype(jnp.int32)[None]
    none = jnp.zeros((1,), jnp.int32)
    seq = lax.dynamic_slice_in_dim(seq_length, section_index, 1, 0)

    qkv_first, out_first, fc_first, proj_first = layers[0]
    qkv_last, out_last, fc_last, proj_last = layers[1]

    projected_first = project(spot, tokens, norm_pair[0], qkv_first)
    attended_first, log_first = attend(seq, projected_first, *prefix_pair[0])
    middle, slope, handed = forward_block(
        spot, attended_first, tokens, norm_pair[0], out_first, fc_first, proj_first
    )
    projected = project(none, handed, norm_pair[1], qkv_last)
    attended, log_sums = attend(seq, projected, *prefix_pair[1])
    final, grad_middle, grad_attended = turn_block(
        spot, attended, handed, cotangent, norm_pair[1], out_last, fc_last, proj_last
    )
    grads, dkp_last, dvp_last = attend_back(
        seq, projected, attended, grad_attended, *prefix_pair[1], log_sums
    )
    grad_handed = unproject(none, grads, handed, grad_middle, norm_pair[1], qkv_last)
    grad_middle, grad_attended = backward_block(
        grad_handed, slope, middle, norm_pair[0], out_first, fc_first, proj_first
    )
    grads, dkp_first, dvp_first = attend_back(
        seq, projected_first, attended_first, grad_attended, *prefix_pair[0], log_first
    )
    grad_tokens = unproject(spot, grads, tokens, grad_middle, norm_pair[0], qkv_first)

    def gathered_rows(first, last):
        kept = jnp.where(is_first, first, last)
        received = swap_sections(jnp.where(is_first, last, first))
        return jnp.concatenate(
            [jnp.where(is_first, kept, received), jnp.where(is_first, received, kept)], axis=0
        )

    activations = gathered_rows(handed, final)
    input_grads = gathered_rows(grad_tokens, grad_handed)

    prefix_first = jnp.concatenate([dkp_first[:PREFIX], dvp_first[:PREFIX]], axis=1)
    prefix_last = jnp.concatenate([dkp_last[:PREFIX], dvp_last[:PREFIX]], axis=1)
    kept = jnp.where(is_first, prefix_first, prefix_last)
    received = swap_sections(jnp.where(is_first, prefix_last, prefix_first))
    prefix_total = sum_dp(kept + received)

    grad_hidden, grad_w2, grad_b2 = jax.vjp(reparam_out, hidden_units, second_weight, second_bias)[
        1
    ](prefix_total)
    grad_hidden = grad_hidden + swap_sections(grad_hidden)
    grad_table, grad_w1, grad_b1 = jax.vjp(reparam_hidden, table_values, first_weight, first_bias)[
        1
    ](grad_hidden)
    return (
        activations[None],
        input_grads[None],
        grad_table,
        grad_w1,
        grad_b1,
        grad_w2[None],
        grad_b2[None],
    )


def solution(mesh):
    in_specs = (
        P("dp", None, None),
        P("dp"),
        P("dp", None, None),
        P("section", None, None),
        P("section", None, None),
        P("section", "dp", None),
        P("section", "dp", None),
        P("section", "dp", None),
        P("section", "dp", None),
        P(),
        P(),
        P(),
        P("section", None, None),
        P("section", None),
    )
    out_specs = (
        P("section", "dp", None, None),
        P("section", "dp", None, None),
        P(),
        P(),
        P(),
        P("section", None, None),
        P("section", None),
    )
    return jax.shard_map(
        per_device, mesh=mesh, in_specs=in_specs, out_specs=out_specs, check_vma=False
    )
```

time: 2410 us -> 665 us (0.28)
  waiting for transfers between devices: 981 us -> 286 us
  matrix products: 686 us -> 11.9 us
  Pallas kernels: 0 us -> 280 us
  other arithmetic: 278 us -> 19.4 us
  local copies, waits for them, and re-layouts: 247 us -> 9.38 us
  starting transfers between devices: 154 us -> 40.2 us
  loops' own time: 42.1 us -> 0 us
    dot_general x84 -> x0, matrix products: 670 us -> none  [the longest x8 92.9 us: attend(): jnp.einsum('hqk,khd->qhd', (row_exp / denominator).astype(jnp.bfloat16),...]
    psum x3 -> x0, waiting for transfers between devices: 604 us -> none  [backward_tick(): prefix_total = prefix_total + lax.psum(grad_prefix, 'dp')]
    pallas_call x0 -> x11, Pallas kernels: none -> 280 us  [the longest x2 54 us: attend_back(): pl.pallas_call(attend_back_kernel, grid_spec=pltpu.PrefetchScalarGridSpec...]
    reduce_sum x32 -> x0, other arithmetic: 122 us -> none  [the longest x8 94 us: attend(): jnp.sum(row_exp, axis=-1, keepdims=True)]
    ppermute x6 -> x9, starting transfers between devices: 154 us -> 40.1 us  [the longest x5 36.3 us: swap_sections(): return lax.ppermute(values, 'section', [(0, 1), (1, 0)])]
    all_gather x4 -> x1, waiting for transfers between devices: 375 us -> 273 us  [gather_weights(): every = lax.all_gather(shard, ('dp', 'section'), axis=0)]
    convert_element_type x12 -> x2, other arithmetic: 94.3 us -> 0.66 us  [the longest x1 0.66 us: per_device(): norm_pair = [part[2 * SLOTS:].astype(F32) for part in small_pair]]
    slice x39 -> x2, local copies, waits for them, and re-layouts: 83.8 us -> 0.69 us  [the longest x1 0.68 us: per_device(): prefix_pair = [(part[:SLOTS], part[SLOTS:2 * SLOTS]) for part in small_pair]]
  transfers between devices with their start and end apart: 13 -> 10, of which waited for: 7 -> 5; matrix products, arithmetic and copies ran while one was open for 5% -> 4% of each run, Pallas kernels for 0% -> 2%
where the time goes in v1:
time: 665 us; the launch traced here: 661 us
  waiting for transfers between devices  286 us (43%)
  Pallas kernels  280 us (42%)
  starting transfers between devices  40.2 us (6%)
  other arithmetic  19.4 us (3%)
  between operations  14.6 us (2%)
  matrix products  11.9 us (2%)
  local copies, waits for them, and re-layouts  9.38 us (1%)
    all_gather x1, waiting for transfers between devices, gather_weights(): every = lax.all_gather(shard, ('dp', 'section'), axis=0)  273 us
    pallas_call x2, Pallas kernels, attend_back(): pl.pallas_call(attend_back_kernel, grid_spec=pltpu.PrefetchScalarGridSpec...  54 us
    pallas_call x1, Pallas kernels, turn_block(): pl.pallas_call(turn_kernel, grid_spec=pltpu.PrefetchScalarGridSpec(num_sc...  52.5 us
    pallas_call x2, Pallas kernels, attend(): pl.pallas_call(attend_kernel, grid_spec=pltpu.PrefetchScalarGridSpec(num_...  46.2 us
    pallas_call x1, Pallas kernels, forward_block(): pl.pallas_call(forward_kernel, grid_spec=pltpu.PrefetchScalarGridSpec(num...  42.1 us
    ppermute x5, starting transfers between devices, swap_sections(): return lax.ppermute(values, 'section', [(0, 1), (1, 0)])  36.3 us
    pallas_call x1, Pallas kernels, backward_block(): pl.pallas_call(backward_kernel, grid=(FF // D,), in_specs=[once((1, lengt...  30.8 us
    pallas_call x2, Pallas kernels, unproject(): pl.pallas_call(unproject_kernel, grid_spec=pltpu.PrefetchScalarGridSpec(n...  30.4 us
  transfers between devices with their start and end apart: 10, of which 5 were waited for; matrix products, arithmetic and copies ran while one was open for 4% of the time, Pallas kernels for 2%

profile of v1, /device:TPU:0, one launch (start us, length us, event | category | flops | bytes accessed | tf_op | source)
XLA Modules:
  0.0 661.4 jit_solution(8829083989109766443)
XLA Ops:
  16.6 273.2 %all-gather.3.cloned.1.call-done = bf16[24576,1024]{1,0:T(8,128)(2,1)} async-done(((bf16[768,1024]{1,0:T(8,128)(2,1)}), bf16[24576,1024]{1,0:T(8,128)(2,1)}) %all-gather.3.cloned.1.call-update) | async-done | bytes 50331664 | tf_op jit(solution)/shard_map/all_gather | solution.py:667
  289.8 12.1 %norm_project.2.q_ref.k_ref.v_ref = bf16[1024,3072]{1,0:T(8,128)(2,1)} custom-call(s32[1]{0:T(128)} %bitcast.spot_ref, bf16[2,1024,1024]{2,1,0:T(8,128)(2,1)} %hidden_ref.5, f32[8,1024]{1,0:T(8,128)} %get-tuple-element.79.norm_ref, bf16[16,2,768,1024]{3,2,1,0:T(8,128)(2,1)} %bitcast.38), custom_call_target="tpu_custom_call" | custom-call | tf_op jit(solution)/shard_map/norm_project/pallas_call | solution.py:108
  301.9 23.1 %attend.2 = (bf16[1024,1024]{1,0:T(8,128)(2,1)}, f32[8,8,1024]{2,1,0:T(8,128)}) custom-call(s32[1]{0:T(128)} %dynamic_slice.3.short_ref, bf16[1024,3072]{1,0:T(8,128)(2,1)} %norm_project.2.q_ref.k_ref.v_ref, bf16[1024,3072]{1,0:T(8,128)(2,1)} %norm_project.2.q_ref.k_ref.v_ref, bf16[1024,3072]{1,0:T(8,128)(2,1)} %norm_project.2.q_ref.k_ref.v_ref, ...), custom_call_target="tpu_custom_call" | custom-call | tf_op jit(solution)/shard_map/attend/pallas_call | solution.py:206
  325.0 42.1 %forward_block.1 = (f32[1024,1024]{1,0:T(8,128)}, bf16[1024,4096]{1,0:T(8,128)(2,1)}, bf16[1,1024,1024]{2,1,0:T(8,128)(2,1)}) custom-call(s32[1]{0:T(128)} %bitcast.spot_ref, bf16[1024,1024]{1,0:T(8,128)(2,1)} %get-tuple-element.25.attended_ref.out_ref, bf16[2,1024,1024]{2,1,0:T(8,128)(2,1)} %hidden_ref.5, f32[8,1024]{1,0:T(8,128)} %get-tuple-element.79.norm_ref, ...), custom_call_target="tpu_custom_call" | custom-call | tf_op jit(solution)/shard_map/forward_block/pallas_call | solution.py:417
  367.1 12.2 %norm_project.3.q_ref.k_ref.v_ref = bf16[1024,3072]{1,0:T(8,128)(2,1)} custom-call(s32[1]{0:T(128)} %constant.5.clone.1.spot_ref, bf16[1,1024,1024]{2,1,0:T(8,128)(2,1)} %get-tuple-element.26.hidden_ref, f32[8,1024]{1,0:T(8,128)} %get-tuple-element.78.norm_ref, bf16[16,2,768,1024]{3,2,1,0:T(8,128)(2,1)} %bitcast.42), custom_call_target="tpu_custom_call" | custom-call | tf_op jit(solution)/shard_map/norm_project/pallas_call | solution.py:108
  379.3 23.1 %attend.3 = (bf16[1024,1024]{1,0:T(8,128)(2,1)}, f32[8,8,1024]{2,1,0:T(8,128)}) custom-call(s32[1]{0:T(128)} %dynamic_slice.3.short_ref, bf16[1024,3072]{1,0:T(8,128)(2,1)} %norm_project.3.q_ref.k_ref.v_ref, bf16[1024,3072]{1,0:T(8,128)(2,1)} %norm_project.3.q_ref.k_ref.v_ref, bf16[1024,3072]{1,0:T(8,128)(2,1)} %norm_project.3.q_ref.k_ref.v_ref, ...), custom_call_target="tpu_custom_call" | custom-call | tf_op jit(solution)/shard_map/attend/pallas_call | solution.py:206
  402.4 52.5 %turn_block.1 = (bf16[1,1024,1024]{2,1,0:T(8,128)(2,1)}, f32[1024,1024]{1,0:T(8,128)}, bf16[1024,1024]{1,0:T(8,128)(2,1)}) custom-call(s32[1]{0:T(128)} %bitcast.spot_ref, bf16[1024,1024]{1,0:T(8,128)(2,1)} %get-tuple-element.27.attended_ref.out_ref, bf16[1,1024,1024]{2,1,0:T(8,128)(2,1)} %get-tuple-element.26.hidden_ref, ...), custom_call_target="tpu_custom_call" | custom-call | tf_op jit(solution)/shard_map/turn_block/pallas_call | solution.py:508
  455.0 26.8 %attend_back.2 = (bf16[3,1024,1024]{2,1,0:T(8,128)(2,1)}, f32[16,1024]{1,0:T(8,128)}, f32[16,1024]{1,0:T(8,128)}) custom-call(s32[1]{0:T(128)} %dynamic_slice.3.short_ref, bf16[1024,3072]{1,0:T(8,128)(2,1)} %norm_project.3.q_ref.k_ref.v_ref, bf16[1024,3072]{1,0:T(8,128)(2,1)} %norm_project.3.q_ref.k_ref.v_ref, ...), custom_call_target="tpu_custom_call" | custom-call | tf_op jit(solution)/shard_map/attend_back/pallas_call | solution.py:320
  481.7 15.2 %unproject.2.upstream_ref = bf16[1,1024,1024]{2,1,0:T(8,128)(2,1)} custom-call(s32[1]{0:T(128)} %constant.5.clone.1.spot_ref, bf16[3,1024,1024]{2,1,0:T(8,128)(2,1)} %get-tuple-element.31.grads_ref, bf16[1,1024,1024]{2,1,0:T(8,128)(2,1)} %get-tuple-element.26.hidden_ref, f32[1024,1024]{1,0:T(8,128)} %get-tuple-element.32.grad_middle_ref, ...), custom_call_target="tpu_custom_call" | custom-call | tf_op jit(solution)/shard_map/unproject/pallas_call | solution.py:629
  496.9 30.8 %backward_block.1 = (f32[1024,1024]{1,0:T(8,128)}, bf16[1024,1024]{1,0:T(8,128)(2,1)}) custom-call(bf16[1,1024,1024]{2,1,0:T(8,128)(2,1)} %unproject.2.upstream_ref, bf16[1024,4096]{1,0:T(8,128)(2,1)} %get-tuple-element.33.slope_ref, f32[1024,1024]{1,0:T(8,128)} %get-tuple-element.34.middle_ref, f32[8,1024]{1,0:T(8,128)} %get-tuple-element.79.norm_ref, ...), custom_call_target="tpu_custom_call" | custom-call | tf_op jit(solution)/shard_map/backward_block/pallas_call | solution.py:578
  527.6 27.2 %attend_back.3 = (bf16[3,1024,1024]{2,1,0:T(8,128)(2,1)}, f32[16,1024]{1,0:T(8,128)}, f32[16,1024]{1,0:T(8,128)}) custom-call(s32[1]{0:T(128)} %dynamic_slice.3.short_ref, bf16[1024,3072]{1,0:T(8,128)(2,1)} %norm_project.2.q_ref.k_ref.v_ref, bf16[1024,3072]{1,0:T(8,128)(2,1)} %norm_project.2.q_ref.k_ref.v_ref, ...), custom_call_target="tpu_custom_call" | custom-call | tf_op jit(solution)/shard_map/attend_back/pallas_call | solution.py:320
  555.8 35.7 %collective-permute-start.3 = (f32[10,2048]{1,0:T(8,128)S(1)}, f32[10,2048]{1,0:T(8,128)S(1)}, u32[]{:S(2)}, u32[]{:S(2)}) collective-permute-start(f32[10,2048]{1,0:T(8,128)S(1)} %fusion.5), channel_id=1, source_target_pairs={{0,1},{1,0},{2,3},{3,2},{4,5},{5,4},{6,7},{7,6},{8,9},{9,8},{10,11... | collective-permute-start | bytes 245768 | tf_op jit(solution)/shard_map/ppermute | solution.py:651
  591.5 3.2 broadcast_select_fusion.6
  596.6 4.2 collective-permute-done.4
  601.2 4.8 collective-permute-done.5
  606.1 15.3 %unproject.3 = bf16[1,1024,1024]{2,1,0:T(8,128)(2,1)} custom-call(s32[1]{0:T(128)} %bitcast.spot_ref, bf16[3,1024,1024]{2,1,0:T(8,128)(2,1)} %get-tuple-element.37.grads_ref, bf16[2,1024,1024]{2,1,0:T(8,128)(2,1)} %hidden_ref.5, f32[1024,1024]{1,0:T(8,128)} %get-tuple-element.38.grad_middle_ref, f32[8,1024]{1,0:T(8,128)} %get-tuple-element.79.norm_ref, ...), custom_call_target="tpu_custom_call" | custom-call | tf_op jit(solution)/shard_map/unproject/pallas_call | solution.py:629
  623.1 3.1 broadcast_select_fusion.2
  626.2 3.1 collective-permute-done.7
  631.1 5.0 convolution_bitcast_fusion
  637.4 2.4 convolution_bitcast_fusion.1
  639.8 3.0 copy.28
  646.3 2.5 maximum_bitcast_fusion
  650.0 2.0 broadcast_select_fusion.1
  652.0 2.4 maximum_bitcast_fusion.1
  (88 shorter events, 21.8 us)
Async XLA Ops:
  7.2 4.1 copy-start
  7.2 2.6 copy-start.9
  7.2 2.6 copy-start.16
  7.2 282.6 %all-gather.3.cloned.1.call-start = ((), (), s32[]{:S(2)}) async-start(), calls=%async_computation | async-start | bytes 51904512 | tf_op jit(solution)/shard_map/all_gather | solution.py:667
  11.2 2.6 copy-start.18
  11.2 3.1 copy-start.21
  13.8 1.4 collective-permute-start
  527.6 27.3 %copy-start.10 = (f32[16,1024]{1,0:T(8,128)S(1)}, f32[16,1024]{1,0:T(8,128)}, u32[]{:S(2)}) copy-start(f32[16,1024]{1,0:T(8,128)} %get-tuple-element.41) | copy-start | bytes 196612
  527.6 27.3 %copy-start.11 = (f32[16,1024]{1,0:T(8,128)S(1)}, f32[16,1024]{1,0:T(8,128)}, u32[]{:S(2)}) copy-start(f32[16,1024]{1,0:T(8,128)} %get-tuple-element.42) | copy-start | bytes 196612
  555.8 39.0 %collective-permute-start.3 = (f32[10,2048]{1,0:T(8,128)S(1)}, f32[10,2048]{1,0:T(8,128)S(1)}, u32[]{:S(2)}, u32[]{:S(2)}) collective-permute-start(f32[10,2048]{1,0:T(8,128)S(1)} %fusion.5), channel_id=1, source_target_pairs={{0,1},{1,0},{2,3},{3,2},{4,5},{5,4},{6,7},{7,6},{8,9},{9,8},{10,11... | collective-permute-start | bytes 245768 | tf_op jit(solution)/shard_map/ppermute | solution.py:651
  591.5 3.3 copy-start.12
  591.5 3.3 copy-start.13
  594.8 49.6 %collective-permute-start.1 = (bf16[1,1024,1024]{2,1,0:T(8,128)(2,1)}, bf16[1,1024,1024]{2,1,0:T(8,128)(2,1)}, u32[]{:S(2)}, u32[]{:S(2)}) collective-permute-start(bf16[1,1024,1024]{2,1,0:T(8,128)(2,1)} %broadcast_select_fusion.6), channel_id=1, source_target_pairs={{0,1},{1,0},{2,3},{3,2},{4,5},{5,4},{6,7},{7,6},{8,9},{9,8},{10,11... | collective-permute-start | bytes 6291464 | tf_op jit(solution)/shard_map/ppermute | solution.py:651
  594.9 5.9 collective-permute-start.4
  600.8 5.1 collective-permute-start.5
  606.0 15.3 %collective-permute-start.6 = (f32[10,2048]{1,0:T(8,128)S(1)}, f32[10,2048]{1,0:T(8,128)S(1)}, u32[]{:S(2)}, u32[]{:S(2)}) collective-permute-start(f32[10,2048]{1,0:T(8,128)S(1)} %add.62), channel_id=1, source_target_pairs={{0,8},{2,10},{4,12},{6,14},{8,0},{10,2},{12,4},{14,6},{16,24},{18,... | collective-permute-start | bytes 245768 | tf_op jit(solution)/shard_map/ppermute | solution.py:720
  621.4 8.0 %copy-start.5 = (bf16[1,512,2048]{2,1,0:T(8,128)(2,1)S(1)}, bf16[1,512,2048]{2,1,0:T(8,128)(2,1)}, u32[]{:S(2)}) copy-start(bf16[1,512,2048]{2,1,0:T(8,128)(2,1)} %param.26) | copy-start | bytes 6291460
  621.4 8.0 %collective-permute-start.7 = (f32[10,2048]{1,0:T(8,128)S(1)}, f32[10,2048]{1,0:T(8,128)S(1)}, u32[]{:S(2)}, u32[]{:S(2)}) collective-permute-start(f32[10,2048]{1,0:T(8,128)S(1)} %add.63), channel_id=1, source_target_pairs={{0,16},{2,18},{4,20},{6,22},{8,24},{10,26},{12,28},{14,30},{16,0},... | collective-permute-start | bytes 245768 | tf_op jit(solution)/shard_map/ppermute | solution.py:720
  626.2 4.9 copy-start.7
  626.2 22.6 %collective-permute-start.2 = (bf16[1,1024,1024]{2,1,0:T(8,128)(2,1)}, bf16[1,1024,1024]{2,1,0:T(8,128)(2,1)}, u32[]{:S(2)}, u32[]{:S(2)}) collective-permute-start(bf16[1,1024,1024]{2,1,0:T(8,128)(2,1)} %broadcast_select_fusion.2), channel_id=1, source_target_pairs={{0,1},{1,0},{2,3},{3,2},{4,5},{5,4},{6,7},{7,6},{8,9},{9,8},{10,11... | collective-permute-start | bytes 6291464 | tf_op jit(solution)/shard_map/ppermute | solution.py:651
  631.1 6.3 copy-start.15
  631.1 5.7 collective-permute-start.8
  639.7 4.6 copy-start.1
  646.3 3.7 copy-start.3
  (8 other events, 15.1 us)
Sparse Core Ops, SparseCore 0:
  11.5 278.2 all-gather.2

commit v2 on v1

v2 whole, which is shorter than its diff:
```python
import functools

import jax
import jax.numpy as jnp
from jax import lax
from jax.experimental import pallas as pl
from jax.experimental.pallas import tpu as pltpu
from jax.sharding import PartitionSpec as P

D = 1024
HEADS = 16
HEAD_DIM = 64
FF = 4096
PREFIX = 10
SLOTS = 16
PAIRS = 8
PAIR_DIM = 128
BLOCK = 256

eps_norm = 1e-05
neg_big = -1e30
highest_mode = lax.Precision.HIGHEST
VMEM_BYTES = 62 * 2**20
F32 = jnp.float32
BF16 = jnp.bfloat16


def dot(left, right, dims):
    return lax.dot_general(left, right, (dims, ((), ())), preferred_element_type=F32)


def dot_nn(left, right):
    return dot(left, right, ((1,), (0,)))


def dot_nt(left, right):
    return dot(left, right, ((1,), (1,)))


def dot_tn(left, right):
    return dot(left, right, ((0,), (0,)))


def normalised(values):
    centre = jnp.mean(values, axis=-1, keepdims=True)
    spread = values - centre
    variance = jnp.mean(spread * spread, axis=-1, keepdims=True)
    inverse = lax.rsqrt(variance + eps_norm)
    return spread * inverse, inverse


def layer_norm(values, gain, offset):
    return normalised(values)[0] * gain + offset


def norm_back(values, gain, upstream):
    unit, inverse = normalised(values)
    scaled = upstream * gain
    mean_scaled = jnp.mean(scaled, axis=-1, keepdims=True)
    mean_unit = jnp.mean(scaled * unit, axis=-1, keepdims=True)
    return (scaled - mean_scaled - unit * mean_unit) * inverse


SQRT_2_PI = 0.7978845608028654
CUBIC = 0.044715


def gelu_pair(values):
    cubic_part = (SQRT_2_PI * CUBIC) * (values * values)
    half_tanh = 0.5 + 0.5 * jnp.tanh(values * (SQRT_2_PI + cubic_part))
    out = values * half_tanh
    slope = half_tanh + out * ((2.0 - 2.0 * half_tanh) * (SQRT_2_PI + 3.0 * cubic_part))
    return out, slope


def params(**kwargs):
    return pltpu.CompilerParams(vmem_limit_bytes=VMEM_BYTES, **kwargs)


def cost(micros):
    return pl.CostEstimate(flops=int(micros * 1.15e9), bytes_accessed=2**20, transcendentals=0)


SHARDS = 16
HALF = 128
SHARD_ROWS = 64
BLOCKS = FF // D


def load_across(array, half, row, target, semaphore):
    return pltpu.make_async_copy(array.at[:, half, pl.ds(row, SHARD_ROWS)], target, semaphore)


def load_qkv(array, row, part, weights, semaphores):
    half, inner = divmod(part, 2)
    return load_across(
        array, half, row + inner * SHARD_ROWS, weights.at[part], semaphores.at[part]
    )


def load_out(array, row, target, semaphore):
    return load_across(array, 1, row + SHARD_ROWS, target, semaphore)


def load_up(array, row, block, target, semaphore):
    half, inner = divmod(block, 2)
    return load_across(array, half, row + inner * SHARD_ROWS, target, semaphore)


def load_down(array, row, block, target, semaphore):
    few = SHARDS // BLOCKS
    return pltpu.make_async_copy(
        array.at[pl.ds(block * few, few), :, pl.ds(row, HALF)], target, semaphore
    )


def across_scratch(count):
    return pltpu.VMEM((count, SHARDS, SHARD_ROWS, D), BF16)


def down_scratch():
    return pltpu.VMEM((BLOCKS, SHARDS // BLOCKS, 2, HALF, D), BF16)


def matrix(ref, *index):
    return ref[index].reshape(D, D) if index else ref[...].reshape(D, D)


ANY = pl.BlockSpec(memory_space=pl.ANY)


def once(shape, index):
    return pl.BlockSpec(shape, index, pipeline_mode=pl.Buffered(1))


def row_tiles(length, size):
    return [slice(start, start + size) for start in range(0, length, size)]


CHUNK = 16


def put_pairs(ref, rows, values):
    for pair in range(PAIRS):
        ref[pair, rows] = values[:, pair * PAIR_DIM : (pair + 1) * PAIR_DIM]


def get_pairs(ref, rows, *lead):
    return jnp.concatenate([ref[(*lead, pair, rows)] for pair in range(PAIRS)], axis=1)


def chunks(rows, size=CHUNK):
    return [slice(start, start + size) for start in range(rows.start, rows.stop, size)]


def shifted(rows, by):
    return slice(rows.start + by, rows.stop + by)


def qkv_kernel(row, spot_ref, hidden_ref, norm_ref, array, out_ref, normed, weights, semaphores):
    step = pl.program_id(0)
    loads = [load_qkv(array, row, part, weights, semaphores) for part in range(3)]
    length = hidden_ref.shape[1]
    tiles = row_tiles(length, 512)

    @pl.when(step == 0)
    def _():
        loads[0].start()
        gain, offset = norm_ref[0:1], norm_ref[2:3]
        for rows in chunks(slice(0, length)):
            values = hidden_ref[0, rows].astype(F32)
            normed[rows] = layer_norm(values, gain, offset).astype(BF16)
        loads[0].wait()
        loads[1].start()
        loads[2].start()
        for rows in tiles:
            queries = dot_nn(normed[rows], matrix(weights, 0))
            put_pairs(out_ref, rows, (queries * HEAD_DIM**-0.5).astype(BF16))

    for part in (1, 2):

        @pl.when(step == part)
        def _(part=part):
            loads[part].wait()
            for rows in tiles:
                put_pairs(out_ref, rows, dot_nn(normed[rows], matrix(weights, part)).astype(BF16))


def project(spot, which, hidden, norms, place):
    length = hidden.shape[1]
    return pl.pallas_call(
        functools.partial(qkv_kernel, place[1]),
        grid_spec=pltpu.PrefetchScalarGridSpec(
            num_scalar_prefetch=1,
            grid=(3,),
            in_specs=[
                once((1, length, D), lambda j, s: (s[which], 0, 0)),
                once((8, D), lambda j, s: (0, 0)),
                ANY,
            ],
            out_specs=pl.BlockSpec((PAIRS, length, PAIR_DIM), lambda j, s: (j, 0, 0)),
            scratch_shapes=[
                pltpu.VMEM((length, D), BF16),
                across_scratch(3),
                pltpu.SemaphoreType.DMA((3,)),
            ],
        ),
        out_shape=jax.ShapeDtypeStruct((3 * PAIRS, length, PAIR_DIM), BF16),
        compiler_params=params(),
        cost_estimate=cost(12),
        name="norm_project",
    )(spot, hidden, norms, place[0])


def lane_halves(block):
    lanes = lax.broadcasted_iota(jnp.int32, block.shape, 1)
    zero = jnp.zeros_like(block)
    return jnp.where(lanes < HEAD_DIM, block, zero), jnp.where(lanes < HEAD_DIM, zero, block)


def key_spans(first, stop):
    if first == 0:
        return [slice(0, SLOTS + stop)]
    return [slice(0, SLOTS), slice(SLOTS + first, SLOTS + stop)]


def read_spans(ref, spans, *rest):
    parts = [ref[(span, *rest)] for span in spans]
    return parts[0] if len(parts) == 1 else jnp.concatenate(parts, axis=0)


def cut_spans(values, spans):
    start = 0
    for span in spans:
        size = span.stop - span.start
        yield span, values[start : start + size]
        start += size


def strips(length, short):
    return [
        (rows, slice(2 * rows.start, 2 * rows.stop), rows.start if short else 0)
        for rows in row_tiles(length, BLOCK)
    ]


def stacked_halves(block):
    return jnp.concatenate(lane_halves(block), axis=0)


def own_heads(product):
    return jnp.concatenate([product[:HEAD_DIM, :BLOCK], product[HEAD_DIM:, BLOCK:]], axis=0)


def either_length(length_ref, length, run):
    short = length_ref[0] < length
    pl.when(short)(lambda: run(True))
    pl.when(jnp.logical_not(short))(lambda: run(False))


def allowed(rows, first_diagonal):
    shape = (rows.stop - rows.start, 2 * BLOCK)
    keys = lax.broadcasted_iota(jnp.int32, shape, 0) + rows.start
    if rows.stop <= SLOTS:
        return keys < PREFIX
    queries = lax.broadcasted_iota(jnp.int32, shape, 1) % BLOCK
    return keys - first_diagonal <= queries


def eight_rows(values, reduce):
    return reduce(values.reshape(-1, 8, values.shape[-1]), axis=0)


def attend_kernel(
    seq_ref, q_ref, k_ref, v_ref, kp_ref, vp_ref, out_ref, probs_ref, scale_ref, keys, values_t, scores
):
    length = q_ref.shape[1]
    keys[:SLOTS], keys[SLOTS:] = kp_ref[0], k_ref[0]
    values_t[...] = v_ref[0].T
    prefix_values = vp_ref[0]

    def run(short):
        def scored(strip, slot):
            rows, _, first = strip
            count = SLOTS + rows.stop - first
            scores[slot, :count] = dot_nt(
                read_spans(keys, key_spans(first, rows.stop)), stacked_halves(q_ref[0, rows])
            )

        todo = strips(length, short)
        scored(todo[0], 0)
        for index, (rows, columns, first) in enumerate(todo):
            slot = index % 2
            if index + 1 < len(todo):
                scored(todo[index + 1], 1 - slot)
            count = SLOTS + rows.stop - first
            parts = chunks(slice(0, count))
            top = None
            for part in parts:
                values = scores[slot, part]
                if part.stop <= SLOTS or part.start >= count - BLOCK:
                    values = jnp.where(allowed(part, count - BLOCK), values, neg_big)
                    scores[slot, part] = values
                values = eight_rows(values, jnp.max)
                top = values if top is None else jnp.maximum(top, values)
            top = jnp.max(top, axis=0, keepdims=True)
            total = None
            for part in parts:
                values = jnp.exp(scores[slot, part] - top)
                place = part if part.stop <= SLOTS else shifted(part, first)
                probs_ref[0, place, columns] = values.astype(BF16)
                values = eight_rows(values, jnp.sum)
                total = values if total is None else total + values
            inverse = 1.0 / jnp.sum(total, axis=0, keepdims=True)
            both = dot_nn(
                values_t[:, first : rows.stop],
                probs_ref[0, SLOTS + first : SLOTS + rows.stop, columns],
            ) + dot_tn(prefix_values, probs_ref[0, :SLOTS, columns])
            inverse = jnp.concatenate(
                [
                    jnp.broadcast_to(inverse[:, :BLOCK], (HEAD_DIM, BLOCK)),
                    jnp.broadcast_to(inverse[:, BLOCK:], (HEAD_DIM, BLOCK)),
                ],
                axis=0,
            )
            out_ref[0, rows] = (own_heads(both) * inverse).T.astype(BF16)
            scale_ref[0, rows] = inverse.T

    either_length(seq_ref, length, run)


def pair_spec(length, part):
    return pl.BlockSpec((1, length, PAIR_DIM), lambda p, s: (part * PAIRS + p, 0, 0))


def probs_spec(length):
    return pl.BlockSpec((1, SLOTS + length, 2 * length), lambda p, s: (p, 0, 0))


def attend(seq, projected, prefix_keys, prefix_values):
    length = projected.shape[1]
    return pl.pallas_call(
        attend_kernel,
        grid_spec=pltpu.PrefetchScalarGridSpec(
            num_scalar_prefetch=1,
            grid=(PAIRS,),
            in_specs=[
                pair_spec(length, 0),
                pair_spec(length, 1),
                pair_spec(length, 2),
                pair_spec(SLOTS, 0),
                pair_spec(SLOTS, 0),
            ],
            out_specs=[pair_spec(length, 0), probs_spec(length), pair_spec(length, 0)],
            scratch_shapes=[
                pltpu.VMEM((SLOTS + length, PAIR_DIM), BF16),
                pltpu.VMEM((PAIR_DIM, length), BF16),
                pltpu.VMEM((2, SLOTS + length, 2 * BLOCK), F32),
            ],
        ),
        out_shape=[
            jax.ShapeDtypeStruct((PAIRS, length, PAIR_DIM), BF16),
            jax.ShapeDtypeStruct((PAIRS, SLOTS + length, 2 * length), BF16),
            jax.ShapeDtypeStruct((PAIRS, length, PAIR_DIM), F32),
        ],
        compiler_params=params(),
        cost_estimate=cost(30),
        name="attend",
    )(seq, projected, projected, projected, prefix_keys, prefix_values)


def attend_back_kernel(
    seq_ref,
    q_ref,
    k_ref,
    v_ref,
    out_ref,
    grad_ref,
    kp_ref,
    vp_ref,
    probs_ref,
    scale_ref,
    grads_ref,
    dkp_ref,
    dvp_ref,
    values,
    keys_t,
    dk,
    dv,
    dprobs,
    ds,
):
    length = q_ref.shape[1]
    values[:SLOTS], values[SLOTS:] = vp_ref[0], v_ref[0]
    keys_t[...] = k_ref[0].T
    prefix_keys = kp_ref[0]
    dk[...] = jnp.zeros_like(dk)
    dv[...] = jnp.zeros_like(dv)

    def run(short):
        def prepared(strip, slot):
            rows, _, first = strip
            grads = (grad_ref[0, rows].astype(F32) * scale_ref[0, rows]).astype(BF16)
            halves = stacked_halves(grads)
            weighted_t = (grads.astype(F32) * out_ref[0, rows].astype(F32)).T
            centre = jnp.concatenate(
                [
                    jnp.sum(weighted_t[:HEAD_DIM], axis=0, keepdims=True),
                    jnp.sum(weighted_t[HEAD_DIM:], axis=0, keepdims=True),
                ],
                axis=1,
            )
            dprobs[slot, : SLOTS + rows.stop - first] = dot_nt(
                read_spans(values, key_spans(first, rows.stop)), halves
            )
            return halves, centre

        todo = strips(length, short)
        ahead = prepared(todo[0], 0)
        for index, (rows, columns, first) in enumerate(todo):
            slot = index % 2
            spans = key_spans(first, rows.stop)
            grad_halves, centre = ahead
            if index + 1 < len(todo):
                ahead = prepared(todo[index + 1], 1 - slot)
            count = SLOTS + rows.stop - first
            for part in chunks(slice(0, count)):
                place = part if part.stop <= SLOTS else shifted(part, first)
                probs = probs_ref[0, place, columns].astype(F32)
                ds[slot, part] = (probs * (dprobs[slot, part] - centre)).astype(BF16)
            for total, left, right in (
                (dv, read_spans(probs_ref.at[0], spans, columns), grad_halves),
                (dk, ds[slot, :count], stacked_halves(q_ref[0, rows])),
            ):
                for span, part in cut_spans(dot_nn(left, right), spans):
                    total[span] += part
            both = dot_nn(keys_t[:, first : rows.stop], ds[slot, SLOTS:count]) + dot_tn(
                prefix_keys, ds[slot, :SLOTS]
            )
            grads_ref[0, 0, rows] = (own_heads(both).T * HEAD_DIM**-0.5).astype(BF16)

    either_length(seq_ref, length, run)
    grads_ref[1, 0] = dk[SLOTS:].astype(BF16)
    grads_ref[2, 0] = dv[SLOTS:].astype(BF16)
    dkp_ref[0] = dk[:SLOTS]
    dvp_ref[0] = dv[:SLOTS]


def attend_back(seq, projected, attended, grad_attended, prefix_keys, prefix_values, probs, scale):
    length = projected.shape[1]
    ext = (SLOTS + length, PAIR_DIM)
    return pl.pallas_call(
        attend_back_kernel,
        grid_spec=pltpu.PrefetchScalarGridSpec(
            num_scalar_prefetch=1,
            grid=(PAIRS,),
            in_specs=[
                pair_spec(length, 0),
                pair_spec(length, 1),
                pair_spec(length, 2),
                pair_spec(length, 0),
                pair_spec(length, 0),
                pair_spec(SLOTS, 0),
                pair_spec(SLOTS, 0),
                probs_spec(length),
                pair_spec(length, 0),
            ],
            out_specs=[
                pl.BlockSpec((3, 1, length, PAIR_DIM), lambda p, s: (0, p, 0, 0)),
                pair_spec(SLOTS, 0),
                pair_spec(SLOTS, 0),
            ],
            scratch_shapes=[
                pltpu.VMEM(ext, BF16),
                pltpu.VMEM((PAIR_DIM, length), BF16),
                pltpu.VMEM(ext, F32),
                pltpu.VMEM(ext, F32),
                pltpu.VMEM((2, SLOTS + length, 2 * BLOCK), F32),
                pltpu.VMEM((2, SLOTS + length, 2 * BLOCK), BF16),
            ],
        ),
        out_shape=[
            jax.ShapeDtypeStruct((3, PAIRS, length, PAIR_DIM), BF16),
            jax.ShapeDtypeStruct((PAIRS, SLOTS, PAIR_DIM), F32),
            jax.ShapeDtypeStruct((PAIRS, SLOTS, PAIR_DIM), F32),
        ],
        compiler_params=params(),
        cost_estimate=cost(30),
        name="attend_back",
    )(
        seq,
        projected,
        projected,
        projected,
        attended,
        grad_attended,
        prefix_keys,
        prefix_values,
        probs,
        scale,
    )


def middle_kernel(row, spot_ref, attended_ref, hidden_ref, norm_ref, array, middle_ref, normed_ref, weights, semaphores):
    step = pl.program_id(0)
    load = load_out(array, row, weights.at[0], semaphores.at[0])

    @pl.when(step == 0)
    def _():
        load.start()
        load.wait()

    middle_ref[...] = dot_nn(get_pairs(attended_ref, slice(None)), matrix(weights, 0))
    gain, offset = norm_ref[1:2], norm_ref[3:4]
    for rows in chunks(slice(0, middle_ref.shape[0])):
        middle = hidden_ref[0, rows].astype(F32) + middle_ref[rows]
        middle_ref[rows] = middle
        normed_ref[rows] = layer_norm(middle, gain, offset).astype(BF16)


def middle_block(spot, which, attended, hidden, norms, place):
    length = attended.shape[1]
    tile = pl.BlockSpec((256, D), lambda m, s: (m, 0))
    return pl.pallas_call(
        functools.partial(middle_kernel, place[1]),
        grid_spec=pltpu.PrefetchScalarGridSpec(
            num_scalar_prefetch=1,
            grid=(length // 256,),
            in_specs=[
                pl.BlockSpec((PAIRS, 256, PAIR_DIM), lambda m, s: (0, m, 0)),
                pl.BlockSpec((1, 256, D), lambda m, s: (s[which], m, 0)),
                once((8, D), lambda m, s: (0, 0)),
                ANY,
            ],
            out_specs=[tile, tile],
            scratch_shapes=[across_scratch(1), pltpu.SemaphoreType.DMA((1,))],
        ),
        out_shape=[
            jax.ShapeDtypeStruct((length, D), F32),
            jax.ShapeDtypeStruct((length, D), BF16),
        ],
        compiler_params=params(),
        cost_estimate=cost(5),
        name="middle_block",
    )(spot, attended, hidden, norms, place[0])


def feed_forward_loads(up, down, rows, up_weights, down_weights, semaphores):
    return [
        (
            load_up(up, rows[0], block, up_weights.at[block], semaphores.at[0, block]),
            load_down(down, rows[1], block, down_weights.at[block], semaphores.at[1, block]),
        )
        for block in range(BLOCKS)
    ]


def start_all(loads):
    for pair in loads:
        for load in pair:
            load.start()


def wait_step(loads, step):
    for block, pair in enumerate(loads):

        @pl.when(step == block)
        def _(pair=pair):
            for load in pair:
                load.wait()


def wait_for(target, semaphore):
    pltpu.make_async_copy(target, target, semaphore).wait()


def feed_forward_scratch():
    return [across_scratch(BLOCKS), down_scratch(), pltpu.SemaphoreType.DMA((2, BLOCKS))]


def forward_kernel(
    rows_at,
    normed_ref,
    middle_ref,
    up,
    down,
    slope_ref,
    out_ref,
    total,
    inner,
    activated,
    up_weights,
    down_weights,
    semaphores,
):
    step = pl.program_id(0)
    tiles = row_tiles(middle_ref.shape[0], TILE)
    loads = feed_forward_loads(up, down, rows_at, up_weights, down_weights, semaphores)

    @pl.when(step == 0)
    def _():
        start_all(loads[:1])
        total[...] = middle_ref[...]

    wait_step(loads, step)
    for later in range(1, BLOCKS):
        pl.when(step == later - 1)(lambda later=later: start_all(loads[later : later + 1]))
    w_fc, w_proj = matrix(up_weights, step), matrix(down_weights, step)
    inner[tiles[0]] = dot_nn(normed_ref[tiles[0]], w_fc)
    for index, rows in enumerate(tiles):
        if index + 1 < len(tiles):
            inner[tiles[index + 1]] = dot_nn(normed_ref[tiles[index + 1]], w_fc)
        for part in chunks(rows):
            value, slope = gelu_pair(inner[part])
            activated[part] = value.astype(BF16)
            slope_ref[part] = slope.astype(BF16)
        total[rows] += dot_nn(activated[rows], w_proj)

    @pl.when(step == pl.num_programs(0) - 1)
    def _():
        out_ref[0] = total[...].astype(BF16)


def forward_block(normed, middle, up, down):
    length = normed.shape[0]
    whole = lambda j: (0, 0)
    return pl.pallas_call(
        functools.partial(forward_kernel, (up[1], down[1])),
        grid=(BLOCKS,),
        in_specs=[once((length, D), whole), once((length, D), whole), ANY, ANY],
        out_specs=[
            pl.BlockSpec((length, D), lambda j: (0, j)),
            once((1, length, D), lambda j: (0, 0, 0)),
        ],
        scratch_shapes=[whole_scratch(F32), whole_scratch(F32), whole_scratch(BF16)]
        + feed_forward_scratch(),
        out_shape=[
            jax.ShapeDtypeStruct((length, FF), BF16),
            jax.ShapeDtypeStruct((1, length, D), BF16),
        ],
        compiler_params=params(),
        cost_estimate=cost(25),
        name="forward_block",
    )(normed, middle, up[0], down[0])


FINISH = 256


def finish_backward(upstream, middle, grad_total, norm_ref, w_out, grad_middle, grad_attended, stores):
    gain = norm_ref[1:2]
    for index, rows in enumerate(row_tiles(D, FINISH)):
        for part in chunks(rows):
            grad = upstream[part].astype(F32) + norm_back(middle[part], gain, grad_total[part])
            grad_middle[part] = grad.astype(BF16)
        put_pairs(grad_attended, rows, dot_nt(grad_middle[rows], w_out).astype(BF16))
        for store in stores(rows, index):
            store.start()
    for index, rows in enumerate(row_tiles(D, FINISH)):
        for store in stores(rows, index):
            store.wait()


def turn_kernel(
    rows_at,
    spot_ref,
    norm_ref,
    normed_ref,
    middle_ref,
    upstream_ref,
    attention,
    up,
    down,
    out_ref,
    grad_middle_ref,
    grad_attended_ref,
    normed,
    middle,
    upstream,
    total,
    grad_total,
    inner,
    grad_act,
    out,
    grad_middle,
    grad_attended,
    up_weights,
    down_weights,
    out_weights,
    semaphores,
    load_semaphores,
    store_semaphores,
):
    activated, grad_inner = grad_middle, out
    loads = feed_forward_loads(up, down, rows_at[1:], up_weights, down_weights, semaphores)
    copy = pltpu.make_async_copy
    get_normed = copy(normed_ref, normed, load_semaphores.at[0])
    get_upstream = copy(upstream_ref.at[spot_ref[0]], upstream, load_semaphores.at[1])
    get_middle = copy(middle_ref, middle, load_semaphores.at[2])
    get_out = load_out(attention, rows_at[0], out_weights, load_semaphores.at[3])
    get_normed.start()
    loads[0][0].start()
    total[...] = jnp.zeros_like(total)
    grad_total[...] = jnp.zeros_like(grad_total)
    get_normed.wait()
    get_upstream.start()
    loads[0][1].start()

    def step(block, carry):
        wait_for(up_weights.at[block], semaphores.at[0, block])
        tiles = row_tiles(D, TILE)
        w_fc = matrix(up_weights, block)
        inner[0] = dot_nn(normed[tiles[0]], w_fc)
        pl.when(block == 0)(get_upstream.wait)
        wait_for(down_weights.at[block], semaphores.at[1, block])
        w_proj = matrix(down_weights, block)
        for later in range(1, BLOCKS):
            pl.when(block == later - 1)(lambda later=later: start_all(loads[later : later + 1]))

        @pl.when(block == BLOCKS - 1)
        def _():
            get_middle.start()
            get_out.start()

        grad_act[0] = dot_nt(upstream[tiles[0]], w_proj)
        for index, rows in enumerate(tiles):
            slot = index % 2
            if index + 1 < len(tiles):
                inner[1 - slot] = dot_nn(normed[tiles[index + 1]], w_fc)
                grad_act[1 - slot] = dot_nt(upstream[tiles[index + 1]], w_proj)
            for part in chunks(rows):
                here = shifted(part, -rows.start)
                value, slope = gelu_pair(inner[slot, here])
                activated[part] = value.astype(BF16)
                grad_inner[part] = (grad_act[slot, here] * slope).astype(BF16)
            total[rows] += dot_nn(activated[rows], w_proj)
            grad_total[rows] += dot_nt(grad_inner[rows], w_fc)
        return carry

    lax.fori_loop(0, BLOCKS, step, 0)
    get_middle.wait()
    for part in chunks(slice(0, D)):
        out[part] = (total[part] + middle[part]).astype(BF16)
    put_out = copy(out, out_ref.at[0], store_semaphores.at[0, 0])
    put_out.start()
    get_out.wait()

    def stores(rows, index):
        return (
            copy(grad_middle.at[rows], grad_middle_ref.at[rows], store_semaphores.at[1, index]),
            copy(grad_attended.at[:, rows], grad_attended_ref.at[:, rows], store_semaphores.at[2, index]),
        )

    finish_backward(
        upstream, middle, grad_total, norm_ref, matrix(out_weights), grad_middle, grad_attended, stores
    )
    put_out.wait()


TILE = 512
SCALARS = pl.BlockSpec(memory_space=pltpu.SMEM)
IN_VMEM = pl.BlockSpec(memory_space=pltpu.VMEM)


def whole_scratch(dtype):
    return pltpu.VMEM((D, D), dtype)


def turn_block(spot, normed, middle, upstream, norms, attention, up, down):
    length = normed.shape[0]
    return pl.pallas_call(
        functools.partial(turn_kernel, (attention[1], up[1], down[1])),
        in_specs=[SCALARS, IN_VMEM] + [ANY] * 6,
        out_specs=[ANY] * 3,
        scratch_shapes=[
            whole_scratch(BF16),
            whole_scratch(F32),
            whole_scratch(BF16),
            whole_scratch(F32),
            whole_scratch(F32),
            pltpu.VMEM((2, TILE, D), F32),
            pltpu.VMEM((2, TILE, D), F32),
            whole_scratch(BF16),
            whole_scratch(BF16),
            pltpu.VMEM((PAIRS, D, PAIR_DIM), BF16),
            across_scratch(BLOCKS),
            down_scratch(),
            pltpu.VMEM((SHARDS, SHARD_ROWS, D), BF16),
            pltpu.SemaphoreType.DMA((2, BLOCKS)),
            pltpu.SemaphoreType.DMA((4,)),
            pltpu.SemaphoreType.DMA((3, D // FINISH)),
        ],
        out_shape=[
            jax.ShapeDtypeStruct((1, length, D), BF16),
            jax.ShapeDtypeStruct((length, D), BF16),
            jax.ShapeDtypeStruct((PAIRS, length, PAIR_DIM), BF16),
        ],
        compiler_params=params(),
        cost_estimate=cost(42),
        name="turn_block",
    )(spot, norms, normed, middle, upstream, attention[0], up[0], down[0])


def backward_kernel(
    rows_at,
    norm_ref,
    slope_ref,
    middle_ref,
    upstream_ref,
    attention,
    up,
    down,
    grad_middle_ref,
    grad_attended_ref,
    slope,
    middle,
    upstream,
    grad_total,
    grad_act,
    grad_middle,
    grad_attended,
    up_weights,
    down_weights,
    out_weights,
    semaphores,
    load_semaphores,
    store_semaphores,
):
    grad_inner = grad_middle
    loads = feed_forward_loads(up, down, rows_at[1:], up_weights, down_weights, semaphores)
    copy = pltpu.make_async_copy
    get_upstream = copy(upstream_ref.at[0], upstream, load_semaphores.at[BLOCKS])
    get_middle = copy(middle_ref, middle, load_semaphores.at[BLOCKS + 1])
    get_out = load_out(attention, rows_at[0], out_weights, load_semaphores.at[BLOCKS + 2])
    get_slopes = [
        copy(slope_ref.at[:, pl.ds(block * D, D)], slope.at[block], load_semaphores.at[block])
        for block in range(BLOCKS)
    ]
    get_upstream.start()
    loads[0][1].start()
    grad_total[...] = jnp.zeros_like(grad_total)
    get_upstream.wait()
    get_slopes[0].start()
    loads[0][0].start()

    def step(block, carry):
        wait_for(down_weights.at[block], semaphores.at[1, block])
        w_proj = matrix(down_weights, block)
        tiles = row_tiles(D, TILE)
        grad_act[tiles[0]] = dot_nt(upstream[tiles[0]], w_proj)
        wait_for(slope.at[block], load_semaphores.at[block])
        wait_for(up_weights.at[block], semaphores.at[0, block])
        w_fc = matrix(up_weights, block)
        for later in range(1, BLOCKS):

            @pl.when(block == later - 1)
            def _(later=later):
                loads[later][1].start()
                get_slopes[later].start()
                loads[later][0].start()

        @pl.when(block == BLOCKS - 1)
        def _():
            get_middle.start()
            get_out.start()

        for index, rows in enumerate(tiles):
            if index + 1 < len(tiles):
                grad_act[tiles[index + 1]] = dot_nt(upstream[tiles[index + 1]], w_proj)
            for part in chunks(rows):
                grad_inner[part] = (grad_act[part] * slope[block, part].astype(F32)).astype(BF16)
            grad_total[rows] += dot_nt(grad_inner[rows], w_fc)
        return carry

    lax.fori_loop(0, BLOCKS, step, 0)
    get_middle.wait()
    get_out.wait()

    def stores(rows, index):
        return (
            copy(grad_middle.at[rows], grad_middle_ref.at[rows], store_semaphores.at[0, index]),
            copy(grad_attended.at[:, rows], grad_attended_ref.at[:, rows], store_semaphores.at[1, index]),
        )

    finish_backward(
        upstream, middle, grad_total, norm_ref, matrix(out_weights), grad_middle, grad_attended, stores
    )


def backward_block(upstream, slope, middle, norms, attention, up, down):
    length = middle.shape[0]
    return pl.pallas_call(
        functools.partial(backward_kernel, (attention[1], up[1], down[1])),
        in_specs=[IN_VMEM] + [ANY] * 6,
        out_specs=[ANY] * 2,
        scratch_shapes=[
            pltpu.VMEM((BLOCKS, D, D), BF16),
            whole_scratch(F32),
            whole_scratch(BF16),
            whole_scratch(F32),
            whole_scratch(F32),
            whole_scratch(BF16),
            pltpu.VMEM((PAIRS, D, PAIR_DIM), BF16),
            across_scratch(BLOCKS),
            down_scratch(),
            pltpu.VMEM((SHARDS, SHARD_ROWS, D), BF16),
            pltpu.SemaphoreType.DMA((2, BLOCKS)),
            pltpu.SemaphoreType.DMA((BLOCKS + 3,)),
            pltpu.SemaphoreType.DMA((2, D // FINISH)),
        ],
        out_shape=[
            jax.ShapeDtypeStruct((length, D), BF16),
            jax.ShapeDtypeStruct((PAIRS, length, PAIR_DIM), BF16),
        ],
        compiler_params=params(),
        cost_estimate=cost(25),
        name="backward_block",
    )(norms, slope, middle, upstream, attention[0], up[0], down[0])


UNPROJECT = 256


def unproject_kernel(
    row,
    which,
    spot_ref,
    norm_ref,
    grads_ref,
    hidden_ref,
    grad_middle_ref,
    array,
    out_ref,
    grads,
    hidden,
    grad_middle,
    out,
    total,
    weights,
    semaphores,
    load_semaphores,
    store_semaphores,
):
    copy = pltpu.make_async_copy
    tiles = row_tiles(D, UNPROJECT)
    get_weights = [load_qkv(array, row, part, weights, semaphores) for part in range(3)]
    get_grads = [
        [
            copy(
                grads_ref.at[part, :, rows], grads.at[part, :, rows], load_semaphores.at[index, part]
            )
            for part in range(3)
        ]
        for index, rows in enumerate(tiles)
    ]
    get_rest = [
        [
            copy(hidden_ref.at[spot_ref[which], rows], hidden.at[rows], load_semaphores.at[index, 3]),
            copy(grad_middle_ref.at[rows], grad_middle.at[rows], load_semaphores.at[index, 4]),
        ]
        for index, rows in enumerate(tiles)
    ]
    for part in range(3):
        get_weights[part].start()
        get_grads[0][part].start()
    stores = []
    gain = norm_ref[0:1]

    def finish(index, rows):
        for load in get_rest[index]:
            load.wait()
        for part in chunks(rows):
            here = shifted(part, -rows.start)
            back = norm_back(hidden[part].astype(F32), gain, total[index % 2, here])
            out[part] = (grad_middle[part].astype(F32) + back).astype(BF16)
        stores.append(copy(out.at[rows], out_ref.at[0, rows], store_semaphores.at[index]))
        stores[-1].start()

    for index, rows in enumerate(tiles):
        product = None
        for part in range(3):
            if index == 0:
                get_weights[part].wait()
            get_grads[index][part].wait()
            if part == 0:
                following = get_grads[index + 1] if index + 1 < len(tiles) else []
                for load in following + get_rest[index]:
                    load.start()
            term = dot_nt(get_pairs(grads, rows, part), matrix(weights, part))
            product = term if product is None else product + term
        total[index % 2] = product
        if index:
            finish(index - 1, tiles[index - 1])
    finish(len(tiles) - 1, tiles[-1])
    for store in stores:
        store.wait()


def unproject(spot, which, grads, hidden, grad_middle, norms, place):
    length = hidden.shape[1]
    count = D // UNPROJECT
    return pl.pallas_call(
        functools.partial(unproject_kernel, place[1], which),
        in_specs=[SCALARS, IN_VMEM] + [ANY] * 4,
        out_specs=ANY,
        scratch_shapes=[
            pltpu.VMEM((3, PAIRS, D, PAIR_DIM), BF16),
            whole_scratch(BF16),
            whole_scratch(BF16),
            whole_scratch(BF16),
            pltpu.VMEM((2, UNPROJECT, D), F32),
            across_scratch(3),
            pltpu.SemaphoreType.DMA((3,)),
            pltpu.SemaphoreType.DMA((count, 5)),
            pltpu.SemaphoreType.DMA((count,)),
        ],
        out_shape=jax.ShapeDtypeStruct((1, length, D), BF16),
        compiler_params=params(),
        cost_estimate=cost(11),
        name="unproject",
    )(spot, norms, grads, hidden, grad_middle, place[0])


def swap_sections(values):
    return lax.ppermute(values, "section", [(0, 1), (1, 0)])


def per_section(section_index, own):
    other = swap_sections(own)
    is_first = section_index == 0
    return jnp.where(is_first, own, other), jnp.where(is_first, other, own)


def halves(w_qkv, w_out, w_fc, w_proj):
    columns = lambda matrix: jnp.moveaxis(matrix.reshape(SHARD_ROWS, -1, D), 1, 0)
    attention = jnp.concatenate([columns(w_qkv), w_out[None]], axis=0).reshape(2, HALF, D)
    up = columns(w_fc).reshape(2, HALF, D)
    down = w_proj.reshape(2, HALF, D)
    return jnp.stack([attention, up, down], axis=1)


def gather_weights(is_first, w_qkv, w_out, w_fc, w_proj):
    if D // w_qkv.shape[1] == SHARDS:
        own = halves(w_qkv[0], w_out[0], w_fc[0], w_proj[0])
        received = swap_sections(jnp.where(is_first, own[1], own[0]))
        first = jnp.where(is_first, own[0], received)
        last = jnp.where(is_first, received, own[1])
        early = jnp.concatenate([first.reshape(3 * HALF, D), last[0]], axis=0)
        gather = lambda rows: lax.all_gather(rows, ("dp", "section"), axis=0).reshape(
            SHARDS, 2, -1, D
        )
        early, late = gather(early), gather(last[1:].reshape(2 * HALF, D))
    else:
        whole = lambda matrix: lax.all_gather(matrix[0], ("dp", "section"), axis=0)
        every = [whole(matrix) for matrix in (w_qkv, w_out, w_fc, w_proj)]
        layers = []
        for layer in range(2):
            mine = [matrix[layer::2] for matrix in every]
            shards = [matrix.reshape(SHARDS, -1, matrix.shape[-1]) for matrix in mine]
            layers.append(jax.vmap(halves)(*shards).reshape(SHARDS, 2, 3 * HALF, D))
        early = jnp.concatenate([layers[0], layers[1][:, :, :HALF]], axis=2)
        late = layers[1][:, :, HALF:]
    return (
        [(early, 0), (early, HALF), (early, 2 * HALF)],
        [(early, 3 * HALF), (late, 0), (late, HALF)],
    )


def reparam_hidden(table, w_first, b_first):
    return jnp.tanh(jnp.dot(table, w_first, precision=highest_mode) + b_first)


def reparam_out(hidden_units, w_second, b_second):
    return jnp.dot(hidden_units, w_second, precision=highest_mode) + b_second


def sum_dp(values):
    count = lax.axis_size("dp")
    step = 1
    while step < count:
        pairs = [(i, i ^ step) for i in range(count)]
        values = values + lax.ppermute(values, "dp", pairs)
        step *= 2
    return values


def per_device(
    tokens,
    seq_length,
    cotangent,
    ln_gain,
    ln_bias,
    w_qkv,
    w_out,
    w_fc,
    w_proj,
    prefix_table,
    reparam_w1,
    reparam_b1,
    reparam_w2,
    reparam_b2,
):
    section_index = lax.axis_index("section")
    is_first = section_index == 0
    first, last = gather_weights(is_first, w_qkv, w_out, w_fc, w_proj)
    spot = jnp.stack([section_index, jnp.zeros_like(section_index)]).astype(jnp.int32)
    seq = lax.dynamic_slice_in_dim(seq_length, section_index, 1, 0)

    table_values = prefix_table.astype(F32)
    first_weight = reparam_w1.astype(F32)
    first_bias = reparam_b1.astype(F32)
    second_weight = reparam_w2[0].astype(F32)
    second_bias = reparam_b2[0].astype(F32)
    hidden_units = reparam_hidden(table_values, first_weight, first_bias)
    prefix_kv = reparam_out(hidden_units, second_weight, second_bias).astype(BF16)
    pad = ((0, SLOTS - PREFIX), (0, 0))
    small = jnp.concatenate(
        [
            jnp.pad(prefix_kv[:, :D], pad),
            jnp.pad(prefix_kv[:, D:], pad),
            ln_gain[0],
            ln_bias[0],
            jnp.zeros((4, D), BF16),
        ],
        axis=0,
    )
    small_pair = per_section(section_index, small)
    pairs_apart = lambda rows: jnp.moveaxis(rows.reshape(SLOTS, PAIRS, PAIR_DIM), 1, 0)
    prefix_pair = [
        (pairs_apart(part[:SLOTS]), pairs_apart(part[SLOTS : 2 * SLOTS])) for part in small_pair
    ]
    norm_pair = [part[2 * SLOTS :].astype(F32) for part in small_pair]

    prefix_first, prefix_last = prefix_pair
    projected_first = project(spot, 0, tokens, norm_pair[0], first[0])
    attended_first, *probs_first = attend(seq, projected_first, *prefix_first)
    middle_first, normed = middle_block(spot, 0, attended_first, tokens, norm_pair[0], first[0])
    slope, handed = forward_block(normed, middle_first, *first[1:])
    projected = project(spot, 1, handed, norm_pair[1], last[0])
    attended, *probs = attend(seq, projected, *prefix_last)
    middle, normed = middle_block(spot, 1, attended, handed, norm_pair[1], last[0])
    final, grad_middle, grad_attended = turn_block(
        spot, normed, middle, cotangent, norm_pair[1], *last
    )
    grads, dkp_last, dvp_last = attend_back(
        seq, projected, attended, grad_attended, *prefix_last, *probs
    )
    grad_handed = unproject(spot, 1, grads, handed, grad_middle, norm_pair[1], last[0])
    grad_middle, grad_attended = backward_block(
        grad_handed, slope, middle_first, norm_pair[0], *first
    )
    grads, dkp_first, dvp_first = attend_back(
        seq, projected_first, attended_first, grad_attended, *prefix_first, *probs_first
    )
    grad_tokens = unproject(spot, 0, grads, tokens, grad_middle, norm_pair[0], first[0])

    def gathered_rows(first, last):
        kept = jnp.where(is_first, first, last)
        received = swap_sections(jnp.where(is_first, last, first))
        return jnp.concatenate(
            [jnp.where(is_first, kept, received), jnp.where(is_first, received, kept)], axis=0
        )

    activations = gathered_rows(handed, final)
    input_grads = gathered_rows(grad_tokens, grad_handed)

    pairs_joined = lambda rows: jnp.moveaxis(rows[:, :PREFIX], 0, 1).reshape(PREFIX, D)
    grad_first = jnp.concatenate([pairs_joined(dkp_first), pairs_joined(dvp_first)], axis=1)
    grad_last = jnp.concatenate([pairs_joined(dkp_last), pairs_joined(dvp_last)], axis=1)
    kept = jnp.where(is_first, grad_first, grad_last)
    received = swap_sections(jnp.where(is_first, grad_last, grad_first))
    prefix_total = sum_dp(kept + received)

    grad_hidden, grad_w2, grad_b2 = jax.vjp(reparam_out, hidden_units, second_weight, second_bias)[
        1
    ](prefix_total)
    grad_hidden = grad_hidden + swap_sections(grad_hidden)
    grad_table, grad_w1, grad_b1 = jax.vjp(reparam_hidden, table_values, first_weight, first_bias)[
        1
    ](grad_hidden)
    return (
        activations[None],
        input_grads[None],
        grad_table,
        grad_w1,
        grad_b1,
        grad_w2[None],
        grad_b2[None],
    )


def solution(mesh):
    in_specs = (
        P("dp", None, None),
        P("dp"),
        P("dp", None, None),
        P("section", None, None),
        P("section", None, None),
        P("section", "dp", None),
        P("section", "dp", None),
        P("section", "dp", None),
        P("section", "dp", None),
        P(),
        P(),
        P(),
        P("section", None, None),
        P("section", None),
    )
    out_specs = (
        P("section", "dp", None, None),
        P("section", "dp", None, None),
        P(),
        P(),
        P(),
        P("section", None, None),
        P("section", None),
    )
    return jax.shard_map(
        per_device, mesh=mesh, in_specs=in_specs, out_specs=out_specs, check_vma=False
    )
```

time: 665 us -> 563 us (0.85)
  waiting for transfers between devices: 286 us -> 201 us
  starting transfers between devices: 40.2 us -> 5.24 us
  Pallas kernels: 280 us -> 288 us
    all_gather x1 -> x2, waiting for transfers between devices: 273 us -> 188 us  [gather_weights(): lax.all_gather(rows, ('dp', 'section'), axis=0).reshape(SHARDS, 2, -1, D)]
    ppermute x5 -> x6, starting transfers between devices: 36.3 us -> 1.46 us  [swap_sections(): return lax.ppermute(values, 'section', [(0, 1), (1, 0)])]
    pallas_call x2, Pallas kernels: 54 us -> 61.3 us  [attend_back(): pl.pallas_call(attend_back_kernel, grid_spec=pltpu.PrefetchScalarGridSpec...]
    pallas_call x7 -> x9, Pallas kernels: 180 us -> 179 us  [the longest x1 48.6 us: turn_block(): pl.pallas_call(functools.partial(turn_kernel, (attention[1], up[1], down[...]
  transfers between devices with their start and end apart: 10 -> 12, of which waited for: 5 -> 6; matrix products, arithmetic and copies ran while one was open for 4% -> 6% of each run, Pallas kernels for 2% -> 24%
where the time goes in v2:
time: 563 us; the launch traced here: 558 us
  Pallas kernels  288 us (51%)
  waiting for transfers between devices  201 us (36%)
  other arithmetic  20.2 us (4%)
  local copies, waits for them, and re-layouts  15.8 us (3%)
  between operations  14.9 us (3%)
  matrix products  12 us (2%)
    all_gather x2, waiting for transfers between devices, gather_weights(): lax.all_gather(rows, ('dp', 'section'), axis=0).reshape(SHARDS, 2, -1, D)  188 us
    pallas_call x2, Pallas kernels, attend_back(): pl.pallas_call(attend_back_kernel, grid_spec=pltpu.PrefetchScalarGridSpec...  61.3 us
    pallas_call x1, Pallas kernels, turn_block(): pl.pallas_call(functools.partial(turn_kernel, (attention[1], up[1], down[...  48.6 us
    pallas_call x2, Pallas kernels, attend(): pl.pallas_call(attend_kernel, grid_spec=pltpu.PrefetchScalarGridSpec(num_...  47.6 us
    pallas_call x2, Pallas kernels, unproject(): pl.pallas_call(functools.partial(unproject_kernel, place[1], which), in_s...  30.4 us
    pallas_call x1, Pallas kernels, backward_block(): pl.pallas_call(functools.partial(backward_kernel, (attention[1], up[1], d...  28.1 us
    pallas_call x1, Pallas kernels, forward_block(): pl.pallas_call(functools.partial(forward_kernel, (up[1], down[1])), grid=...  27.2 us
    pallas_call x2, Pallas kernels, project(): pl.pallas_call(functools.partial(qkv_kernel, place[1]), grid_spec=pltpu.P...  26.6 us
  transfers between devices with their start and end apart: 12, of which 6 were waited for; matrix products, arithmetic and copies ran while one was open for 6% of the time, Pallas kernels for 24%

profile of v2, /device:TPU:0, one launch (start us, length us, event | category | flops | bytes accessed | tf_op | source)
XLA Modules:
  0.0 557.6 jit_solution(6428903683306893437)
XLA Ops:
  25.5 188.3 %all-gather.6.cloned.1.call-done = bf16[16384,1024]{1,0:T(8,128)(2,1)} async-done(((bf16[512,1024]{1,0:T(8,128)(2,1)}), bf16[16384,1024]{1,0:T(8,128)(2,1)}) %all-gather.6.cloned.1.call-update) | async-done | bytes 33554448 | tf_op jit(solution)/shard_map/all_gather | solution.py:1049
  213.8 13.2 %norm_project.2.q_ref.k_ref.v_ref = bf16[24,1024,128]{2,1,0:T(8,128)(2,1)} custom-call(s32[2]{0:T(128)} %pad_add_fusion.spot_ref, bf16[2,1024,1024]{2,1,0:T(8,128)(2,1)} %hidden_ref.5, f32[8,1024]{1,0:T(8,128)} %slice_convert_fusion.1.norm_ref, bf16[16,2,512,1024]{3,2,1,0:T(8,128)(2,1)} %bitcast.104), custom_call_target="tpu_custom_call" | custom-call | flops 13799999488 | bytes 1048576 | tf_op jit(solution)/shard_map/norm_project/pallas_call | solution.py:191
  227.0 23.6 %attend.2 = (bf16[8,1024,128]{2,1,0:T(8,128)(2,1)}, bf16[8,1040,2048]{2,1,0:T(8,128)(2,1)}, f32[8,1024,128]{2,1,0:T(8,128)}) custom-call(s32[1]{0:T(128)} %dynamic_slice.3.seq_ref, bf16[24,1024,128]{2,1,0:T(8,128)(2,1)} %norm_project.2.q_ref.k_ref.v_ref, bf16[24,1024,128]{2,1,0:T(8,128)(2,1)} %norm_project.2.q_ref.k_ref.v_ref, ...), custom_call_target="tpu_custom_call" | custom-call | flops 34500001792 | bytes 1048576 | tf_op jit(solution)/shard_map/attend/pallas_call | solution.py:342
  250.7 9.0 %middle_block.2 = (f32[1024,1024]{1,0:T(8,128)}, bf16[1024,1024]{1,0:T(8,128)(2,1)}) custom-call(s32[2]{0:T(128)} %pad_add_fusion.spot_ref, bf16[8,1024,128]{2,1,0:T(8,128)(2,1)} %get-tuple-element.30.attended_ref.out_ref, bf16[2,1024,1024]{2,1,0:T(8,128)(2,1)} %hidden_ref.5, f32[8,1024]{1,0:T(8,128)} %slice_convert_fusion.1.norm_ref, ...), custom_call_target="tpu_custom_call" | custom-call | flops 5750000128 | bytes 1048576 | tf_op jit(solution)/shard_map/middle_block/pallas_call | solution.py:524
  259.7 27.2 %forward_block.1 = (bf16[1024,4096]{1,0:T(8,128)(2,1)}, bf16[1,1024,1024]{2,1,0:T(8,128)(2,1)}) custom-call(bf16[1024,1024]{1,0:T(8,128)(2,1)} %get-tuple-element.31.normed_ref, f32[1024,1024]{1,0:T(8,128)} %get-tuple-element.32.middle_ref, bf16[16,2,512,1024]{3,2,1,0:T(8,128)(2,1)} %bitcast.106, bf16[16,2,512,1024]{3,2,1,0:T(8,128)(2,1)} %bitcast.107), custom_call_target="tpu_custom_call" | custom-call | flops 28750000128 | bytes 1048576 | tf_op jit(solution)/shard_map/forward_block/pallas_call | solution.py:627
  286.9 13.3 %norm_project.3.q_ref.k_ref.v_ref = bf16[24,1024,128]{2,1,0:T(8,128)(2,1)} custom-call(s32[2]{0:T(128)} %pad_add_fusion.spot_ref, bf16[1,1024,1024]{2,1,0:T(8,128)(2,1)} %get-tuple-element.33.hidden_ref, f32[8,1024]{1,0:T(8,128)} %slice_convert_fusion.norm_ref, bf16[16,2,512,1024]{3,2,1,0:T(8,128)(2,1)} %bitcast.108), custom_call_target="tpu_custom_call" | custom-call | flops 13799999488 | bytes 1048576 | tf_op jit(solution)/shard_map/norm_project/pallas_call | solution.py:191
  300.3 23.9 %attend.3 = (bf16[8,1024,128]{2,1,0:T(8,128)(2,1)}, bf16[8,1040,2048]{2,1,0:T(8,128)(2,1)}, f32[8,1024,128]{2,1,0:T(8,128)}) custom-call(s32[1]{0:T(128)} %dynamic_slice.3.seq_ref, bf16[24,1024,128]{2,1,0:T(8,128)(2,1)} %norm_project.3.q_ref.k_ref.v_ref, bf16[24,1024,128]{2,1,0:T(8,128)(2,1)} %norm_project.3.q_ref.k_ref.v_ref, ...), custom_call_target="tpu_custom_call" | custom-call | flops 34500001792 | bytes 1048576 | tf_op jit(solution)/shard_map/attend/pallas_call | solution.py:342
  324.2 9.3 %middle_block.3 = (f32[1024,1024]{1,0:T(8,128)}, bf16[1024,1024]{1,0:T(8,128)(2,1)}) custom-call(s32[2]{0:T(128)} %pad_add_fusion.spot_ref, bf16[8,1024,128]{2,1,0:T(8,128)(2,1)} %get-tuple-element.34.attended_ref.out_ref, bf16[1,1024,1024]{2,1,0:T(8,128)(2,1)} %get-tuple-element.33.hidden_ref, f32[8,1024]{1,0:T(8,128)} %slice_convert_fusion.norm_ref, ...), custom_call_target="tpu_custom_call" | custom-call | flops 5750000128 | bytes 1048576 | tf_op jit(solution)/shard_map/middle_block/pallas_call | solution.py:524
  333.5 48.6 %turn_block.1 = (bf16[1,1024,1024]{2,1,0:T(8,128)(2,1)}, bf16[1024,1024]{1,0:T(8,128)(2,1)}, bf16[8,1024,128]{2,1,0:T(8,128)(2,1)}) custom-call(s32[2]{0:T(128)} %pad_add_fusion.spot_ref, f32[8,1024]{1,0:T(8,128)} %slice_convert_fusion.norm_ref, bf16[1024,1024]{1,0:T(8,128)(2,1)} %get-tuple-element.35.normed_ref, f32[1024,1024]{1,0:T(8,128)} %get-tuple-element.36.middle_ref, ...), custom_call_target="tpu_custom_call" | custom-call | flops 48299999232 | bytes 1048576 | tf_op jit(solution)/shard_map/turn_block/pallas_call | solution.py:771
  382.2 30.5 %attend_back.2 = (bf16[3,8,1024,128]{3,2,1,0:T(8,128)(2,1)}, f32[8,16,128]{2,1,0:T(8,128)}, f32[8,16,128]{2,1,0:T(8,128)}) custom-call(s32[1]{0:T(128)} %dynamic_slice.3.seq_ref, bf16[24,1024,128]{2,1,0:T(8,128)(2,1)} %norm_project.3.q_ref.k_ref.v_ref, bf16[24,1024,128]{2,1,0:T(8,128)(2,1)} %norm_project.3.q_ref.k_ref.v_ref, ...), custom_call_target="tpu_custom_call" | custom-call | flops 34500001792 | bytes 1048576 | tf_op jit(solution)/shard_map/attend_back/pallas_call | solution.py:452
  412.7 15.2 %unproject.2.upstream_ref = bf16[1,1024,1024]{2,1,0:T(8,128)(2,1)} custom-call(s32[2]{0:T(128)} %pad_add_fusion.spot_ref, f32[8,1024]{1,0:T(8,128)} %slice_convert_fusion.norm_ref, bf16[3,8,1024,128]{3,2,1,0:T(8,128)(2,1)} %get-tuple-element.42.grads_ref, bf16[1,1024,1024]{2,1,0:T(8,128)(2,1)} %get-tuple-element.33.hidden_ref, ...), custom_call_target="tpu_custom_call" | custom-call | flops 12650000384 | bytes 1048576 | tf_op jit(solution)/shard_map/unproject/pallas_call | solution.py:1002
  427.9 28.1 %backward_block.1 = (bf16[1024,1024]{1,0:T(8,128)(2,1)}, bf16[8,1024,128]{2,1,0:T(8,128)(2,1)}) custom-call(f32[8,1024]{1,0:T(8,128)} %slice_convert_fusion.1.norm_ref, bf16[1024,4096]{1,0:T(8,128)(2,1)} %get-tuple-element.38.slope_ref, f32[1024,1024]{1,0:T(8,128)} %get-tuple-element.32.middle_ref, bf16[1,1024,1024]{2,1,0:T(8,128)(2,1)} %unproject.2.upstream_ref, ...), custom_call_target="tpu_custom_call" | custom-call | flops 28750000128 | bytes 1048576 | tf_op jit(solution)/shard_map/backward_block/pallas_call | solution.py:892
  456.0 30.8 %attend_back.3 = (bf16[3,8,1024,128]{3,2,1,0:T(8,128)(2,1)}, f32[8,16,128]{2,1,0:T(8,128)}, f32[8,16,128]{2,1,0:T(8,128)}) custom-call(s32[1]{0:T(128)} %dynamic_slice.3.seq_ref, bf16[24,1024,128]{2,1,0:T(8,128)(2,1)} %norm_project.2.q_ref.k_ref.v_ref, bf16[24,1024,128]{2,1,0:T(8,128)(2,1)} %norm_project.2.q_ref.k_ref.v_ref, ...), custom_call_target="tpu_custom_call" | custom-call | flops 34500001792 | bytes 1048576 | tf_op jit(solution)/shard_map/attend_back/pallas_call | solution.py:452
  492.0 4.3 collective-permute-done.5
  496.4 3.1 broadcast_select_fusion.6
  501.5 15.2 %unproject.3 = bf16[1,1024,1024]{2,1,0:T(8,128)(2,1)} custom-call(s32[2]{0:T(128)} %pad_add_fusion.spot_ref, f32[8,1024]{1,0:T(8,128)} %slice_convert_fusion.1.norm_ref, bf16[3,8,1024,128]{3,2,1,0:T(8,128)(2,1)} %get-tuple-element.47.grads_ref, bf16[2,1024,1024]{2,1,0:T(8,128)(2,1)} %hidden_ref.5, bf16[1024,1024]{1,0:T(8,128)(2,1)} %get-tuple-element.48.grad_middle_ref, ...), custom_call_target="tpu_custom_call" | custom-call | flops 12650000384 | bytes 1048576 | tf_op jit(solution)/shard_map/unproject/pallas_call | solution.py:1002
  518.3 3.1 broadcast_select_fusion.2
  521.4 3.9 collective-permute-done.8
  527.1 5.2 convolution_bitcast_fusion
  533.6 2.4 convolution_bitcast_fusion.1
  535.9 3.0 copy.67
  542.5 2.5 maximum_bitcast_fusion
  546.2 2.0 broadcast_select_fusion.1
  548.2 2.4 maximum_bitcast_fusion.1
  (126 shorter events, 34.4 us)
Async XLA Ops:
  7.2 11.6 %copy-start = (bf16[1024,512]{1,0:T(8,128)(2,1)S(1)}, bf16[1024,512]{1,0:T(8,128)(2,1)}, u32[]{:S(2)}) copy-start(bf16[1024,512]{1,0:T(8,128)(2,1)} %param.24) | copy-start | bytes 3145732
  7.2 3.7 copy-start.10
  7.2 206.6 %all-gather.6.cloned.1.call-start = ((), (), s32[]{:S(2)}) async-start(), calls=%async_computation.1 | async-start | bytes 34603008 | tf_op jit(solution)/shard_map/all_gather | solution.py:1049
  11.7 2.4 collective-permute-start.1
  15.2 3.6 copy-start.16
  15.2 3.6 copy-start.12
  16.2 317.3 %all-gather.4.cloned.1.call-start = ((), (), s32[]{:S(2)}) async-start(), calls=%async_computation | async-start | bytes 17301504 | tf_op jit(solution)/shard_map/all_gather | solution.py:1049
  20.2 1.6 collective-permute-start
  456.0 32.8 %copy-start.15 = (f32[8,16,128]{2,1,0:T(8,128)S(1)}, f32[8,16,128]{2,1,0:T(8,128)}, u32[]{:S(2)}) copy-start(f32[8,16,128]{2,1,0:T(8,128)} %get-tuple-element.51) | copy-start | bytes 196612
  456.0 32.9 %copy-start.14 = (f32[8,16,128]{2,1,0:T(8,128)S(1)}, f32[8,16,128]{2,1,0:T(8,128)}, u32[]{:S(2)}) copy-start(f32[8,16,128]{2,1,0:T(8,128)} %get-tuple-element.52) | copy-start | bytes 196612
  486.8 9.6 %copy-start.2 = (bf16[1,1024,1024]{2,1,0:T(8,128)(2,1)S(1)}, bf16[1,1024,1024]{2,1,0:T(8,128)(2,1)}, u32[]{:S(2)}) copy-start(bf16[1,1024,1024]{2,1,0:T(8,128)(2,1)} %get-tuple-element.33.hidden_ref) | copy-start | bytes 6291460
  489.0 1.5 collective-permute-start.4
  490.5 5.8 %collective-permute-start.5 = (f32[10,2048]{1,0:T(8,128)S(1)}, f32[10,2048]{1,0:T(8,128)S(1)}, u32[]{:S(2)}, u32[]{:S(2)}) collective-permute-start(f32[10,2048]{1,0:T(8,128)S(1)} %select_add_fusion), channel_id=1, source_target_pairs={{0,2},{2,0},{4,6},{6,4},{8,10},{10,8},{12,14},{14,12},{16,18},{18,... | collective-permute-start | bytes 245768 | tf_op jit(solution)/shard_map/ppermute | solution.py:1082
  496.4 5.0 collective-permute-start.6
  499.6 40.9 %collective-permute-start.2 = (bf16[1,1024,1024]{2,1,0:T(8,128)(2,1)}, bf16[1,1024,1024]{2,1,0:T(8,128)(2,1)}, u32[]{:S(2)}, u32[]{:S(2)}) collective-permute-start(bf16[1,1024,1024]{2,1,0:T(8,128)(2,1)} %broadcast_select_fusion.6), channel_id=1, source_target_pairs={{0,1},{1,0},{2,3},{3,2},{4,5},{5,4},{6,7},{7,6},{8,9},{9,8},{10,11... | collective-permute-start | bytes 6291464 | tf_op jit(solution)/shard_map/ppermute | solution.py:1025
  501.4 15.3 %collective-permute-start.7 = (f32[10,2048]{1,0:T(8,128)S(1)}, f32[10,2048]{1,0:T(8,128)S(1)}, u32[]{:S(2)}, u32[]{:S(2)}) collective-permute-start(f32[10,2048]{1,0:T(8,128)S(1)} %add.62), channel_id=1, source_target_pairs={{0,8},{2,10},{4,12},{6,14},{8,0},{10,2},{12,4},{14,6},{16,24},{18,... | collective-permute-start | bytes 245768 | tf_op jit(solution)/shard_map/ppermute | solution.py:1082
  516.8 8.6 %copy-start.6 = (bf16[1,512,2048]{2,1,0:T(8,128)(2,1)S(1)}, bf16[1,512,2048]{2,1,0:T(8,128)(2,1)}, u32[]{:S(2)}) copy-start(bf16[1,512,2048]{2,1,0:T(8,128)(2,1)} %param.26) | copy-start | bytes 6291460
  516.8 8.6 %collective-permute-start.8 = (f32[10,2048]{1,0:T(8,128)S(1)}, f32[10,2048]{1,0:T(8,128)S(1)}, u32[]{:S(2)}, u32[]{:S(2)}) collective-permute-start(f32[10,2048]{1,0:T(8,128)S(1)} %add.63), channel_id=1, source_target_pairs={{0,16},{2,18},{4,20},{6,22},{8,24},{10,26},{12,28},{14,30},{16,0},... | collective-permute-start | bytes 245768 | tf_op jit(solution)/shard_map/ppermute | solution.py:1082
  521.4 5.7 %copy-start.9 = (f32[10,512]{1,0:T(8,128)S(1)}, f32[10,512]{1,0:T(8,128)}, u32[]{:S(2)}) copy-start(f32[10,512]{1,0:T(8,128)} %copy-done.8) | copy-start | bytes 61444
  521.4 23.6 %collective-permute-start.3 = (bf16[1,1024,1024]{2,1,0:T(8,128)(2,1)}, bf16[1,1024,1024]{2,1,0:T(8,128)(2,1)}, u32[]{:S(2)}, u32[]{:S(2)}) collective-permute-start(bf16[1,1024,1024]{2,1,0:T(8,128)(2,1)} %broadcast_select_fusion.2), channel_id=1, source_target_pairs={{0,1},{1,0},{2,3},{3,2},{4,5},{5,4},{6,7},{7,6},{8,9},{9,8},{10,11... | collective-permute-start | bytes 6291464 | tf_op jit(solution)/shard_map/ppermute | solution.py:1025
  527.1 6.5 %copy-start.13 = (bf16[10,1024]{1,0:T(8,128)(2,1)S(1)}, bf16[10,1024]{1,0:T(8,128)(2,1)}, u32[]{:S(2)}) copy-start(bf16[10,1024]{1,0:T(8,128)(2,1)} %param.23) | copy-start | bytes 61444
  527.1 5.9 %collective-permute-start.9 = (f32[10,512]{1,0:T(8,128)S(1)}, f32[10,512]{1,0:T(8,128)S(1)}, u32[]{:S(2)}, u32[]{:S(2)}) collective-permute-start(f32[10,512]{1,0:T(8,128)S(1)} %fusion.1), channel_id=1, source_target_pairs={{0,1},{1,0},{2,3},{3,2},{4,5},{5,4},{6,7},{7,6},{8,9},{9,8},{10,11... | collective-permute-start | bytes 61448 | tf_op jit(solution)/shard_map/ppermute | solution.py:1025
  535.9 4.6 copy-start.3
  542.5 3.7 copy-start.4
  (9 other events, 16.8 us)
Sparse Core Ops, SparseCore 0:
  16.4 197.3 all-gather.5
  216.7 113.0 all-gather.3

commit v3 on v2

--- a/solution.py
+++ b/solution.py
@@ -13,6 +13,7 @@
 FF = 4096
 PREFIX = 10
 SLOTS = 16
+BOTH = 24
 PAIRS = 8
 PAIR_DIM = 128
 BLOCK = 256
@@ -381,8 +382,7 @@
     probs_ref,
     scale_ref,
     grads_ref,
-    dkp_ref,
-    dvp_ref,
+    prefix_ref,
     values,
     keys_t,
     dk,
@@ -442,8 +442,9 @@
     either_length(seq_ref, length, run)
     grads_ref[1, 0] = dk[SLOTS:].astype(BF16)
     grads_ref[2, 0] = dv[SLOTS:].astype(BF16)
-    dkp_ref[0] = dk[:SLOTS]
-    dvp_ref[0] = dv[:SLOTS]
+    prefix_ref[0, :PREFIX] = dk[:PREFIX]
+    prefix_ref[0, PREFIX : 2 * PREFIX] = dv[:PREFIX]
+    prefix_ref[0, 2 * PREFIX :] = jnp.zeros_like(prefix_ref[0, 2 * PREFIX :])
 
 
 def attend_back(seq, projected, attended, grad_attended, prefix_keys, prefix_values, probs, scale):
@@ -467,8 +468,7 @@
             ],
             out_specs=[
                 pl.BlockSpec((3, 1, length, PAIR_DIM), lambda p, s: (0, p, 0, 0)),
-                pair_spec(SLOTS, 0),
-                pair_spec(SLOTS, 0),
+                pair_spec(BOTH, 0),
             ],
             scratch_shapes=[
                 pltpu.VMEM(ext, BF16),
@@ -481,8 +481,7 @@
         ),
         out_shape=[
             jax.ShapeDtypeStruct((3, PAIRS, length, PAIR_DIM), BF16),
-            jax.ShapeDtypeStruct((PAIRS, SLOTS, PAIR_DIM), F32),
-            jax.ShapeDtypeStruct((PAIRS, SLOTS, PAIR_DIM), F32),
+            jax.ShapeDtypeStruct((PAIRS, BOTH, PAIR_DIM), F32),
         ],
         compiler_params=params(),
         cost_estimate=cost(30),
@@ -668,10 +667,12 @@
     normed_ref,
     middle_ref,
     upstream_ref,
+    hidden_ref,
     attention,
     up,
     down,
     out_ref,
+    sent_ref,
     grad_middle_ref,
     grad_attended_ref,
     normed,
@@ -743,6 +744,11 @@
         out[part] = (total[part] + middle[part]).astype(BF16)
     put_out = copy(out, out_ref.at[0], store_semaphores.at[0, 0])
     put_out.start()
+    put_sent = copy(out, sent_ref.at[0], store_semaphores.at[0, 1])
+    get_hidden = copy(hidden_ref.at[0], normed, load_semaphores.at[4])
+    put_hidden = copy(normed, sent_ref.at[0], store_semaphores.at[0, 1])
+    pl.when(spot_ref[0] == 0)(put_sent.start)
+    pl.when(spot_ref[0] != 0)(get_hidden.start)
     get_out.wait()
 
     def stores(rows, index):
@@ -756,6 +762,13 @@
     )
     put_out.wait()
 
+    @pl.when(spot_ref[0] != 0)
+    def _():
+        get_hidden.wait()
+        put_hidden.start()
+
+    put_sent.wait()
+
 
 TILE = 512
 SCALARS = pl.BlockSpec(memory_space=pltpu.SMEM)
@@ -766,12 +779,12 @@
     return pltpu.VMEM((D, D), dtype)
 
 
-def turn_block(spot, normed, middle, upstream, norms, attention, up, down):
+def turn_block(spot, normed, middle, upstream, hidden, norms, attention, up, down):
     length = normed.shape[0]
     return pl.pallas_call(
         functools.partial(turn_kernel, (attention[1], up[1], down[1])),
-        in_specs=[SCALARS, IN_VMEM] + [ANY] * 6,
-        out_specs=[ANY] * 3,
+        in_specs=[SCALARS, IN_VMEM] + [ANY] * 7,
+        out_specs=[ANY] * 4,
         scratch_shapes=[
             whole_scratch(BF16),
             whole_scratch(F32),
@@ -787,10 +800,11 @@
             down_scratch(),
             pltpu.VMEM((SHARDS, SHARD_ROWS, D), BF16),
             pltpu.SemaphoreType.DMA((2, BLOCKS)),
-            pltpu.SemaphoreType.DMA((4,)),
+            pltpu.SemaphoreType.DMA((5,)),
             pltpu.SemaphoreType.DMA((3, D // FINISH)),
         ],
         out_shape=[
+            jax.ShapeDtypeStruct((1, length, D), BF16),
             jax.ShapeDtypeStruct((1, length, D), BF16),
             jax.ShapeDtypeStruct((length, D), BF16),
             jax.ShapeDtypeStruct((PAIRS, length, PAIR_DIM), BF16),
@@ -798,18 +812,23 @@
         compiler_params=params(),
         cost_estimate=cost(42),
         name="turn_block",
-    )(spot, norms, normed, middle, upstream, attention[0], up[0], down[0])
+    )(spot, norms, normed, middle, upstream, hidden, attention[0], up[0], down[0])
 
 
 def backward_kernel(
     rows_at,
+    spot_ref,
     norm_ref,
     slope_ref,
     middle_ref,
     upstream_ref,
+    first_ref,
+    last_ref,
+    received_ref,
     attention,
     up,
     down,
+    activations_ref,
     grad_middle_ref,
     grad_attended_ref,
     slope,
@@ -825,13 +844,20 @@
     semaphores,
     load_semaphores,
     store_semaphores,
+    activations,
+    output_semaphores,
 ):
     grad_inner = grad_middle
+    section = spot_ref[0]
     loads = feed_forward_loads(up, down, rows_at[1:], up_weights, down_weights, semaphores)
     copy = pltpu.make_async_copy
     get_upstream = copy(upstream_ref.at[0], upstream, load_semaphores.at[BLOCKS])
     get_middle = copy(middle_ref, middle, load_semaphores.at[BLOCKS + 1])
     get_out = load_out(attention, rows_at[0], out_weights, load_semaphores.at[BLOCKS + 2])
+    take = copy(received_ref.at[0], activations.at[1 - section], output_semaphores.at[0])
+    keep_first = copy(first_ref.at[0], activations.at[section], output_semaphores.at[1])
+    keep_last = copy(last_ref.at[0], activations.at[section], output_semaphores.at[1])
+    put_activations = copy(activations, activations_ref, output_semaphores.at[2])
     get_slopes = [
         copy(slope_ref.at[:, pl.ds(block * D, D)], slope.at[block], load_semaphores.at[block])
         for block in range(BLOCKS)
@@ -864,6 +890,18 @@
             get_middle.start()
             get_out.start()
 
+        @pl.when(block == 1)
+        def _():
+            take.start()
+            pl.when(section == 0)(keep_first.start)
+            pl.when(section != 0)(keep_last.start)
+
+        @pl.when(block == 2)
+        def _():
+            take.wait()
+            keep_first.wait()
+            put_activations.start()
+
         for index, rows in enumerate(tiles):
             if index + 1 < len(tiles):
                 grad_act[tiles[index + 1]] = dot_nt(upstream[tiles[index + 1]], w_proj)
@@ -885,14 +923,15 @@
     finish_backward(
         upstream, middle, grad_total, norm_ref, matrix(out_weights), grad_middle, grad_attended, stores
     )
-
-
-def backward_block(upstream, slope, middle, norms, attention, up, down):
+    put_activations.wait()
+
+
+def backward_block(spot, upstream, slope, middle, outputs, norms, attention, up, down):
     length = middle.shape[0]
     return pl.pallas_call(
         functools.partial(backward_kernel, (attention[1], up[1], down[1])),
-        in_specs=[IN_VMEM] + [ANY] * 6,
-        out_specs=[ANY] * 2,
+        in_specs=[SCALARS, IN_VMEM] + [ANY] * 9,
+        out_specs=[ANY] * 3,
         scratch_shapes=[
             pltpu.VMEM((BLOCKS, D, D), BF16),
             whole_scratch(F32),
@@ -907,15 +946,18 @@
             pltpu.SemaphoreType.DMA((2, BLOCKS)),
             pltpu.SemaphoreType.DMA((BLOCKS + 3,)),
             pltpu.SemaphoreType.DMA((2, D // FINISH)),
+            pltpu.VMEM((2, D, D), BF16),
+            pltpu.SemaphoreType.DMA((3,)),
         ],
         out_shape=[
+            jax.ShapeDtypeStruct((2, length, D), BF16),
             jax.ShapeDtypeStruct((length, D), BF16),
             jax.ShapeDtypeStruct((PAIRS, length, PAIR_DIM), BF16),
         ],
         compiler_params=params(),
         cost_estimate=cost(25),
         name="backward_block",
-    )(norms, slope, middle, upstream, attention[0], up[0], down[0])
+    )(spot, norms, slope, middle, upstream, *outputs, attention[0], up[0], down[0])
 
 
 UNPROJECT = 256
@@ -930,6 +972,25 @@
     hidden_ref,
     grad_middle_ref,
     array,
+    *refs,
+):
+    last = (*refs[:3], *refs[-2:]) if len(refs) > 10 else None
+    out_ref, *refs = (refs[3:5], *refs[5:-2]) if last else refs
+    unproject_body(
+        row, which, spot_ref, norm_ref, grads_ref, hidden_ref, grad_middle_ref, array, last, out_ref, *refs
+    )
+
+
+def unproject_body(
+    row,
+    which,
+    spot_ref,
+    norm_ref,
+    grads_ref,
+    hidden_ref,
+    grad_middle_ref,
+    array,
+    last,
     out_ref,
     grads,
     hidden,
@@ -943,6 +1004,14 @@
 ):
     copy = pltpu.make_async_copy
     tiles = row_tiles(D, UNPROJECT)
+    if last:
+        kept_ref, received_ref, outputs_ref, rows_of_two, last_semaphores = last
+        get_others = [
+            copy(received_ref.at[0], rows_of_two.at[0], last_semaphores.at[0]),
+            copy(kept_ref.at[0], rows_of_two.at[1], last_semaphores.at[1]),
+        ]
+        put_others = copy(rows_of_two, outputs_ref, last_semaphores.at[2])
+
     get_weights = [load_qkv(array, row, part, weights, semaphores) for part in range(3)]
     get_grads = [
         [
@@ -973,10 +1042,35 @@
             here = shifted(part, -rows.start)
             back = norm_back(hidden[part].astype(F32), gain, total[index % 2, here])
             out[part] = (grad_middle[part].astype(F32) + back).astype(BF16)
-        stores.append(copy(out.at[rows], out_ref.at[0, rows], store_semaphores.at[index]))
-        stores[-1].start()
+        if last:
+            piece, start = divmod(rows.start, D // 2)
+            target = out_ref[piece].at[0, start : start + UNPROJECT]
+        else:
+            target = out_ref.at[0, rows]
+        stores.append(copy(out.at[rows], target, store_semaphores.at[index]))
+        if last:
+            pl.when(spot_ref[0] != 0)(stores[-1].start)
+            straight = copy(out.at[rows], outputs_ref.at[0, rows], store_semaphores.at[index])
+            pl.when(spot_ref[0] == 0)(straight.start)
+        else:
+            stores[-1].start()
 
     for index, rows in enumerate(tiles):
+        if last and index == 1:
+
+            @pl.when(spot_ref[0] != 0)
+            def _():
+                for other in get_others:
+                    other.start()
+
+        if last and index == 3:
+
+            @pl.when(spot_ref[0] != 0)
+            def _():
+                for other in get_others:
+                    other.wait()
+                put_others.start()
+
         product = None
         for part in range(3):
             if index == 0:
@@ -994,15 +1088,19 @@
     finish(len(tiles) - 1, tiles[-1])
     for store in stores:
         store.wait()
-
-
-def unproject(spot, which, grads, hidden, grad_middle, norms, place):
+    if last:
+        pl.when(spot_ref[0] != 0)(put_others.wait)
+
+
+def unproject(spot, which, grads, hidden, grad_middle, norms, place, others=()):
     length = hidden.shape[1]
     count = D // UNPROJECT
+    row = jax.ShapeDtypeStruct((1, length, D), BF16)
+    piece = jax.ShapeDtypeStruct((1, length // 2, D), BF16)
     return pl.pallas_call(
         functools.partial(unproject_kernel, place[1], which),
-        in_specs=[SCALARS, IN_VMEM] + [ANY] * 4,
-        out_specs=ANY,
+        in_specs=[SCALARS, IN_VMEM] + [ANY] * (4 + len(others)),
+        out_specs=[ANY] * 3 if others else ANY,
         scratch_shapes=[
             pltpu.VMEM((3, PAIRS, D, PAIR_DIM), BF16),
             whole_scratch(BF16),
@@ -1013,12 +1111,156 @@
             pltpu.SemaphoreType.DMA((3,)),
             pltpu.SemaphoreType.DMA((count, 5)),
             pltpu.SemaphoreType.DMA((count,)),
-        ],
-        out_shape=jax.ShapeDtypeStruct((1, length, D), BF16),
+        ]
+        + ([pltpu.VMEM((2, D, D), BF16), pltpu.SemaphoreType.DMA((3,))] if others else []),
+        out_shape=[jax.ShapeDtypeStruct((2, length, D), BF16), piece, piece] if others else row,
         compiler_params=params(),
         cost_estimate=cost(11),
         name="unproject",
-    )(spot, norms, grads, hidden, grad_middle, place[0])
+    )(spot, norms, grads, hidden, grad_middle, place[0], *others)
+
+
+def place_kernel(spot_ref, outputs_in, top_ref, bottom_ref, outputs_ref, buffer, semaphores):
+    del outputs_in
+    half = D // 2
+    tiles = row_tiles(D, 256)
+    loads = [
+        pltpu.make_async_copy(
+            (bottom_ref if rows.start >= half else top_ref).at[0, pl.ds(rows.start % half, 256)],
+            buffer.at[rows],
+            semaphores.at[0, index],
+        )
+        for index, rows in enumerate(tiles)
+    ]
+    stores = [
+        pltpu.make_async_copy(buffer.at[rows], outputs_ref.at[1, rows], semaphores.at[1, index])
+        for index, rows in enumerate(tiles)
+    ]
+
+    @pl.when(spot_ref[0] == 0)
+    def _():
+        for load in loads:
+            load.start()
+        for load, store in zip(loads, stores):
+            load.wait()
+            store.start()
+        for store in stores:
+            store.wait()
+
+
+def place_received(spot, outputs, pieces):
+    return pl.pallas_call(
+        place_kernel,
+        in_specs=[SCALARS, ANY, ANY, ANY],
+        out_specs=ANY,
+        scratch_shapes=[whole_scratch(BF16), pltpu.SemaphoreType.DMA((2, 4))],
+        out_shape=jax.ShapeDtypeStruct(outputs.shape, outputs.dtype),
+        input_output_aliases={1: 0},
+        compiler_params=params(),
+        cost_estimate=cost(2),
+        name="place_received",
+    )(spot, outputs, *pieces)
+
+
+def three_terms(values):
+    high = values.astype(BF16)
+    rest = values - high.astype(F32)
+    middle = rest.astype(BF16)
+    return high, middle, (rest - middle.astype(F32)).astype(BF16)
+
+
+def exact_nt(values, right):
+    count = values.shape[0]
+    product = dot_nt(jnp.concatenate(three_terms(values), axis=0), right)
+    return (product[2 * count :] + product[count : 2 * count]) + product[:count]
+
+
+def exact_tn(left, right):
+    high, middle, low = three_terms(left)
+    first, second, third = three_terms(right)
+    return dot_tn(
+        jnp.concatenate([low, middle, high, middle, high, high], axis=0),
+        jnp.concatenate([first, second, third, first, second, first], axis=0),
+    )
+
+
+def joined(ref):
+    return jnp.concatenate(
+        [
+            ref[pair, part * PREFIX : (part + 1) * PREFIX]
+            for part in range(2)
+            for pair in range(PAIRS)
+        ],
+        axis=1,
+    )
+
+
+def hidden_kernel(total_ref, w2_ref, out_ref, total):
+    total[...] = jnp.zeros_like(total)
+    total[:PREFIX] = joined(total_ref)
+    out_ref[...] = exact_nt(total[...], w2_ref[0])
+
+
+def hidden_back(total, w2):
+    return pl.pallas_call(
+        hidden_kernel,
+        in_specs=[IN_VMEM] * 2,
+        out_specs=IN_VMEM,
+        scratch_shapes=[pltpu.VMEM((SLOTS, 2 * D), F32)],
+        out_shape=jax.ShapeDtypeStruct((SLOTS, w2.shape[1]), F32),
+        compiler_params=params(),
+        cost_estimate=cost(2),
+        name="hidden_back",
+    )(total, w2)
+
+
+def second_kernel(total_ref, hidden_ref, w2_out, b2_out, total):
+    total[...] = jnp.zeros_like(total)
+    total[:PREFIX] = joined(total_ref)
+    for columns in row_tiles(2 * D, 512):
+        w2_out[0, :, columns] = exact_tn(hidden_ref[...], total[:, columns])
+    b2_out[...] = jnp.sum(total[...], axis=0, keepdims=True)
+
+
+def second_back(total, hidden):
+    rh = hidden.shape[1]
+    return pl.pallas_call(
+        second_kernel,
+        in_specs=[IN_VMEM] * 2,
+        out_specs=[IN_VMEM] * 2,
+        scratch_shapes=[pltpu.VMEM((SLOTS, 2 * D), F32)],
+        out_shape=[
+            jax.ShapeDtypeStruct((1, rh, 2 * D), F32),
+            jax.ShapeDtypeStruct((1, 2 * D), F32),
+        ],
+        compiler_params=params(),
+        cost_estimate=cost(3),
+        name="second_back",
+    )(total, hidden)
+
+
+def first_kernel(own_ref, other_ref, hidden_ref, table_ref, w1_ref, table_out, w1_out, b1_out):
+    hidden = hidden_ref[...]
+    grad_pre = (own_ref[...] + other_ref[...]) * (1.0 - hidden * hidden)
+    b1_out[...] = jnp.sum(grad_pre, axis=0, keepdims=True)
+    w1_out[...] = exact_tn(table_ref[...].astype(F32), grad_pre)
+    table_out[...] = exact_nt(grad_pre, w1_ref[...])[:PREFIX]
+
+
+def first_back(own, other, hidden, table, w1):
+    return pl.pallas_call(
+        first_kernel,
+        in_specs=[IN_VMEM] * 5,
+        out_specs=[IN_VMEM] * 3,
+        out_shape=[
+            jax.ShapeDtypeStruct((PREFIX, D), F32),
+            jax.ShapeDtypeStruct(w1.shape, F32),
+            jax.ShapeDtypeStruct((1, w1.shape[1]), F32),
+        ],
+        compiler_params=params(),
+        cost_estimate=cost(2),
+        name="first_back",
+    )(own, other, hidden, table, w1)
 
 
 def swap_sections(values):
@@ -1076,11 +1318,15 @@
 
 def sum_dp(values):
     count = lax.axis_size("dp")
-    step = 1
-    while step < count:
-        pairs = [(i, i ^ step) for i in range(count)]
-        values = values + lax.ppermute(values, "dp", pairs)
-        step *= 2
+    moved = lambda bits: lax.ppermute(values, "dp", [(i, i ^ bits) for i in range(count)])
+    step = count
+    while step > 1:
+        if step % 4 == 0:
+            step //= 4
+            values = (values + moved(step)) + (moved(2 * step) + moved(3 * step))
+        else:
+            step //= 2
+            values = values + moved(step)
     return values
 
 
@@ -1139,53 +1385,57 @@
     projected = project(spot, 1, handed, norm_pair[1], last[0])
     attended, *probs = attend(seq, projected, *prefix_last)
     middle, normed = middle_block(spot, 1, attended, handed, norm_pair[1], last[0])
-    final, grad_middle, grad_attended = turn_block(
-        spot, normed, middle, cotangent, norm_pair[1], *last
-    )
-    grads, dkp_last, dvp_last = attend_back(
+    final, sent, grad_middle, grad_attended = turn_block(
+        spot, normed, middle, cotangent, handed, norm_pair[1], *last
+    )
+    received = swap_sections(sent)
+    grads, prefix_grad_last = attend_back(
         seq, projected, attended, grad_attended, *prefix_last, *probs
     )
     grad_handed = unproject(spot, 1, grads, handed, grad_middle, norm_pair[1], last[0])
-    grad_middle, grad_attended = backward_block(
-        grad_handed, slope, middle_first, norm_pair[0], *first
-    )
-    grads, dkp_first, dvp_first = attend_back(
-        seq, projected_first, attended_first, grad_attended, *prefix_first, *probs_first
-    )
-    grad_tokens = unproject(spot, 0, grads, tokens, grad_middle, norm_pair[0], first[0])
-
-    def gathered_rows(first, last):
-        kept = jnp.where(is_first, first, last)
-        received = swap_sections(jnp.where(is_first, last, first))
-        return jnp.concatenate(
-            [jnp.where(is_first, kept, received), jnp.where(is_first, received, kept)], axis=0
-        )
-
-    activations = gathered_rows(handed, final)
-    input_grads = gathered_rows(grad_tokens, grad_handed)
-
-    pairs_joined = lambda rows: jnp.moveaxis(rows[:, :PREFIX], 0, 1).reshape(PREFIX, D)
-    grad_first = jnp.concatenate([pairs_joined(dkp_first), pairs_joined(dvp_first)], axis=1)
-    grad_last = jnp.concatenate([pairs_joined(dkp_last), pairs_joined(dvp_last)], axis=1)
-    kept = jnp.where(is_first, grad_first, grad_last)
-    received = swap_sections(jnp.where(is_first, grad_last, grad_first))
-    prefix_total = sum_dp(kept + received)
-
-    grad_hidden, grad_w2, grad_b2 = jax.vjp(reparam_out, hidden_units, second_weight, second_bias)[
-        1
-    ](prefix_total)
-    grad_hidden = grad_hidden + swap_sections(grad_hidden)
-    grad_table, grad_w1, grad_b1 = jax.vjp(reparam_hidden, table_values, first_weight, first_bias)[
-        1
-    ](grad_hidden)
+    received_grad = lax.ppermute(grad_handed, "section", [(0, 1)])
+    activations, grad_middle, grad_attended = backward_block(
+        spot, grad_handed, slope, middle_first, (handed, final, received), norm_pair[0], *first
+    )
+    grads, prefix_grad_first = attend_back(
+        seq,
+        projected_first,
+        attended_first,
+        grad_attended,
+        *prefix_first,
+        *probs_first,
+    )
+    input_grads, *pieces = unproject(
+        spot,
+        0,
+        grads,
+        tokens,
+        grad_middle,
+        norm_pair[0],
+        first[0],
+        (grad_handed, received_grad),
+    )
+    pieces = [lax.ppermute(piece, "section", [(1, 0)]) for piece in pieces]
+    input_grads = place_received(spot, input_grads, pieces)
+
+    kept = jnp.where(is_first, prefix_grad_first, prefix_grad_last)
+    sent = jnp.where(is_first, prefix_grad_last, prefix_grad_first)
+    total = sum_dp(kept + swap_sections(sent))
+    slots = lambda rows: jnp.pad(rows, ((0, SLOTS - PREFIX), (0, 0)))
+    hidden_slots, table_slots = slots(hidden_units), slots(prefix_table)
+    grad_hidden = hidden_back(total, reparam_w2)
+    grad_w2, grad_b2 = second_back(total, hidden_slots)
+    grad_table, grad_w1, grad_b1 = first_back(
+        grad_hidden, swap_sections(grad_hidden), hidden_slots, table_slots, reparam_w1
+    )
     return (
         activations[None],
         input_grads[None],
         grad_table,
         grad_w1,
-        grad_b1,
-        grad_w2[None],
-        grad_b2[None],
+        grad_b1[0],
+        grad_w2,
+        grad_b2,
     )
 
 

time: 563 us -> 552 us (0.980)
  starting transfers between devices: 5.24 us -> 36.7 us
  other arithmetic: 20.2 us -> 5.49 us
  Pallas kernels: 288 us -> 274 us
  matrix products: 12 us -> 2.41 us
  local copies, waits for them, and re-layouts: 15.8 us -> 9.39 us
    ppermute x4 -> x9, starting transfers between devices: 3.17 us -> 21 us  [the longest x1 10.8 us: per_device(): received_grad = lax.ppermute(grad_handed, 'section', [(0, 1)])]
    pallas_call x2, Pallas kernels: 61.3 us -> 46.2 us  [attend_back(): pl.pallas_call(attend_back_kernel, grid_spec=pltpu.PrefetchScalarGridSpec...]
    ppermute x6 -> x5, starting transfers between devices: 1.46 us -> 15.1 us  [swap_sections(): return lax.ppermute(values, 'section', [(0, 1), (1, 0)])]
    pallas_call x0 -> x4, Pallas kernels: none -> 12.8 us  [the longest x1 3.65 us: second_back(): pl.pallas_call(second_kernel, in_specs=[IN_VMEM] * 2, out_specs=[IN_VMEM]...]
    pallas_call x2, Pallas kernels: 47.6 us -> 35.7 us  [attend(): pl.pallas_call(attend_kernel, grid_spec=pltpu.PrefetchScalarGridSpec(num_...]
    select_n x5 -> x1, other arithmetic: 10.2 us -> 0.02 us  [per_device(): sent = jnp.where(is_first, prefix_grad_last, prefix_grad_first)]
    all_gather x2, waiting for transfers between devices: 188 us -> 196 us  [gather_weights(): lax.all_gather(rows, ('dp', 'section'), axis=0).reshape(SHARDS, 2, -1, D)]
    dot_general x3 -> x1, matrix products: 7.86 us -> 0.93 us  [reparam_out(): return jnp.dot(hidden_units, w_second, precision=highest_mode) + b_second]
  transfers between devices with their start and end apart: 12 -> 16, of which waited for: 6 -> 6; matrix products, arithmetic and copies ran while one was open for 6% -> 2% of each run, Pallas kernels for 24% -> 41%
where the time goes in v3:
time: 552 us; the launch traced here: 548 us
  Pallas kernels  274 us (50%)
  waiting for transfers between devices  205 us (37%)
  starting transfers between devices  36.7 us (7%)
  between operations  15 us (3%)
  local copies, waits for them, and re-layouts  9.39 us (2%)
    all_gather x2, waiting for transfers between devices, gather_weights(): lax.all_gather(rows, ('dp', 'section'), axis=0).reshape(SHARDS, 2, -1, D)  196 us
    pallas_call x1, Pallas kernels, turn_block(): pl.pallas_call(functools.partial(turn_kernel, (attention[1], up[1], down[...  48.7 us
    pallas_call x2, Pallas kernels, attend_back(): pl.pallas_call(attend_back_kernel, grid_spec=pltpu.PrefetchScalarGridSpec...  46.2 us
    pallas_call x2, Pallas kernels, attend(): pl.pallas_call(attend_kernel, grid_spec=pltpu.PrefetchScalarGridSpec(num_...  35.7 us
    pallas_call x2, Pallas kernels, unproject(): pl.pallas_call(functools.partial(unproject_kernel, place[1], which), in_s...  30.4 us
    pallas_call x1, Pallas kernels, backward_block(): pl.pallas_call(functools.partial(backward_kernel, (attention[1], up[1], d...  28.2 us
    pallas_call x1, Pallas kernels, forward_block(): pl.pallas_call(functools.partial(forward_kernel, (up[1], down[1])), grid=...  27.2 us
    pallas_call x2, Pallas kernels, project(): pl.pallas_call(functools.partial(qkv_kernel, place[1]), grid_spec=pltpu.P...  26.6 us
  transfers between devices with their start and end apart: 16, of which 6 were waited for; matrix products, arithmetic and copies ran while one was open for 2% of the time, Pallas kernels for 41%

profile of v3, /device:TPU:0, one launch (start us, length us, event | category | flops | bytes accessed | tf_op | source)
XLA Modules:
  0.0 548.1 jit_solution(14698879709022874120)
XLA Ops:
  23.8 188.2 %all-gather.6.cloned.1.call-done = bf16[16384,1024]{1,0:T(8,128)(2,1)} async-done(((bf16[512,1024]{1,0:T(8,128)(2,1)}), bf16[16384,1024]{1,0:T(8,128)(2,1)}) %all-gather.6.cloned.1.call-update) | async-done | bytes 33554448 | tf_op jit(solution)/shard_map/all_gather | solution.py:1291
  212.0 13.3 %norm_project.2.q_ref.k_ref.v_ref = bf16[24,1024,128]{2,1,0:T(8,128)(2,1)} custom-call(s32[2]{0:T(128)} %pad_add_fusion.spot_ref, bf16[2,1024,1024]{2,1,0:T(8,128)(2,1)} %hidden_ref.5, f32[8,1024]{1,0:T(8,128)} %slice_convert_fusion.1.norm_ref, bf16[16,2,512,1024]{3,2,1,0:T(8,128)(2,1)} %bitcast.71), custom_call_target="tpu_custom_call" | custom-call | flops 13799999488 | bytes 1048576 | tf_op jit(solution)/shard_map/norm_project/pallas_call | solution.py:192
  225.2 17.7 %attend.2 = (bf16[8,1024,128]{2,1,0:T(8,128)(2,1)}, bf16[8,1040,2048]{2,1,0:T(8,128)(2,1)}, f32[8,1024,128]{2,1,0:T(8,128)}) custom-call(s32[1]{0:T(128)} %dynamic_slice.3.seq_ref, bf16[24,1024,128]{2,1,0:T(8,128)(2,1)} %norm_project.2.q_ref.k_ref.v_ref, bf16[24,1024,128]{2,1,0:T(8,128)(2,1)} %norm_project.2.q_ref.k_ref.v_ref, ...), custom_call_target="tpu_custom_call" | custom-call | flops 34500001792 | bytes 1048576 | tf_op jit(solution)/shard_map/attend/pallas_call | solution.py:343
  243.0 9.0 %middle_block.2 = (f32[1024,1024]{1,0:T(8,128)}, bf16[1024,1024]{1,0:T(8,128)(2,1)}) custom-call(s32[2]{0:T(128)} %pad_add_fusion.spot_ref, bf16[8,1024,128]{2,1,0:T(8,128)(2,1)} %get-tuple-element.38.attended_ref.out_ref, bf16[2,1024,1024]{2,1,0:T(8,128)(2,1)} %hidden_ref.5, f32[8,1024]{1,0:T(8,128)} %slice_convert_fusion.1.norm_ref, ...), custom_call_target="tpu_custom_call" | custom-call | flops 5750000128 | bytes 1048576 | tf_op jit(solution)/shard_map/middle_block/pallas_call | solution.py:523
  252.0 27.2 %forward_block.1 = (bf16[1024,4096]{1,0:T(8,128)(2,1)}, bf16[1,1024,1024]{2,1,0:T(8,128)(2,1)}) custom-call(bf16[1024,1024]{1,0:T(8,128)(2,1)} %get-tuple-element.39.normed_ref, f32[1024,1024]{1,0:T(8,128)} %get-tuple-element.40.middle_ref, bf16[16,2,512,1024]{3,2,1,0:T(8,128)(2,1)} %bitcast.73, bf16[16,2,512,1024]{3,2,1,0:T(8,128)(2,1)} %bitcast.74), custom_call_target="tpu_custom_call" | custom-call | flops 28750000128 | bytes 1048576 | tf_op jit(solution)/shard_map/forward_block/pallas_call | solution.py:626
  279.2 13.3 %norm_project.3.q_ref.k_ref.v_ref = bf16[24,1024,128]{2,1,0:T(8,128)(2,1)} custom-call(s32[2]{0:T(128)} %pad_add_fusion.spot_ref, bf16[1,1024,1024]{2,1,0:T(8,128)(2,1)} %get-tuple-element.42.hidden_ref.first_ref, f32[8,1024]{1,0:T(8,128)} %slice_convert_fusion.norm_ref, bf16[16,2,512,1024]{3,2,1,0:T(8,128)(2,1)} %bitcast.75), custom_call_target="tpu_custom_call" | custom-call | flops 13799999488 | bytes 1048576 | tf_op jit(solution)/shard_map/norm_project/pallas_call | solution.py:192
  292.6 17.9 %attend.3 = (bf16[8,1024,128]{2,1,0:T(8,128)(2,1)}, bf16[8,1040,2048]{2,1,0:T(8,128)(2,1)}, f32[8,1024,128]{2,1,0:T(8,128)}) custom-call(s32[1]{0:T(128)} %dynamic_slice.3.seq_ref, bf16[24,1024,128]{2,1,0:T(8,128)(2,1)} %norm_project.3.q_ref.k_ref.v_ref, bf16[24,1024,128]{2,1,0:T(8,128)(2,1)} %norm_project.3.q_ref.k_ref.v_ref, ...), custom_call_target="tpu_custom_call" | custom-call | flops 34500001792 | bytes 1048576 | tf_op jit(solution)/shard_map/attend/pallas_call | solution.py:343
  310.5 9.2 %middle_block.3 = (f32[1024,1024]{1,0:T(8,128)}, bf16[1024,1024]{1,0:T(8,128)(2,1)}) custom-call(s32[2]{0:T(128)} %pad_add_fusion.spot_ref, bf16[8,1024,128]{2,1,0:T(8,128)(2,1)} %get-tuple-element.43.attended_ref.out_ref, bf16[1,1024,1024]{2,1,0:T(8,128)(2,1)} %get-tuple-element.42.hidden_ref.first_ref, f32[8,1024]{1,0:T(8,128)} %slice_convert_fusion.norm_ref, ...), custom_call_target="tpu_custom_call" | custom-call | flops 5750000128 | bytes 1048576 | tf_op jit(solution)/shard_map/middle_block/pallas_call | solution.py:523
  319.7 8.2 %all-gather.4.cloned.1.call-done = bf16[32,256,1024]{2,1,0:T(8,128)(2,1)} async-done(((bf16[1,256,1024]{2,1,0:T(8,128)(2,1)}), bf16[32,256,1024]{2,1,0:T(8,128)(2,1)}) %all-gather.4.cloned.1.call-update) | async-done | bytes 16777232 | tf_op jit(solution)/shard_map/all_gather | solution.py:1291
  327.9 48.7 %turn_block.1 = (bf16[1,1024,1024]{2,1,0:T(8,128)(2,1)}, bf16[1,1024,1024]{2,1,0:T(8,128)(2,1)}, bf16[1024,1024]{1,0:T(8,128)(2,1)}, bf16[8,1024,128]{2,1,0:T(8,128)(2,1)}) custom-call(s32[2]{0:T(128)} %pad_add_fusion.spot_ref, f32[8,1024]{1,0:T(8,128)} %slice_convert_fusion.norm_ref, bf16[1024,1024]{1,0:T(8,128)(2,1)} %get-tuple-element.44.normed_ref, ...), custom_call_target="tpu_custom_call" | custom-call | flops 48299999232 | bytes 1048576 | tf_op jit(solution)/shard_map/turn_block/pallas_call | solution.py:784
  376.6 5.6 %collective-permute-start.2 = (bf16[1,1024,1024]{2,1,0:T(8,128)(2,1)}, bf16[1,1024,1024]{2,1,0:T(8,128)(2,1)}, u32[]{:S(2)}, u32[]{:S(2)}) collective-permute-start(bf16[1,1024,1024]{2,1,0:T(8,128)(2,1)} %get-tuple-element.52), channel_id=1, source_target_pairs={{0,1},{1,0},{2,3},{3,2},{4,5},{5,4},{6,7},{7,6},{8,9},{9,8},{10,11... | collective-permute-start | bytes 6291464 | tf_op jit(solution)/shard_map/ppermute | solution.py:1267
  382.2 23.0 %attend_back.2 = (bf16[3,8,1024,128]{3,2,1,0:T(8,128)(2,1)}, f32[8,24,128]{2,1,0:T(8,128)}) custom-call(s32[1]{0:T(128)} %dynamic_slice.3.seq_ref, bf16[24,1024,128]{2,1,0:T(8,128)(2,1)} %norm_project.3.q_ref.k_ref.v_ref, bf16[24,1024,128]{2,1,0:T(8,128)(2,1)} %norm_project.3.q_ref.k_ref.v_ref, bf16[24,1024,128]{2,1,0:T(8,128)(2,1)} %norm_project.3.q_ref.k_ref.v_ref, ...), custom_call_target="tpu_custom_call" | custom-call | flops 34500001792 | bytes 1048576 | tf_op jit(solution)/shard_map/attend_back/pallas_call | solution.py:453
  405.2 15.2 %unproject.2.upstream_ref.refs_0_ = bf16[1,1024,1024]{2,1,0:T(8,128)(2,1)} custom-call(s32[2]{0:T(128)} %pad_add_fusion.spot_ref, f32[8,1024]{1,0:T(8,128)} %slice_convert_fusion.norm_ref, bf16[3,8,1024,128]{3,2,1,0:T(8,128)(2,1)} %get-tuple-element.49.grads_ref, bf16[1,1024,1024]{2,1,0:T(8,128)(2,1)} %get-tuple-element.42.hidden_ref.first_ref, ...), custom_call_target="tpu_custom_call" | custom-call | flops 12650000384 | bytes 1048576 | tf_op jit(solution)/shard_map/unproject/pallas_call | solution.py:1100
  420.4 10.8 %collective-permute-start.3 = (bf16[1,1024,1024]{2,1,0:T(8,128)(2,1)}, bf16[1,1024,1024]{2,1,0:T(8,128)(2,1)}, u32[]{:S(2)}, u32[]{:S(2)}) collective-permute-start(bf16[1,1024,1024]{2,1,0:T(8,128)(2,1)} %unproject.2.upstream_ref.refs_0_), channel_id=1, source_target_pairs={{0,1},{2,3},{4,5},{6,7},{8,9},{10,11},{12,13},{14,15},{16,17},{18,... | collective-permute-start | bytes 6291464 | tf_op jit(solution)/shard_map/ppermute | solution.py:1396
  431.2 28.2 %backward_block.1 = (bf16[2,1024,1024]{2,1,0:T(8,128)(2,1)}, bf16[1024,1024]{1,0:T(8,128)(2,1)}, bf16[8,1024,128]{2,1,0:T(8,128)(2,1)}) custom-call(s32[2]{0:T(128)} %pad_add_fusion.spot_ref, f32[8,1024]{1,0:T(8,128)} %slice_convert_fusion.1.norm_ref, bf16[1024,4096]{1,0:T(8,128)(2,1)} %get-tuple-element.41.slope_ref, ...), custom_call_target="tpu_custom_call" | custom-call | flops 28750000128 | bytes 1048576 | tf_op jit(solution)/shard_map/backward_block/pallas_call | solution.py:931
  459.5 23.1 %attend_back.3 = (bf16[3,8,1024,128]{3,2,1,0:T(8,128)(2,1)}, f32[8,24,128]{2,1,0:T(8,128)}) custom-call(s32[1]{0:T(128)} %dynamic_slice.3.seq_ref, bf16[24,1024,128]{2,1,0:T(8,128)(2,1)} %norm_project.2.q_ref.k_ref.v_ref, bf16[24,1024,128]{2,1,0:T(8,128)(2,1)} %norm_project.2.q_ref.k_ref.v_ref, bf16[24,1024,128]{2,1,0:T(8,128)(2,1)} %norm_project.2.q_ref.k_ref.v_ref, ...), custom_call_target="tpu_custom_call" | custom-call | flops 34500001792 | bytes 1048576 | tf_op jit(solution)/shard_map/attend_back/pallas_call | solution.py:453
  482.7 6.4 %collective-permute-start.6 = (f32[8,24,128]{2,1,0:T(8,128)S(1)}, f32[8,24,128]{2,1,0:T(8,128)S(1)}, u32[]{:S(2)}, u32[]{:S(2)}) collective-permute-start(f32[8,24,128]{2,1,0:T(8,128)S(1)} %broadcast_select_fusion.5), channel_id=1, source_target_pairs={{0,1},{1,0},{2,3},{3,2},{4,5},{5,4},{6,7},{7,6},{8,9},{9,8},{10,11... | collective-permute-start | bytes 294920 | tf_op jit(solution)/shard_map/ppermute | solution.py:1267
  491.1 3.4 collective-permute-start.7
  494.5 4.7 collective-permute-done.8
  504.4 15.2 %unproject.3 = (bf16[2,1024,1024]{2,1,0:T(8,128)(2,1)}, bf16[1,512,1024]{2,1,0:T(8,128)(2,1)}, bf16[1,512,1024]{2,1,0:T(8,128)(2,1)}) custom-call(s32[2]{0:T(128)} %pad_add_fusion.spot_ref, f32[8,1024]{1,0:T(8,128)} %slice_convert_fusion.1.norm_ref, bf16[3,8,1024,128]{3,2,1,0:T(8,128)(2,1)} %get-tuple-element.57.grads_ref, ...), custom_call_target="tpu_custom_call" | custom-call | flops 12650000384 | bytes 1048576 | tf_op jit(solution)/shard_map/unproject/pallas_call | solution.py:1100
  524.2 3.0 hidden_back.1.own_ref
  529.3 3.7 second_back.1
  533.6 3.1 first_back.1
  537.7 3.1 place_received.1
  (96 shorter events, 31.7 us)
Async XLA Ops:
  7.2 204.8 %all-gather.6.cloned.1.call-start = ((), (), s32[]{:S(2)}) async-start(), calls=%async_computation.1 | async-start | bytes 34603008 | tf_op jit(solution)/shard_map/all_gather | solution.py:1291
  10.7 2.4 collective-permute-start.1
  13.3 2.5 copy-start.8
  14.4 3.0 copy-start
  14.4 313.5 %all-gather.4.cloned.1.call-start = ((), (), s32[]{:S(2)}) async-start(), calls=%async_computation | async-start | bytes 17301504 | tf_op jit(solution)/shard_map/all_gather | solution.py:1291
  15.8 2.6 copy-start.11
  15.8 2.6 copy-start.12
  15.8 3.1 copy-start.15
  18.4 1.7 collective-permute-start
  376.6 54.7 %collective-permute-start.2 = (bf16[1,1024,1024]{2,1,0:T(8,128)(2,1)}, bf16[1,1024,1024]{2,1,0:T(8,128)(2,1)}, u32[]{:S(2)}, u32[]{:S(2)}) collective-permute-start(bf16[1,1024,1024]{2,1,0:T(8,128)(2,1)} %get-tuple-element.52), channel_id=1, source_target_pairs={{0,1},{1,0},{2,3},{3,2},{4,5},{5,4},{6,7},{7,6},{8,9},{9,8},{10,11... | collective-permute-start | bytes 6291464 | tf_op jit(solution)/shard_map/ppermute | solution.py:1267
  420.4 84.0 %collective-permute-start.3 = (bf16[1,1024,1024]{2,1,0:T(8,128)(2,1)}, bf16[1,1024,1024]{2,1,0:T(8,128)(2,1)}, u32[]{:S(2)}, u32[]{:S(2)}) collective-permute-start(bf16[1,1024,1024]{2,1,0:T(8,128)(2,1)} %unproject.2.upstream_ref.refs_0_), channel_id=1, source_target_pairs={{0,1},{2,3},{4,5},{6,7},{8,9},{10,11},{12,13},{14,15},{16,17},{18,... | collective-permute-start | bytes 6291464 | tf_op jit(solution)/shard_map/ppermute | solution.py:1396
  459.5 23.2 %copy-start.4 = (f32[8,24,128]{2,1,0:T(8,128)S(1)}, f32[8,24,128]{2,1,0:T(8,128)}, u32[]{:S(2)}) copy-start(f32[8,24,128]{2,1,0:T(8,128)} %get-tuple-element.63) | copy-start | bytes 294916
  482.7 7.4 %collective-permute-start.6 = (f32[8,24,128]{2,1,0:T(8,128)S(1)}, f32[8,24,128]{2,1,0:T(8,128)S(1)}, u32[]{:S(2)}, u32[]{:S(2)}) collective-permute-start(f32[8,24,128]{2,1,0:T(8,128)S(1)} %broadcast_select_fusion.5), channel_id=1, source_target_pairs={{0,1},{1,0},{2,3},{3,2},{4,5},{5,4},{6,7},{7,6},{8,9},{9,8},{10,11... | collective-permute-start | bytes 294920 | tf_op jit(solution)/shard_map/ppermute | solution.py:1267
  491.0 8.3 %collective-permute-start.8 = (f32[8,24,128]{2,1,0:T(8,128)S(1)}, f32[8,24,128]{2,1,0:T(8,128)S(1)}, u32[]{:S(2)}, u32[]{:S(2)}) collective-permute-start(f32[8,24,128]{2,1,0:T(8,128)S(1)} %select_add_fusion), channel_id=1, source_target_pairs={{0,16},{2,18},{4,20},{6,22},{8,24},{10,26},{12,28},{14,30},{16,0},... | collective-permute-start | bytes 294920 | tf_op jit(solution)/shard_map/ppermute | solution.py:1321
  491.0 8.2 %collective-permute-start.9 = (f32[8,24,128]{2,1,0:T(8,128)S(1)}, f32[8,24,128]{2,1,0:T(8,128)S(1)}, u32[]{:S(2)}, u32[]{:S(2)}) collective-permute-start(f32[8,24,128]{2,1,0:T(8,128)S(1)} %select_add_fusion), channel_id=1, source_target_pairs={{0,24},{2,26},{4,28},{6,30},{8,16},{10,18},{12,20},{14,22},{16,8},... | collective-permute-start | bytes 294920 | tf_op jit(solution)/shard_map/ppermute | solution.py:1321
  491.1 9.2 %collective-permute-start.7 = (f32[8,24,128]{2,1,0:T(8,128)S(1)}, f32[8,24,128]{2,1,0:T(8,128)S(1)}, u32[]{:S(2)}, u32[]{:S(2)}) collective-permute-start(f32[8,24,128]{2,1,0:T(8,128)S(1)} %select_add_fusion), channel_id=1, source_target_pairs={{0,8},{2,10},{4,12},{6,14},{8,0},{10,2},{12,4},{14,6},{16,24},{18,... | collective-permute-start | bytes 294920 | tf_op jit(solution)/shard_map/ppermute | solution.py:1321
  500.3 23.2 %collective-permute-start.11 = (f32[8,24,128]{2,1,0:T(8,128)S(1)}, f32[8,24,128]{2,1,0:T(8,128)S(1)}, u32[]{:S(2)}, u32[]{:S(2)}) collective-permute-start(f32[8,24,128]{2,1,0:T(8,128)S(1)} %add_add_fusion.1), channel_id=1, source_target_pairs={{0,4},{2,6},{4,0},{6,2},{8,12},{10,14},{12,8},{14,10},{16,20},{18,... | collective-permute-start | bytes 294920 | tf_op jit(solution)/shard_map/ppermute | solution.py:1321
  502.9 20.6 %collective-permute-start.12 = (f32[8,24,128]{2,1,0:T(8,128)S(1)}, f32[8,24,128]{2,1,0:T(8,128)S(1)}, u32[]{:S(2)}, u32[]{:S(2)}) collective-permute-start(f32[8,24,128]{2,1,0:T(8,128)S(1)} %add_add_fusion.1), channel_id=1, source_target_pairs={{0,6},{2,4},{4,2},{6,0},{8,14},{10,12},{12,10},{14,8},{16,22},{18,... | collective-permute-start | bytes 294920 | tf_op jit(solution)/shard_map/ppermute | solution.py:1321
  502.9 20.6 %collective-permute-start.10 = (f32[8,24,128]{2,1,0:T(8,128)S(1)}, f32[8,24,128]{2,1,0:T(8,128)S(1)}, u32[]{:S(2)}, u32[]{:S(2)}) collective-permute-start(f32[8,24,128]{2,1,0:T(8,128)S(1)} %add_add_fusion.1), channel_id=1, source_target_pairs={{0,2},{2,0},{4,6},{6,4},{8,10},{10,8},{12,14},{14,12},{16,18},{18,... | collective-permute-start | bytes 294920 | tf_op jit(solution)/shard_map/ppermute | solution.py:1321
  504.4 17.8 %copy-start.9 = (bf16[10,1024]{1,0:T(8,128)(2,1)S(1)}, bf16[10,1024]{1,0:T(8,128)(2,1)}, u32[]{:S(2)}) copy-start(bf16[10,1024]{1,0:T(8,128)(2,1)} %param.23) | copy-start | bytes 61444
  504.4 18.4 %copy-start.6 = (f32[10,512]{1,0:T(8,128)S(1)}, f32[10,512]{1,0:T(8,128)}, u32[]{:S(2)}) copy-start(f32[10,512]{1,0:T(8,128)} %copy-done.5) | copy-start | bytes 61444
  519.7 17.0 %collective-permute-start.4 = (bf16[1,512,1024]{2,1,0:T(8,128)(2,1)}, bf16[1,512,1024]{2,1,0:T(8,128)(2,1)S(1)}, u32[]{:S(2)}, u32[]{:S(2)}) collective-permute-start(bf16[1,512,1024]{2,1,0:T(8,128)(2,1)} %get-tuple-element.60), channel_id=1, source_target_pairs={{1,0},{3,2},{5,4},{7,6},{9,8},{11,10},{13,12},{15,14},{17,16},{19,... | collective-permute-start | bytes 3145736 | tf_op jit(solution)/shard_map/ppermute | solution.py:1418
  521.0 15.7 %collective-permute-start.5 = (bf16[1,512,1024]{2,1,0:T(8,128)(2,1)}, bf16[1,512,1024]{2,1,0:T(8,128)(2,1)}, u32[]{:S(2)}, u32[]{:S(2)}) collective-permute-start(bf16[1,512,1024]{2,1,0:T(8,128)(2,1)} %get-tuple-element.61), channel_id=1, source_target_pairs={{1,0},{3,2},{5,4},{7,6},{9,8},{11,10},{13,12},{15,14},{17,16},{19,... | collective-permute-start | bytes 3145736 | tf_op jit(solution)/shard_map/ppermute | solution.py:1418
  527.1 5.8 %collective-permute-start.13 = (f32[16,512]{1,0:T(8,128)}, f32[16,512]{1,0:T(8,128)S(1)}, u32[]{:S(2)}, u32[]{:S(2)}) collective-permute-start(f32[16,512]{1,0:T(8,128)} %hidden_back.1.own_ref), channel_id=1, source_target_pairs={{0,1},{1,0},{2,3},{3,2},{4,5},{5,4},{6,7},{7,6},{8,9},{9,8},{10,11... | collective-permute-start | bytes 98312 | tf_op jit(solution)/shard_map/ppermute | solution.py:1267
  (8 other events, 12.8 us)
Sparse Core Ops, SparseCore 0:
  14.5 197.3 all-gather.5
  214.8 113.0 all-gather.3

commit v4 on v3

--- a/solution.py
+++ b/solution.py
@@ -128,6 +128,13 @@
 
 
 ANY = pl.BlockSpec(memory_space=pl.ANY)
+TILE = 512
+SCALARS = pl.BlockSpec(memory_space=pltpu.SMEM)
+IN_VMEM = pl.BlockSpec(memory_space=pltpu.VMEM)
+
+
+def whole_scratch(dtype):
+    return pltpu.VMEM((D, D), dtype)
 
 
 def once(shape, index):
@@ -162,19 +169,25 @@
     step = pl.program_id(0)
     loads = [load_qkv(array, row, part, weights, semaphores) for part in range(3)]
     length = hidden_ref.shape[1]
-    tiles = row_tiles(length, 512)
+    tiles = row_tiles(length, 256)
 
     @pl.when(step == 0)
     def _():
         loads[0].start()
         gain, offset = norm_ref[0:1], norm_ref[2:3]
-        for rows in chunks(slice(0, length)):
-            values = hidden_ref[0, rows].astype(F32)
-            normed[rows] = layer_norm(values, gain, offset).astype(BF16)
+
+        def norm(tile):
+            for rows in chunks(tile):
+                values = hidden_ref[0, rows].astype(F32)
+                normed[rows] = layer_norm(values, gain, offset).astype(BF16)
+
+        norm(tiles[0])
         loads[0].wait()
         loads[1].start()
         loads[2].start()
-        for rows in tiles:
+        for index, rows in enumerate(tiles):
+            if index + 1 < len(tiles):
+                norm(tiles[index + 1])
             queries = dot_nn(normed[rows], matrix(weights, 0))
             put_pairs(out_ref, rows, (queries * HEAD_DIM**-0.5).astype(BF16))
 
@@ -500,40 +513,81 @@
     )
 
 
-def middle_kernel(row, spot_ref, attended_ref, hidden_ref, norm_ref, array, middle_ref, normed_ref, weights, semaphores):
-    step = pl.program_id(0)
-    load = load_out(array, row, weights.at[0], semaphores.at[0])
-
-    @pl.when(step == 0)
-    def _():
-        load.start()
-        load.wait()
-
-    middle_ref[...] = dot_nn(get_pairs(attended_ref, slice(None)), matrix(weights, 0))
+def middle_kernel(
+    row,
+    which,
+    spot_ref,
+    norm_ref,
+    attended_ref,
+    hidden_ref,
+    array,
+    middle_ref,
+    normed_ref,
+    attended,
+    hidden,
+    middle,
+    normed,
+    weights,
+    semaphores,
+    load_semaphores,
+    store_semaphores,
+):
+    copy = pltpu.make_async_copy
+    tiles = row_tiles(D, 256)
+    get_weights = load_out(array, row, weights, semaphores.at[0])
+    get_attended = [
+        copy(attended_ref.at[:, rows], attended.at[:, rows], load_semaphores.at[0, index])
+        for index, rows in enumerate(tiles)
+    ]
+    get_hidden = [
+        copy(hidden_ref.at[spot_ref[which], rows], hidden.at[rows], load_semaphores.at[1, index])
+        for index, rows in enumerate(tiles)
+    ]
+    get_weights.start()
+    for loads in zip(get_attended, get_hidden):
+        for load in loads:
+            load.start()
     gain, offset = norm_ref[1:2], norm_ref[3:4]
-    for rows in chunks(slice(0, middle_ref.shape[0])):
-        middle = hidden_ref[0, rows].astype(F32) + middle_ref[rows]
-        middle_ref[rows] = middle
-        normed_ref[rows] = layer_norm(middle, gain, offset).astype(BF16)
+    stores = []
+
+    def finish(index, rows):
+        get_hidden[index].wait()
+        for part in chunks(rows):
+            values = hidden[part].astype(F32) + middle[part]
+            middle[part] = values
+            normed[part] = layer_norm(values, gain, offset).astype(BF16)
+        for source, target, kind in ((middle, middle_ref, 0), (normed, normed_ref, 1)):
+            stores.append(copy(source.at[rows], target.at[rows], store_semaphores.at[kind, index]))
+            stores[-1].start()
+
+    get_weights.wait()
+    for index, rows in enumerate(tiles):
+        get_attended[index].wait()
+        middle[rows] = dot_nn(get_pairs(attended, rows), matrix(weights))
+        if index:
+            finish(index - 1, tiles[index - 1])
+    finish(len(tiles) - 1, tiles[-1])
+    for store in stores:
+        store.wait()
 
 
 def middle_block(spot, which, attended, hidden, norms, place):
     length = attended.shape[1]
-    tile = pl.BlockSpec((256, D), lambda m, s: (m, 0))
+    count = D // 256
     return pl.pallas_call(
-        functools.partial(middle_kernel, place[1]),
-        grid_spec=pltpu.PrefetchScalarGridSpec(
-            num_scalar_prefetch=1,
-            grid=(length // 256,),
-            in_specs=[
-                pl.BlockSpec((PAIRS, 256, PAIR_DIM), lambda m, s: (0, m, 0)),
-                pl.BlockSpec((1, 256, D), lambda m, s: (s[which], m, 0)),
-                once((8, D), lambda m, s: (0, 0)),
-                ANY,
-            ],
-            out_specs=[tile, tile],
-            scratch_shapes=[across_scratch(1), pltpu.SemaphoreType.DMA((1,))],
-        ),
+        functools.partial(middle_kernel, place[1], which),
+        in_specs=[SCALARS, IN_VMEM] + [ANY] * 3,
+        out_specs=[ANY] * 2,
+        scratch_shapes=[
+            pltpu.VMEM((PAIRS, D, PAIR_DIM), BF16),
+            whole_scratch(BF16),
+            whole_scratch(F32),
+            whole_scratch(BF16),
+            pltpu.VMEM((SHARDS, SHARD_ROWS, D), BF16),
+            pltpu.SemaphoreType.DMA((1,)),
+            pltpu.SemaphoreType.DMA((2, count)),
+            pltpu.SemaphoreType.DMA((2, count)),
+        ],
         out_shape=[
             jax.ShapeDtypeStruct((length, D), F32),
             jax.ShapeDtypeStruct((length, D), BF16),
@@ -541,7 +595,7 @@
         compiler_params=params(),
         cost_estimate=cost(5),
         name="middle_block",
-    )(spot, attended, hidden, norms, place[0])
+    )(spot, norms, attended, hidden, place[0])
 
 
 def feed_forward_loads(up, down, rows, up_weights, down_weights, semaphores):
@@ -768,15 +822,6 @@
         put_hidden.start()
 
     put_sent.wait()
-
-
-TILE = 512
-SCALARS = pl.BlockSpec(memory_space=pltpu.SMEM)
-IN_VMEM = pl.BlockSpec(memory_space=pltpu.VMEM)
-
-
-def whole_scratch(dtype):
-    return pltpu.VMEM((D, D), dtype)
 
 
 def turn_block(spot, normed, middle, upstream, hidden, norms, attention, up, down):
@@ -1014,33 +1059,22 @@
 
     get_weights = [load_qkv(array, row, part, weights, semaphores) for part in range(3)]
     get_grads = [
-        [
-            copy(
-                grads_ref.at[part, :, rows], grads.at[part, :, rows], load_semaphores.at[index, part]
-            )
-            for part in range(3)
-        ]
-        for index, rows in enumerate(tiles)
+        copy(grads_ref.at[part], grads.at[part], load_semaphores.at[0, part]) for part in range(3)
     ]
-    get_rest = [
-        [
-            copy(hidden_ref.at[spot_ref[which], rows], hidden.at[rows], load_semaphores.at[index, 3]),
-            copy(grad_middle_ref.at[rows], grad_middle.at[rows], load_semaphores.at[index, 4]),
-        ]
-        for index, rows in enumerate(tiles)
-    ]
-    for part in range(3):
+    get_hidden = copy(hidden_ref.at[spot_ref[which]], hidden, load_semaphores.at[1, 0])
+    get_grad_middle = copy(grad_middle_ref, grad_middle, load_semaphores.at[1, 1])
+
+    def start_part(part):
         get_weights[part].start()
-        get_grads[0][part].start()
+        get_grads[part].start()
+
+    start_part(0)
     stores = []
     gain = norm_ref[0:1]
 
     def finish(index, rows):
-        for load in get_rest[index]:
-            load.wait()
         for part in chunks(rows):
-            here = shifted(part, -rows.start)
-            back = norm_back(hidden[part].astype(F32), gain, total[index % 2, here])
+            back = norm_back(hidden[part].astype(F32), gain, total[part])
             out[part] = (grad_middle[part].astype(F32) + back).astype(BF16)
         if last:
             piece, start = divmod(rows.start, D // 2)
@@ -1055,36 +1089,37 @@
         else:
             stores[-1].start()
 
-    for index, rows in enumerate(tiles):
-        if last and index == 1:
+    for part in range(3):
+        get_weights[part].wait()
+        get_grads[part].wait()
+        if part < 2:
+            start_part(part + 1)
+        if part == 1:
+            get_hidden.start()
+            get_grad_middle.start()
+        if part == 2:
+            get_hidden.wait()
+            get_grad_middle.wait()
+        if part == 2 and last:
 
             @pl.when(spot_ref[0] != 0)
             def _():
                 for other in get_others:
                     other.start()
 
-        if last and index == 3:
-
-            @pl.when(spot_ref[0] != 0)
-            def _():
-                for other in get_others:
-                    other.wait()
-                put_others.start()
-
-        product = None
-        for part in range(3):
-            if index == 0:
-                get_weights[part].wait()
-            get_grads[index][part].wait()
-            if part == 0:
-                following = get_grads[index + 1] if index + 1 < len(tiles) else []
-                for load in following + get_rest[index]:
-                    load.start()
+        for index, rows in enumerate(tiles):
             term = dot_nt(get_pairs(grads, rows, part), matrix(weights, part))
-            product = term if product is None else product + term
-        total[index % 2] = product
-        if index:
-            finish(index - 1, tiles[index - 1])
+            total[rows] = term if part == 0 else total[rows] + term
+            if part == 2 and index:
+                finish(index - 1, tiles[index - 1])
+            if part == 2 and last and index == len(tiles) - 1:
+
+                @pl.when(spot_ref[0] != 0)
+                def _():
+                    for other in get_others:
+                        other.wait()
+                    put_others.start()
+
     finish(len(tiles) - 1, tiles[-1])
     for store in stores:
         store.wait()
@@ -1106,10 +1141,10 @@
             whole_scratch(BF16),
             whole_scratch(BF16),
             whole_scratch(BF16),
-            pltpu.VMEM((2, UNPROJECT, D), F32),
+            whole_scratch(F32),
             across_scratch(3),
             pltpu.SemaphoreType.DMA((3,)),
-            pltpu.SemaphoreType.DMA((count, 5)),
+            pltpu.SemaphoreType.DMA((2, 3)),
             pltpu.SemaphoreType.DMA((count,)),
         ]
         + ([pltpu.VMEM((2, D, D), BF16), pltpu.SemaphoreType.DMA((3,))] if others else []),
@@ -1118,48 +1153,6 @@
         cost_estimate=cost(11),
         name="unproject",
     )(spot, norms, grads, hidden, grad_middle, place[0], *others)
-
-
-def place_kernel(spot_ref, outputs_in, top_ref, bottom_ref, outputs_ref, buffer, semaphores):
-    del outputs_in
-    half = D // 2
-    tiles = row_tiles(D, 256)
-    loads = [
-        pltpu.make_async_copy(
-            (bottom_ref if rows.start >= half else top_ref).at[0, pl.ds(rows.start % half, 256)],
-            buffer.at[rows],
-            semaphores.at[0, index],
-        )
-        for index, rows in enumerate(tiles)
-    ]
-    stores = [
-        pltpu.make_async_copy(buffer.at[rows], outputs_ref.at[1, rows], semaphores.at[1, index])
-        for index, rows in enumerate(tiles)
-    ]
-
-    @pl.when(spot_ref[0] == 0)
-    def _():
-        for load in loads:
-            load.start()
-        for load, store in zip(loads, stores):
-            load.wait()
-            store.start()
-        for store in stores:
-            store.wait()
-
-
-def place_received(spot, outputs, pieces):
-    return pl.pallas_call(
-        place_kernel,
-        in_specs=[SCALARS, ANY, ANY, ANY],
-        out_specs=ANY,
-        scratch_shapes=[whole_scratch(BF16), pltpu.SemaphoreType.DMA((2, 4))],
-        out_shape=jax.ShapeDtypeStruct(outputs.shape, outputs.dtype),
-        input_output_aliases={1: 0},
-        compiler_params=params(),
-        cost_estimate=cost(2),
-        name="place_received",
-    )(spot, outputs, *pieces)
 
 
 def three_terms(values):
@@ -1214,11 +1207,18 @@
     )(total, w2)
 
 
-def second_kernel(total_ref, hidden_ref, w2_out, b2_out, total):
+def slots(ref, scratch):
+    scratch[...] = jnp.zeros_like(scratch)
+    scratch[:PREFIX] = ref[...].astype(F32)
+    return scratch[...]
+
+
+def second_kernel(total_ref, hidden_ref, w2_out, b2_out, total, hidden):
     total[...] = jnp.zeros_like(total)
     total[:PREFIX] = joined(total_ref)
+    units = slots(hidden_ref, hidden)
     for columns in row_tiles(2 * D, 512):
-        w2_out[0, :, columns] = exact_tn(hidden_ref[...], total[:, columns])
+        w2_out[0, :, columns] = exact_tn(units, total[:, columns])
     b2_out[...] = jnp.sum(total[...], axis=0, keepdims=True)
 
 
@@ -1228,7 +1228,7 @@
         second_kernel,
         in_specs=[IN_VMEM] * 2,
         out_specs=[IN_VMEM] * 2,
-        scratch_shapes=[pltpu.VMEM((SLOTS, 2 * D), F32)],
+        scratch_shapes=[pltpu.VMEM((SLOTS, 2 * D), F32), pltpu.VMEM((SLOTS, rh), F32)],
         out_shape=[
             jax.ShapeDtypeStruct((1, rh, 2 * D), F32),
             jax.ShapeDtypeStruct((1, 2 * D), F32),
@@ -1239,28 +1239,84 @@
     )(total, hidden)
 
 
-def first_kernel(own_ref, other_ref, hidden_ref, table_ref, w1_ref, table_out, w1_out, b1_out):
-    hidden = hidden_ref[...]
-    grad_pre = (own_ref[...] + other_ref[...]) * (1.0 - hidden * hidden)
+def last_kernel(
+    spot_ref,
+    own_ref,
+    other_ref,
+    hidden_ref,
+    table_ref,
+    w1_ref,
+    outputs_in,
+    top_ref,
+    bottom_ref,
+    table_out,
+    w1_out,
+    b1_out,
+    outputs_ref,
+    hidden,
+    table,
+    buffer,
+    semaphores,
+):
+    del outputs_in
+    half = D // 2
+    pieces = [(top_ref, slice(0, half)), (bottom_ref, slice(half, D))]
+    loads = [
+        pltpu.make_async_copy(piece.at[0], buffer.at[rows], semaphores.at[0, index])
+        for index, (piece, rows) in enumerate(pieces)
+    ]
+    stores = [
+        pltpu.make_async_copy(buffer.at[rows], outputs_ref.at[1, rows], semaphores.at[1, index])
+        for index, (_, rows) in enumerate(pieces)
+    ]
+
+    @pl.when(spot_ref[0] == 0)
+    def _():
+        for load in loads:
+            load.start()
+
+    units = slots(hidden_ref, hidden)
+    grad_pre = (own_ref[...] + other_ref[...]) * (1.0 - units * units)
     b1_out[...] = jnp.sum(grad_pre, axis=0, keepdims=True)
-    w1_out[...] = exact_tn(table_ref[...].astype(F32), grad_pre)
     table_out[...] = exact_nt(grad_pre, w1_ref[...])[:PREFIX]
 
-
-def first_back(own, other, hidden, table, w1):
+    @pl.when(spot_ref[0] == 0)
+    def _():
+        for load, store in zip(loads, stores):
+            load.wait()
+            store.start()
+
+    w1_out[...] = exact_tn(slots(table_ref, table), grad_pre)
+
+    @pl.when(spot_ref[0] == 0)
+    def _():
+        for store in stores:
+            store.wait()
+
+
+def last_block(spot, own, other, hidden, table, w1, outputs, pieces):
+    rh = w1.shape[1]
     return pl.pallas_call(
-        first_kernel,
-        in_specs=[IN_VMEM] * 5,
-        out_specs=[IN_VMEM] * 3,
+        last_kernel,
+        in_specs=[SCALARS] + [IN_VMEM] * 5 + [ANY] * 3,
+        out_specs=[IN_VMEM] * 3 + [ANY],
+        scratch_shapes=[
+            pltpu.VMEM((SLOTS, rh), F32),
+            pltpu.VMEM((SLOTS, D), F32),
+            whole_scratch(BF16),
+            pltpu.SemaphoreType.DMA((2, 2)),
+        ],
         out_shape=[
             jax.ShapeDtypeStruct((PREFIX, D), F32),
             jax.ShapeDtypeStruct(w1.shape, F32),
-            jax.ShapeDtypeStruct((1, w1.shape[1]), F32),
+            jax.ShapeDtypeStruct((1, rh), F32),
+            jax.ShapeDtypeStruct(outputs.shape, outputs.dtype),
         ],
+        input_output_aliases={6: 3},
         compiler_params=params(),
-        cost_estimate=cost(2),
-        name="first_back",
-    )(own, other, hidden, table, w1)
+        cost_estimate=cost(3),
+        name="last_block",
+    )(spot, own, other, hidden, table, w1, outputs, *pieces)
 
 
 def swap_sections(values):
@@ -1416,17 +1472,21 @@
         (grad_handed, received_grad),
     )
     pieces = [lax.ppermute(piece, "section", [(1, 0)]) for piece in pieces]
-    input_grads = place_received(spot, input_grads, pieces)
 
     kept = jnp.where(is_first, prefix_grad_first, prefix_grad_last)
     sent = jnp.where(is_first, prefix_grad_last, prefix_grad_first)
     total = sum_dp(kept + swap_sections(sent))
-    slots = lambda rows: jnp.pad(rows, ((0, SLOTS - PREFIX), (0, 0)))
-    hidden_slots, table_slots = slots(hidden_units), slots(prefix_table)
     grad_hidden = hidden_back(total, reparam_w2)
-    grad_w2, grad_b2 = second_back(total, hidden_slots)
-    grad_table, grad_w1, grad_b1 = first_back(
-        grad_hidden, swap_sections(grad_hidden), hidden_slots, table_slots, reparam_w1
+    grad_w2, grad_b2 = second_back(total, hidden_units)
+    grad_table, grad_w1, grad_b1, input_grads = last_block(
+        spot,
+        grad_hidden,
+        swap_sections(grad_hidden),
+        hidden_units,
+        prefix_table,
+        reparam_w1,
+        input_grads,
+        pieces,
     )
     return (
         activations[None],

time: 552 us -> 545 us (0.987)
    pallas_call x4 -> x3, Pallas kernels: 24.4 us -> 23.1 us  [the longest x2 17.9 us: middle_block(): pl.pallas_call(functools.partial(middle_kernel, place[1], which), in_spec...]
  transfers between devices with their start and end apart: 16 -> 16, of which waited for: 6 -> 7; matrix products, arithmetic and copies ran while one was open for 2% -> 2% of each run, Pallas kernels for 41% -> 40%
where the time goes in v4:
time: 545 us; the launch traced here: 541 us
  Pallas kernels  269 us (49%)
  waiting for transfers between devices  206 us (38%)
  starting transfers between devices  34.4 us (6%)
  between operations  14.8 us (3%)
  local copies, waits for them, and re-layouts  8.56 us (2%)
  other arithmetic  5.51 us (1%)
    all_gather x2, waiting for transfers between devices, gather_weights(): lax.all_gather(rows, ('dp', 'section'), axis=0).reshape(SHARDS, 2, -1, D)  198 us
    pallas_call x1, Pallas kernels, turn_block(): pl.pallas_call(functools.partial(turn_kernel, (attention[1], up[1], down[...  48.5 us
    pallas_call x2, Pallas kernels, attend_back(): pl.pallas_call(attend_back_kernel, grid_spec=pltpu.PrefetchScalarGridSpec...  46.4 us
    pallas_call x2, Pallas kernels, attend(): pl.pallas_call(attend_kernel, grid_spec=pltpu.PrefetchScalarGridSpec(num_...  35.9 us
    pallas_call x1, Pallas kernels, backward_block(): pl.pallas_call(functools.partial(backward_kernel, (attention[1], up[1], d...  28.2 us
    pallas_call x2, Pallas kernels, unproject(): pl.pallas_call(functools.partial(unproject_kernel, place[1], which), in_s...  27.8 us
    pallas_call x1, Pallas kernels, forward_block(): pl.pallas_call(functools.partial(forward_kernel, (up[1], down[1])), grid=...  27.1 us
    pallas_call x2, Pallas kernels, project(): pl.pallas_call(functools.partial(qkv_kernel, place[1]), grid_spec=pltpu.P...  25.5 us
  transfers between devices with their start and end apart: 16, of which 7 were waited for; matrix products, arithmetic and copies ran while one was open for 2% of the time, Pallas kernels for 40%

profile of v4, /device:TPU:0, one launch (start us, length us, event | category | flops | bytes accessed | tf_op | source)
XLA Modules:
  0.0 540.7 jit_solution(6232569806889262037)
XLA Ops:
  24.5 188.4 %all-gather.6.cloned.1.call-done = bf16[16384,1024]{1,0:T(8,128)(2,1)} async-done(((bf16[512,1024]{1,0:T(8,128)(2,1)}), bf16[16384,1024]{1,0:T(8,128)(2,1)}) %all-gather.6.cloned.1.call-update) | async-done | bytes 33554448 | tf_op jit(solution)/shard_map/all_gather | solution.py:1347
  212.9 12.5 %norm_project.2.q_ref.k_ref.v_ref = bf16[24,1024,128]{2,1,0:T(8,128)(2,1)} custom-call(s32[2]{0:T(128)} %pad_add_fusion.spot_ref, bf16[2,1024,1024]{2,1,0:T(8,128)(2,1)} %hidden_ref.5, f32[8,1024]{1,0:T(8,128)} %slice_convert_fusion.1.norm_ref, bf16[16,2,512,1024]{3,2,1,0:T(8,128)(2,1)} %bitcast.71), custom_call_target="tpu_custom_call" | custom-call | flops 13799999488 | bytes 1048576 | tf_op jit(solution)/shard_map/norm_project/pallas_call | solution.py:205
  225.4 17.9 %attend.2 = (bf16[8,1024,128]{2,1,0:T(8,128)(2,1)}, bf16[8,1040,2048]{2,1,0:T(8,128)(2,1)}, f32[8,1024,128]{2,1,0:T(8,128)}) custom-call(s32[1]{0:T(128)} %dynamic_slice.3.seq_ref, bf16[24,1024,128]{2,1,0:T(8,128)(2,1)} %norm_project.2.q_ref.k_ref.v_ref, bf16[24,1024,128]{2,1,0:T(8,128)(2,1)} %norm_project.2.q_ref.k_ref.v_ref, ...), custom_call_target="tpu_custom_call" | custom-call | flops 34500001792 | bytes 1048576 | tf_op jit(solution)/shard_map/attend/pallas_call | solution.py:356
  243.4 8.9 %middle_block.2 = (f32[1024,1024]{1,0:T(8,128)}, bf16[1024,1024]{1,0:T(8,128)(2,1)}) custom-call(s32[2]{0:T(128)} %pad_add_fusion.spot_ref, f32[8,1024]{1,0:T(8,128)} %slice_convert_fusion.1.norm_ref, bf16[8,1024,128]{2,1,0:T(8,128)(2,1)} %get-tuple-element.39.attended_ref.out_ref, bf16[2,1024,1024]{2,1,0:T(8,128)(2,1)} %hidden_ref.5, ...), custom_call_target="tpu_custom_call" | custom-call | flops 5750000128 | bytes 1048576 | tf_op jit(solution)/shard_map/middle_block/pallas_call | solution.py:577
  252.3 27.1 %forward_block.1 = (bf16[1024,4096]{1,0:T(8,128)(2,1)}, bf16[1,1024,1024]{2,1,0:T(8,128)(2,1)}) custom-call(bf16[1024,1024]{1,0:T(8,128)(2,1)} %get-tuple-element.40.normed_ref, f32[1024,1024]{1,0:T(8,128)} %get-tuple-element.41.middle_ref, bf16[16,2,512,1024]{3,2,1,0:T(8,128)(2,1)} %bitcast.73, bf16[16,2,512,1024]{3,2,1,0:T(8,128)(2,1)} %bitcast.74), custom_call_target="tpu_custom_call" | custom-call | flops 28750000128 | bytes 1048576 | tf_op jit(solution)/shard_map/forward_block/pallas_call | solution.py:680
  279.4 13.0 %norm_project.3.q_ref.k_ref.v_ref = bf16[24,1024,128]{2,1,0:T(8,128)(2,1)} custom-call(s32[2]{0:T(128)} %pad_add_fusion.spot_ref, bf16[1,1024,1024]{2,1,0:T(8,128)(2,1)} %get-tuple-element.43.hidden_ref.first_ref, f32[8,1024]{1,0:T(8,128)} %slice_convert_fusion.norm_ref, bf16[16,2,512,1024]{3,2,1,0:T(8,128)(2,1)} %bitcast.75), custom_call_target="tpu_custom_call" | custom-call | flops 13799999488 | bytes 1048576 | tf_op jit(solution)/shard_map/norm_project/pallas_call | solution.py:205
  292.4 17.9 %attend.3 = (bf16[8,1024,128]{2,1,0:T(8,128)(2,1)}, bf16[8,1040,2048]{2,1,0:T(8,128)(2,1)}, f32[8,1024,128]{2,1,0:T(8,128)}) custom-call(s32[1]{0:T(128)} %dynamic_slice.3.seq_ref, bf16[24,1024,128]{2,1,0:T(8,128)(2,1)} %norm_project.3.q_ref.k_ref.v_ref, bf16[24,1024,128]{2,1,0:T(8,128)(2,1)} %norm_project.3.q_ref.k_ref.v_ref, ...), custom_call_target="tpu_custom_call" | custom-call | flops 34500001792 | bytes 1048576 | tf_op jit(solution)/shard_map/attend/pallas_call | solution.py:356
  310.3 9.0 %middle_block.3 = (f32[1024,1024]{1,0:T(8,128)}, bf16[1024,1024]{1,0:T(8,128)(2,1)}) custom-call(s32[2]{0:T(128)} %pad_add_fusion.spot_ref, f32[8,1024]{1,0:T(8,128)} %slice_convert_fusion.norm_ref, bf16[8,1024,128]{2,1,0:T(8,128)(2,1)} %get-tuple-element.44.attended_ref.out_ref, bf16[1,1024,1024]{2,1,0:T(8,128)(2,1)} %get-tuple-element.43.hidden_ref.first_ref, ...), custom_call_target="tpu_custom_call" | custom-call | flops 5750000128 | bytes 1048576 | tf_op jit(solution)/shard_map/middle_block/pallas_call | solution.py:577
  319.3 9.6 %all-gather.4.cloned.1.call-done = bf16[32,256,1024]{2,1,0:T(8,128)(2,1)} async-done(((bf16[1,256,1024]{2,1,0:T(8,128)(2,1)}), bf16[32,256,1024]{2,1,0:T(8,128)(2,1)}) %all-gather.4.cloned.1.call-update) | async-done | bytes 16777232 | tf_op jit(solution)/shard_map/all_gather | solution.py:1347
  328.8 48.5 %turn_block.1 = (bf16[1,1024,1024]{2,1,0:T(8,128)(2,1)}, bf16[1,1024,1024]{2,1,0:T(8,128)(2,1)}, bf16[1024,1024]{1,0:T(8,128)(2,1)}, bf16[8,1024,128]{2,1,0:T(8,128)(2,1)}) custom-call(s32[2]{0:T(128)} %pad_add_fusion.spot_ref, f32[8,1024]{1,0:T(8,128)} %slice_convert_fusion.norm_ref, bf16[1024,1024]{1,0:T(8,128)(2,1)} %get-tuple-element.45.normed_ref, ...), custom_call_target="tpu_custom_call" | custom-call | flops 48299999232 | bytes 1048576 | tf_op jit(solution)/shard_map/turn_block/pallas_call | solution.py:829
  377.4 4.0 collective-permute-start.2
  381.4 23.3 %attend_back.2 = (bf16[3,8,1024,128]{3,2,1,0:T(8,128)(2,1)}, f32[8,24,128]{2,1,0:T(8,128)}) custom-call(s32[1]{0:T(128)} %dynamic_slice.3.seq_ref, bf16[24,1024,128]{2,1,0:T(8,128)(2,1)} %norm_project.3.q_ref.k_ref.v_ref, bf16[24,1024,128]{2,1,0:T(8,128)(2,1)} %norm_project.3.q_ref.k_ref.v_ref, bf16[24,1024,128]{2,1,0:T(8,128)(2,1)} %norm_project.3.q_ref.k_ref.v_ref, ...), custom_call_target="tpu_custom_call" | custom-call | flops 34500001792 | bytes 1048576 | tf_op jit(solution)/shard_map/attend_back/pallas_call | solution.py:466
  404.7 13.9 %unproject.2.upstream_ref.refs_0_ = bf16[1,1024,1024]{2,1,0:T(8,128)(2,1)} custom-call(s32[2]{0:T(128)} %pad_add_fusion.spot_ref, f32[8,1024]{1,0:T(8,128)} %slice_convert_fusion.norm_ref, bf16[3,8,1024,128]{3,2,1,0:T(8,128)(2,1)} %get-tuple-element.50.grads_ref, bf16[1,1024,1024]{2,1,0:T(8,128)(2,1)} %get-tuple-element.43.hidden_ref.first_ref, ...), custom_call_target="tpu_custom_call" | custom-call | flops 12650000384 | bytes 1048576 | tf_op jit(solution)/shard_map/unproject/pallas_call | solution.py:1135
  418.6 10.8 %collective-permute-start.11 = (bf16[1,1024,1024]{2,1,0:T(8,128)(2,1)}, bf16[1,1024,1024]{2,1,0:T(8,128)(2,1)}, u32[]{:S(2)}, u32[]{:S(2)}) collective-permute-start(bf16[1,1024,1024]{2,1,0:T(8,128)(2,1)} %unproject.2.upstream_ref.refs_0_), channel_id=1, source_target_pairs={{0,1},{2,3},{4,5},{6,7},{8,9},{10,11},{12,13},{14,15},{16,17},{18,... | collective-permute-start | bytes 6291464 | tf_op jit(solution)/shard_map/ppermute | solution.py:1452
  429.4 28.2 %backward_block.1 = (bf16[2,1024,1024]{2,1,0:T(8,128)(2,1)}, bf16[1024,1024]{1,0:T(8,128)(2,1)}, bf16[8,1024,128]{2,1,0:T(8,128)(2,1)}) custom-call(s32[2]{0:T(128)} %pad_add_fusion.spot_ref, f32[8,1024]{1,0:T(8,128)} %slice_convert_fusion.1.norm_ref, bf16[1024,4096]{1,0:T(8,128)(2,1)} %get-tuple-element.42.slope_ref, ...), custom_call_target="tpu_custom_call" | custom-call | flops 28750000128 | bytes 1048576 | tf_op jit(solution)/shard_map/backward_block/pallas_call | solution.py:976
  457.6 23.1 %attend_back.3 = (bf16[3,8,1024,128]{3,2,1,0:T(8,128)(2,1)}, f32[8,24,128]{2,1,0:T(8,128)}) custom-call(s32[1]{0:T(128)} %dynamic_slice.3.seq_ref, bf16[24,1024,128]{2,1,0:T(8,128)(2,1)} %norm_project.2.q_ref.k_ref.v_ref, bf16[24,1024,128]{2,1,0:T(8,128)(2,1)} %norm_project.2.q_ref.k_ref.v_ref, bf16[24,1024,128]{2,1,0:T(8,128)(2,1)} %norm_project.2.q_ref.k_ref.v_ref, ...), custom_call_target="tpu_custom_call" | custom-call | flops 34500001792 | bytes 1048576 | tf_op jit(solution)/shard_map/attend_back/pallas_call | solution.py:466
  480.8 6.4 %collective-permute-start.3 = (f32[8,24,128]{2,1,0:T(8,128)S(1)}, f32[8,24,128]{2,1,0:T(8,128)S(1)}, u32[]{:S(2)}, u32[]{:S(2)}) collective-permute-start(f32[8,24,128]{2,1,0:T(8,128)S(1)} %broadcast_select_fusion.5), channel_id=1, source_target_pairs={{0,1},{1,0},{2,3},{3,2},{4,5},{5,4},{6,7},{7,6},{8,9},{9,8},{10,11... | collective-permute-start | bytes 294920 | tf_op jit(solution)/shard_map/ppermute | solution.py:1323
  490.1 2.1 collective-permute-start.5
  493.5 14.0 %unproject.3 = (bf16[2,1024,1024]{2,1,0:T(8,128)(2,1)}, bf16[1,512,1024]{2,1,0:T(8,128)(2,1)}, bf16[1,512,1024]{2,1,0:T(8,128)(2,1)}) custom-call(s32[2]{0:T(128)} %pad_add_fusion.spot_ref, f32[8,1024]{1,0:T(8,128)} %slice_convert_fusion.1.norm_ref, bf16[3,8,1024,128]{3,2,1,0:T(8,128)(2,1)} %get-tuple-element.60.grads_ref, ...), custom_call_target="tpu_custom_call" | custom-call | flops 12650000384 | bytes 1048576 | tf_op jit(solution)/shard_map/unproject/pallas_call | solution.py:1135
  510.2 4.4 collective-permute-start.8
  515.7 2.8 collective-permute-done.8
  520.4 3.0 hidden_back.1.own_ref
  523.8 3.7 second_back.1
  528.4 5.2 last_block.1
  (87 shorter events, 28.3 us)
Async XLA Ops:
  7.2 3.6 copy-start.1
  7.2 205.7 %all-gather.6.cloned.1.call-start = ((), (), s32[]{:S(2)}) async-start(), calls=%async_computation.1 | async-start | bytes 34603008 | tf_op jit(solution)/shard_map/all_gather | solution.py:1347
  11.6 2.4 collective-permute-start.1
  14.2 2.2 copy-start.6
  14.3 2.2 copy-start.5
  15.3 2.7 copy-start
  15.3 313.5 %all-gather.4.cloned.1.call-start = ((), (), s32[]{:S(2)}) async-start(), calls=%async_computation | async-start | bytes 17301504 | tf_op jit(solution)/shard_map/all_gather | solution.py:1347
  16.4 2.6 copy-start.7
  16.4 2.6 copy-start.8
  16.4 3.1 copy-start.12
  19.0 1.7 collective-permute-start
  377.4 52.0 %collective-permute-start.2 = (bf16[1,1024,1024]{2,1,0:T(8,128)(2,1)}, bf16[1,1024,1024]{2,1,0:T(8,128)(2,1)}, u32[]{:S(2)}, u32[]{:S(2)}) collective-permute-start(bf16[1,1024,1024]{2,1,0:T(8,128)(2,1)} %get-tuple-element.53), channel_id=1, source_target_pairs={{0,1},{1,0},{2,3},{3,2},{4,5},{5,4},{6,7},{7,6},{8,9},{9,8},{10,11... | collective-permute-start | bytes 6291464 | tf_op jit(solution)/shard_map/ppermute | solution.py:1323
  418.6 74.9 %collective-permute-start.11 = (bf16[1,1024,1024]{2,1,0:T(8,128)(2,1)}, bf16[1,1024,1024]{2,1,0:T(8,128)(2,1)}, u32[]{:S(2)}, u32[]{:S(2)}) collective-permute-start(bf16[1,1024,1024]{2,1,0:T(8,128)(2,1)} %unproject.2.upstream_ref.refs_0_), channel_id=1, source_target_pairs={{0,1},{2,3},{4,5},{6,7},{8,9},{10,11},{12,13},{14,15},{16,17},{18,... | collective-permute-start | bytes 6291464 | tf_op jit(solution)/shard_map/ppermute | solution.py:1452
  457.6 23.1 %copy-start.3 = (f32[8,24,128]{2,1,0:T(8,128)S(1)}, f32[8,24,128]{2,1,0:T(8,128)}, u32[]{:S(2)}) copy-start(f32[8,24,128]{2,1,0:T(8,128)} %get-tuple-element.59) | copy-start | bytes 294916
  480.8 7.4 %collective-permute-start.3 = (f32[8,24,128]{2,1,0:T(8,128)S(1)}, f32[8,24,128]{2,1,0:T(8,128)S(1)}, u32[]{:S(2)}, u32[]{:S(2)}) collective-permute-start(f32[8,24,128]{2,1,0:T(8,128)S(1)} %broadcast_select_fusion.5), channel_id=1, source_target_pairs={{0,1},{1,0},{2,3},{3,2},{4,5},{5,4},{6,7},{7,6},{8,9},{9,8},{10,11... | collective-permute-start | bytes 294920 | tf_op jit(solution)/shard_map/ppermute | solution.py:1323
  489.1 21.0 %collective-permute-start.6 = (f32[8,24,128]{2,1,0:T(8,128)S(1)}, f32[8,24,128]{2,1,0:T(8,128)S(1)}, u32[]{:S(2)}, u32[]{:S(2)}) collective-permute-start(f32[8,24,128]{2,1,0:T(8,128)S(1)} %select_add_fusion), channel_id=1, source_target_pairs={{0,24},{2,26},{4,28},{6,30},{8,16},{10,18},{12,20},{14,22},{16,8},... | collective-permute-start | bytes 294920 | tf_op jit(solution)/shard_map/ppermute | solution.py:1377
  490.1 20.0 %collective-permute-start.5 = (f32[8,24,128]{2,1,0:T(8,128)S(1)}, f32[8,24,128]{2,1,0:T(8,128)S(1)}, u32[]{:S(2)}, u32[]{:S(2)}) collective-permute-start(f32[8,24,128]{2,1,0:T(8,128)S(1)} %select_add_fusion), channel_id=1, source_target_pairs={{0,16},{2,18},{4,20},{6,22},{8,24},{10,26},{12,28},{14,30},{16,0},... | collective-permute-start | bytes 294920 | tf_op jit(solution)/shard_map/ppermute | solution.py:1377
  492.2 17.9 %collective-permute-start.4 = (f32[8,24,128]{2,1,0:T(8,128)S(1)}, f32[8,24,128]{2,1,0:T(8,128)S(1)}, u32[]{:S(2)}, u32[]{:S(2)}) collective-permute-start(f32[8,24,128]{2,1,0:T(8,128)S(1)} %select_add_fusion), channel_id=1, source_target_pairs={{0,8},{2,10},{4,12},{6,14},{8,0},{10,2},{12,4},{14,6},{16,24},{18,... | collective-permute-start | bytes 294920 | tf_op jit(solution)/shard_map/ppermute | solution.py:1377
  507.5 19.9 %collective-permute-start.12 = (bf16[1,512,1024]{2,1,0:T(8,128)(2,1)}, bf16[1,512,1024]{2,1,0:T(8,128)(2,1)S(1)}, u32[]{:S(2)}, u32[]{:S(2)}) collective-permute-start(bf16[1,512,1024]{2,1,0:T(8,128)(2,1)} %get-tuple-element.63), channel_id=1, source_target_pairs={{1,0},{3,2},{5,4},{7,6},{9,8},{11,10},{13,12},{15,14},{17,16},{19,... | collective-permute-start | bytes 3145736 | tf_op jit(solution)/shard_map/ppermute | solution.py:1474
  508.8 18.7 %collective-permute-start.13 = (bf16[1,512,1024]{2,1,0:T(8,128)(2,1)}, bf16[1,512,1024]{2,1,0:T(8,128)(2,1)}, u32[]{:S(2)}, u32[]{:S(2)}) collective-permute-start(bf16[1,512,1024]{2,1,0:T(8,128)(2,1)} %get-tuple-element.64), channel_id=1, source_target_pairs={{1,0},{3,2},{5,4},{7,6},{9,8},{11,10},{13,12},{15,14},{17,16},{19,... | collective-permute-start | bytes 3145736 | tf_op jit(solution)/shard_map/ppermute | solution.py:1474
  510.1 5.6 %collective-permute-start.9 = (f32[8,24,128]{2,1,0:T(8,128)S(1)}, f32[8,24,128]{2,1,0:T(8,128)S(1)}, u32[]{:S(2)}, u32[]{:S(2)}) collective-permute-start(f32[8,24,128]{2,1,0:T(8,128)S(1)} %add_add_fusion.1), channel_id=1, source_target_pairs={{0,6},{2,4},{4,2},{6,0},{8,14},{10,12},{12,10},{14,8},{16,22},{18,... | collective-permute-start | bytes 294920 | tf_op jit(solution)/shard_map/ppermute | solution.py:1377
  510.2 8.3 %collective-permute-start.8 = (f32[8,24,128]{2,1,0:T(8,128)S(1)}, f32[8,24,128]{2,1,0:T(8,128)S(1)}, u32[]{:S(2)}, u32[]{:S(2)}) collective-permute-start(f32[8,24,128]{2,1,0:T(8,128)S(1)} %add_add_fusion.1), channel_id=1, source_target_pairs={{0,4},{2,6},{4,0},{6,2},{8,12},{10,14},{12,8},{14,10},{16,20},{18,... | collective-permute-start | bytes 294920 | tf_op jit(solution)/shard_map/ppermute | solution.py:1377
  514.6 5.1 collective-permute-start.7
  523.3 4.1 collective-permute-start.10
  (5 other events, 6.1 us)
Sparse Core Ops, SparseCore 0:
  15.5 197.4 all-gather.5
  215.8 113.0 all-gather.3

commit v5 on v4

--- a/solution.py
+++ b/solution.py
@@ -21,7 +21,6 @@
 eps_norm = 1e-05
 neg_big = -1e30
 highest_mode = lax.Precision.HIGHEST
-VMEM_BYTES = 62 * 2**20
 F32 = jnp.float32
 BF16 = jnp.bfloat16
 
@@ -74,8 +73,8 @@
     return out, slope
 
 
-def params(**kwargs):
-    return pltpu.CompilerParams(vmem_limit_bytes=VMEM_BYTES, **kwargs)
+def params(mebibytes=62):
+    return pltpu.CompilerParams(vmem_limit_bytes=mebibytes * 2**20)
 
 
 def cost(micros):
@@ -1201,7 +1200,7 @@
         out_specs=IN_VMEM,
         scratch_shapes=[pltpu.VMEM((SLOTS, 2 * D), F32)],
         out_shape=jax.ShapeDtypeStruct((SLOTS, w2.shape[1]), F32),
-        compiler_params=params(),
+        compiler_params=params(16),
         cost_estimate=cost(2),
         name="hidden_back",
     )(total, w2)
@@ -1233,7 +1232,7 @@
             jax.ShapeDtypeStruct((1, rh, 2 * D), F32),
             jax.ShapeDtypeStruct((1, 2 * D), F32),
         ],
-        compiler_params=params(),
+        compiler_params=params(16),
         cost_estimate=cost(3),
         name="second_back",
     )(total, hidden)
@@ -1313,7 +1312,7 @@
             jax.ShapeDtypeStruct(outputs.shape, outputs.dtype),
         ],
         input_output_aliases={6: 3},
-        compiler_params=params(),
+        compiler_params=params(16),
         cost_estimate=cost(3),
         name="last_block",
     )(spot, own, other, hidden, table, w1, outputs, *pieces)

time: 545 us -> 540 us (level)
  Pallas kernels: 269 us -> 292 us
  starting transfers between devices: 34.4 us -> 14.8 us
  waiting for transfers between devices: 206 us -> 197 us
    pallas_call x2, Pallas kernels: 46.4 us -> 61.3 us  [attend_back(): pl.pallas_call(attend_back_kernel, grid_spec=pltpu.PrefetchScalarGridSpec...]
    pallas_call x2, Pallas kernels: 35.9 us -> 47.8 us  [attend(): pl.pallas_call(attend_kernel, grid_spec=pltpu.PrefetchScalarGridSpec(num_...]
    ppermute x5, starting transfers between devices: 11.8 us -> 1.24 us  [swap_sections(): return lax.ppermute(values, 'section', [(0, 1), (1, 0)])]
    all_gather x2, waiting for transfers between devices: 198 us -> 189 us  [gather_weights(): lax.all_gather(rows, ('dp', 'section'), axis=0).reshape(SHARDS, 2, -1, D)]
    ppermute x1, starting transfers between devices: 10.8 us -> 2.71 us  [per_device(): received_grad = lax.ppermute(grad_handed, 'section', [(0, 1)])]
  transfers between devices with their start and end apart: 16 -> 16, of which waited for: 7 -> 5; matrix products, arithmetic and copies ran while one was open for 2% -> 2% of each run, Pallas kernels for 40% -> 45%
where the time goes in v5:
time: 540 us; the launch traced here: 535 us
  Pallas kernels  292 us (54%)
  waiting for transfers between devices  197 us (36%)
  starting transfers between devices  14.8 us (3%)
  between operations  14.8 us (3%)
  local copies, waits for them, and re-layouts  11.1 us (2%)
    all_gather x2, waiting for transfers between devices, gather_weights(): lax.all_gather(rows, ('dp', 'section'), axis=0).reshape(SHARDS, 2, -1, D)  189 us
    pallas_call x2, Pallas kernels, attend_back(): pl.pallas_call(attend_back_kernel, grid_spec=pltpu.PrefetchScalarGridSpec...  61.3 us
    pallas_call x1, Pallas kernels, turn_block(): pl.pallas_call(functools.partial(turn_kernel, (attention[1], up[1], down[...  48.5 us
    pallas_call x2, Pallas kernels, attend(): pl.pallas_call(attend_kernel, grid_spec=pltpu.PrefetchScalarGridSpec(num_...  47.8 us
    pallas_call x1, Pallas kernels, backward_block(): pl.pallas_call(functools.partial(backward_kernel, (attention[1], up[1], d...  28.2 us
    pallas_call x2, Pallas kernels, unproject(): pl.pallas_call(functools.partial(unproject_kernel, place[1], which), in_s...  27.8 us
    pallas_call x1, Pallas kernels, forward_block(): pl.pallas_call(functools.partial(forward_kernel, (up[1], down[1])), grid=...  27.1 us
    pallas_call x2, Pallas kernels, project(): pl.pallas_call(functools.partial(qkv_kernel, place[1]), grid_spec=pltpu.P...  25.5 us
  transfers between devices with their start and end apart: 16, of which 5 were waited for; matrix products, arithmetic and copies ran while one was open for 2% of the time, Pallas kernels for 45%

profile of v5, /device:TPU:0, one launch (start us, length us, event | category | flops | bytes accessed | tf_op | source)
XLA Modules:
  0.0 535.4 jit_solution(10386788702261086046)
XLA Ops:
  8.4 1.7 reshape_squeeze.6
  12.2 1.9 collective-permute-done.1
  16.4 2.0 slice.61
  25.2 188.5 %all-gather.6.cloned.1.call-done = bf16[16384,1024]{1,0:T(8,128)(2,1)} async-done(((bf16[512,1024]{1,0:T(8,128)(2,1)}), bf16[16384,1024]{1,0:T(8,128)(2,1)}) %all-gather.6.cloned.1.call-update) | async-done | bytes 33554448 | tf_op jit(solution)/shard_map/all_gather | solution.py:1346
  213.7 12.5 %norm_project.2.q_ref.k_ref.v_ref = bf16[24,1024,128]{2,1,0:T(8,128)(2,1)} custom-call(s32[2]{0:T(128)} %pad_add_fusion.spot_ref, bf16[2,1024,1024]{2,1,0:T(8,128)(2,1)} %hidden_ref.5, f32[8,1024]{1,0:T(8,128)} %slice_convert_fusion.1.norm_ref, bf16[16,2,512,1024]{3,2,1,0:T(8,128)(2,1)} %bitcast.71), custom_call_target="tpu_custom_call" | custom-call | flops 13799999488 | bytes 1048576 | tf_op jit(solution)/shard_map/norm_project/pallas_call | solution.py:204
  226.2 23.9 %attend.2 = (bf16[8,1024,128]{2,1,0:T(8,128)(2,1)}, bf16[8,1040,2048]{2,1,0:T(8,128)(2,1)}, f32[8,1024,128]{2,1,0:T(8,128)}) custom-call(s32[1]{0:T(128)} %dynamic_slice.3.seq_ref, bf16[24,1024,128]{2,1,0:T(8,128)(2,1)} %norm_project.2.q_ref.k_ref.v_ref, bf16[24,1024,128]{2,1,0:T(8,128)(2,1)} %norm_project.2.q_ref.k_ref.v_ref, ...), custom_call_target="tpu_custom_call" | custom-call | flops 34500001792 | bytes 1048576 | tf_op jit(solution)/shard_map/attend/pallas_call | solution.py:355
  250.2 8.9 %middle_block.2 = (f32[1024,1024]{1,0:T(8,128)}, bf16[1024,1024]{1,0:T(8,128)(2,1)}) custom-call(s32[2]{0:T(128)} %pad_add_fusion.spot_ref, f32[8,1024]{1,0:T(8,128)} %slice_convert_fusion.1.norm_ref, bf16[8,1024,128]{2,1,0:T(8,128)(2,1)} %get-tuple-element.39.attended_ref.out_ref, bf16[2,1024,1024]{2,1,0:T(8,128)(2,1)} %hidden_ref.5, ...), custom_call_target="tpu_custom_call" | custom-call | flops 5750000128 | bytes 1048576 | tf_op jit(solution)/shard_map/middle_block/pallas_call | solution.py:576
  259.1 27.1 %forward_block.1 = (bf16[1024,4096]{1,0:T(8,128)(2,1)}, bf16[1,1024,1024]{2,1,0:T(8,128)(2,1)}) custom-call(bf16[1024,1024]{1,0:T(8,128)(2,1)} %get-tuple-element.40.normed_ref, f32[1024,1024]{1,0:T(8,128)} %get-tuple-element.41.middle_ref, bf16[16,2,512,1024]{3,2,1,0:T(8,128)(2,1)} %bitcast.73, bf16[16,2,512,1024]{3,2,1,0:T(8,128)(2,1)} %bitcast.74), custom_call_target="tpu_custom_call" | custom-call | flops 28750000128 | bytes 1048576 | tf_op jit(solution)/shard_map/forward_block/pallas_call | solution.py:679
  286.2 13.0 %norm_project.3.q_ref.k_ref.v_ref = bf16[24,1024,128]{2,1,0:T(8,128)(2,1)} custom-call(s32[2]{0:T(128)} %pad_add_fusion.spot_ref, bf16[1,1024,1024]{2,1,0:T(8,128)(2,1)} %get-tuple-element.43.hidden_ref.first_ref, f32[8,1024]{1,0:T(8,128)} %slice_convert_fusion.norm_ref, bf16[16,2,512,1024]{3,2,1,0:T(8,128)(2,1)} %bitcast.75), custom_call_target="tpu_custom_call" | custom-call | flops 13799999488 | bytes 1048576 | tf_op jit(solution)/shard_map/norm_project/pallas_call | solution.py:204
  299.2 23.9 %attend.3 = (bf16[8,1024,128]{2,1,0:T(8,128)(2,1)}, bf16[8,1040,2048]{2,1,0:T(8,128)(2,1)}, f32[8,1024,128]{2,1,0:T(8,128)}) custom-call(s32[1]{0:T(128)} %dynamic_slice.3.seq_ref, bf16[24,1024,128]{2,1,0:T(8,128)(2,1)} %norm_project.3.q_ref.k_ref.v_ref, bf16[24,1024,128]{2,1,0:T(8,128)(2,1)} %norm_project.3.q_ref.k_ref.v_ref, ...), custom_call_target="tpu_custom_call" | custom-call | flops 34500001792 | bytes 1048576 | tf_op jit(solution)/shard_map/attend/pallas_call | solution.py:355
  323.1 9.3 %middle_block.3 = (f32[1024,1024]{1,0:T(8,128)}, bf16[1024,1024]{1,0:T(8,128)(2,1)}) custom-call(s32[2]{0:T(128)} %pad_add_fusion.spot_ref, f32[8,1024]{1,0:T(8,128)} %slice_convert_fusion.norm_ref, bf16[8,1024,128]{2,1,0:T(8,128)(2,1)} %get-tuple-element.44.attended_ref.out_ref, bf16[1,1024,1024]{2,1,0:T(8,128)(2,1)} %get-tuple-element.43.hidden_ref.first_ref, ...), custom_call_target="tpu_custom_call" | custom-call | flops 5750000128 | bytes 1048576 | tf_op jit(solution)/shard_map/middle_block/pallas_call | solution.py:576
  332.4 48.5 %turn_block.1 = (bf16[1,1024,1024]{2,1,0:T(8,128)(2,1)}, bf16[1,1024,1024]{2,1,0:T(8,128)(2,1)}, bf16[1024,1024]{1,0:T(8,128)(2,1)}, bf16[8,1024,128]{2,1,0:T(8,128)(2,1)}) custom-call(s32[2]{0:T(128)} %pad_add_fusion.spot_ref, f32[8,1024]{1,0:T(8,128)} %slice_convert_fusion.norm_ref, bf16[1024,1024]{1,0:T(8,128)(2,1)} %get-tuple-element.45.normed_ref, ...), custom_call_target="tpu_custom_call" | custom-call | flops 48299999232 | bytes 1048576 | tf_op jit(solution)/shard_map/turn_block/pallas_call | solution.py:828
  380.9 30.7 %attend_back.2 = (bf16[3,8,1024,128]{3,2,1,0:T(8,128)(2,1)}, f32[8,24,128]{2,1,0:T(8,128)}) custom-call(s32[1]{0:T(128)} %dynamic_slice.3.seq_ref, bf16[24,1024,128]{2,1,0:T(8,128)(2,1)} %norm_project.3.q_ref.k_ref.v_ref, bf16[24,1024,128]{2,1,0:T(8,128)(2,1)} %norm_project.3.q_ref.k_ref.v_ref, bf16[24,1024,128]{2,1,0:T(8,128)(2,1)} %norm_project.3.q_ref.k_ref.v_ref, ...), custom_call_target="tpu_custom_call" | custom-call | flops 34500001792 | bytes 1048576 | tf_op jit(solution)/shard_map/attend_back/pallas_call | solution.py:465
  411.7 13.9 %unproject.2.upstream_ref.refs_0_ = bf16[1,1024,1024]{2,1,0:T(8,128)(2,1)} custom-call(s32[2]{0:T(128)} %pad_add_fusion.spot_ref, f32[8,1024]{1,0:T(8,128)} %slice_convert_fusion.norm_ref, bf16[3,8,1024,128]{3,2,1,0:T(8,128)(2,1)} %get-tuple-element.50.grads_ref, bf16[1,1024,1024]{2,1,0:T(8,128)(2,1)} %get-tuple-element.43.hidden_ref.first_ref, ...), custom_call_target="tpu_custom_call" | custom-call | flops 12650000384 | bytes 1048576 | tf_op jit(solution)/shard_map/unproject/pallas_call | solution.py:1134
  425.6 2.7 collective-permute-start.11
  428.3 28.2 %backward_block.1 = (bf16[2,1024,1024]{2,1,0:T(8,128)(2,1)}, bf16[1024,1024]{1,0:T(8,128)(2,1)}, bf16[8,1024,128]{2,1,0:T(8,128)(2,1)}) custom-call(s32[2]{0:T(128)} %pad_add_fusion.spot_ref, f32[8,1024]{1,0:T(8,128)} %slice_convert_fusion.1.norm_ref, bf16[1024,4096]{1,0:T(8,128)(2,1)} %get-tuple-element.42.slope_ref, ...), custom_call_target="tpu_custom_call" | custom-call | flops 28750000128 | bytes 1048576 | tf_op jit(solution)/shard_map/backward_block/pallas_call | solution.py:975
  456.5 30.6 %attend_back.3 = (bf16[3,8,1024,128]{3,2,1,0:T(8,128)(2,1)}, f32[8,24,128]{2,1,0:T(8,128)}) custom-call(s32[1]{0:T(128)} %dynamic_slice.3.seq_ref, bf16[24,1024,128]{2,1,0:T(8,128)(2,1)} %norm_project.2.q_ref.k_ref.v_ref, bf16[24,1024,128]{2,1,0:T(8,128)(2,1)} %norm_project.2.q_ref.k_ref.v_ref, bf16[24,1024,128]{2,1,0:T(8,128)(2,1)} %norm_project.2.q_ref.k_ref.v_ref, ...), custom_call_target="tpu_custom_call" | custom-call | flops 34500001792 | bytes 1048576 | tf_op jit(solution)/shard_map/attend_back/pallas_call | solution.py:465
  491.5 2.4 collective-permute-start.4
  493.9 14.0 %unproject.3 = (bf16[2,1024,1024]{2,1,0:T(8,128)(2,1)}, bf16[1,512,1024]{2,1,0:T(8,128)(2,1)}, bf16[1,512,1024]{2,1,0:T(8,128)(2,1)}) custom-call(s32[2]{0:T(128)} %pad_add_fusion.spot_ref, f32[8,1024]{1,0:T(8,128)} %slice_convert_fusion.1.norm_ref, bf16[3,8,1024,128]{3,2,1,0:T(8,128)(2,1)} %get-tuple-element.60.grads_ref, ...), custom_call_target="tpu_custom_call" | custom-call | flops 12650000384 | bytes 1048576 | tf_op jit(solution)/shard_map/unproject/pallas_call | solution.py:1134
  511.9 2.2 collective-permute-start.7
  514.1 2.9 collective-permute-done.9
  517.0 2.3 collective-permute-done.8
  521.7 2.8 second_back.1
  524.5 3.8 last_block.1
  (93 shorter events, 23.1 us)
Async XLA Ops:
  7.2 3.6 copy-start.8
  7.2 206.5 %all-gather.6.cloned.1.call-start = ((), (), s32[]{:S(2)}) async-start(), calls=%async_computation.1 | async-start | bytes 34603008 | tf_op jit(solution)/shard_map/all_gather | solution.py:1346
  11.6 2.4 collective-permute-start.1
  15.1 3.3 copy-start.14
  15.1 3.4 copy-start.11
  15.1 3.4 copy-start.2
  15.1 3.4 copy-start.5
  16.1 2.6 copy-start
  16.2 316.2 %all-gather.4.cloned.1.call-start = ((), (), s32[]{:S(2)}) async-start(), calls=%async_computation | async-start | bytes 17301504 | tf_op jit(solution)/shard_map/all_gather | solution.py:1346
  19.8 1.7 collective-permute-start
  380.9 47.4 %collective-permute-start.2 = (bf16[1,1024,1024]{2,1,0:T(8,128)(2,1)}, bf16[1,1024,1024]{2,1,0:T(8,128)(2,1)}, u32[]{:S(2)}, u32[]{:S(2)}) collective-permute-start(bf16[1,1024,1024]{2,1,0:T(8,128)(2,1)} %get-tuple-element.53), channel_id=1, source_target_pairs={{0,1},{1,0},{2,3},{3,2},{4,5},{5,4},{6,7},{7,6},{8,9},{9,8},{10,11... | collective-permute-start | bytes 6291464 | tf_op jit(solution)/shard_map/ppermute | solution.py:1322
  425.6 68.3 %collective-permute-start.11 = (bf16[1,1024,1024]{2,1,0:T(8,128)(2,1)}, bf16[1,1024,1024]{2,1,0:T(8,128)(2,1)}, u32[]{:S(2)}, u32[]{:S(2)}) collective-permute-start(bf16[1,1024,1024]{2,1,0:T(8,128)(2,1)} %unproject.2.upstream_ref.refs_0_), channel_id=1, source_target_pairs={{0,1},{2,3},{4,5},{6,7},{8,9},{10,11},{12,13},{14,15},{16,17},{18,... | collective-permute-start | bytes 6291464 | tf_op jit(solution)/shard_map/ppermute | solution.py:1451
  456.5 30.6 %copy-start.10 = (f32[8,24,128]{2,1,0:T(8,128)S(1)}, f32[8,24,128]{2,1,0:T(8,128)}, u32[]{:S(2)}) copy-start(f32[8,24,128]{2,1,0:T(8,128)} %get-tuple-element.59) | copy-start | bytes 294916
  487.1 1.4 collective-permute-start.3
  489.4 21.0 %collective-permute-start.6 = (f32[8,24,128]{2,1,0:T(8,128)S(1)}, f32[8,24,128]{2,1,0:T(8,128)S(1)}, u32[]{:S(2)}, u32[]{:S(2)}) collective-permute-start(f32[8,24,128]{2,1,0:T(8,128)S(1)} %select_add_fusion), channel_id=1, source_target_pairs={{0,24},{2,26},{4,28},{6,30},{8,16},{10,18},{12,20},{14,22},{16,8},... | collective-permute-start | bytes 294920 | tf_op jit(solution)/shard_map/ppermute | solution.py:1376
  490.8 19.7 %collective-permute-start.5 = (f32[8,24,128]{2,1,0:T(8,128)S(1)}, f32[8,24,128]{2,1,0:T(8,128)S(1)}, u32[]{:S(2)}, u32[]{:S(2)}) collective-permute-start(f32[8,24,128]{2,1,0:T(8,128)S(1)} %select_add_fusion), channel_id=1, source_target_pairs={{0,16},{2,18},{4,20},{6,22},{8,24},{10,26},{12,28},{14,30},{16,0},... | collective-permute-start | bytes 294920 | tf_op jit(solution)/shard_map/ppermute | solution.py:1376
  491.5 19.0 %collective-permute-start.4 = (f32[8,24,128]{2,1,0:T(8,128)S(1)}, f32[8,24,128]{2,1,0:T(8,128)S(1)}, u32[]{:S(2)}, u32[]{:S(2)}) collective-permute-start(f32[8,24,128]{2,1,0:T(8,128)S(1)} %select_add_fusion), channel_id=1, source_target_pairs={{0,8},{2,10},{4,12},{6,14},{8,0},{10,2},{12,4},{14,6},{16,24},{18,... | collective-permute-start | bytes 294920 | tf_op jit(solution)/shard_map/ppermute | solution.py:1376
  507.9 16.6 %collective-permute-start.12 = (bf16[1,512,1024]{2,1,0:T(8,128)(2,1)}, bf16[1,512,1024]{2,1,0:T(8,128)(2,1)S(1)}, u32[]{:S(2)}, u32[]{:S(2)}) collective-permute-start(bf16[1,512,1024]{2,1,0:T(8,128)(2,1)} %get-tuple-element.63), channel_id=1, source_target_pairs={{1,0},{3,2},{5,4},{7,6},{9,8},{11,10},{13,12},{15,14},{17,16},{19,... | collective-permute-start | bytes 3145736 | tf_op jit(solution)/shard_map/ppermute | solution.py:1473
  509.2 15.3 %collective-permute-start.13 = (bf16[1,512,1024]{2,1,0:T(8,128)(2,1)}, bf16[1,512,1024]{2,1,0:T(8,128)(2,1)S(1)}, u32[]{:S(2)}, u32[]{:S(2)}) collective-permute-start(bf16[1,512,1024]{2,1,0:T(8,128)(2,1)} %get-tuple-element.64), channel_id=1, source_target_pairs={{1,0},{3,2},{5,4},{7,6},{9,8},{11,10},{13,12},{15,14},{17,16},{19,... | collective-permute-start | bytes 3145736 | tf_op jit(solution)/shard_map/ppermute | solution.py:1473
  510.5 6.4 %collective-permute-start.9 = (f32[8,24,128]{2,1,0:T(8,128)S(1)}, f32[8,24,128]{2,1,0:T(8,128)S(1)}, u32[]{:S(2)}, u32[]{:S(2)}) collective-permute-start(f32[8,24,128]{2,1,0:T(8,128)S(1)} %add_add_fusion.1), channel_id=1, source_target_pairs={{0,6},{2,4},{4,2},{6,0},{8,14},{10,12},{12,10},{14,8},{16,22},{18,... | collective-permute-start | bytes 294920 | tf_op jit(solution)/shard_map/ppermute | solution.py:1376
  511.9 7.3 %collective-permute-start.8 = (f32[8,24,128]{2,1,0:T(8,128)S(1)}, f32[8,24,128]{2,1,0:T(8,128)S(1)}, u32[]{:S(2)}, u32[]{:S(2)}) collective-permute-start(f32[8,24,128]{2,1,0:T(8,128)S(1)} %add_add_fusion.1), channel_id=1, source_target_pairs={{0,4},{2,6},{4,0},{6,2},{8,12},{10,14},{12,8},{14,10},{16,20},{18,... | collective-permute-start | bytes 294920 | tf_op jit(solution)/shard_map/ppermute | solution.py:1376
  511.9 7.3 %collective-permute-start.7 = (f32[8,24,128]{2,1,0:T(8,128)S(1)}, f32[8,24,128]{2,1,0:T(8,128)S(1)}, u32[]{:S(2)}, u32[]{:S(2)}) collective-permute-start(f32[8,24,128]{2,1,0:T(8,128)S(1)} %add_add_fusion.1), channel_id=1, source_target_pairs={{0,2},{2,0},{4,6},{6,4},{8,10},{10,8},{12,14},{14,12},{16,18},{18,... | collective-permute-start | bytes 294920 | tf_op jit(solution)/shard_map/ppermute | solution.py:1376
  521.6 2.9 copy-start.6
  521.6 2.9 collective-permute-start.10
  (8 other events, 10.2 us)
Sparse Core Ops, SparseCore 0:
  16.3 197.3 all-gather.5
  216.6 113.0 all-gather.3

commit v6 on v5

--- a/solution.py
+++ b/solution.py
@@ -1148,7 +1148,7 @@
         ]
         + ([pltpu.VMEM((2, D, D), BF16), pltpu.SemaphoreType.DMA((3,))] if others else []),
         out_shape=[jax.ShapeDtypeStruct((2, length, D), BF16), piece, piece] if others else row,
-        compiler_params=params(),
+        compiler_params=params(44),
         cost_estimate=cost(11),
         name="unproject",
     )(spot, norms, grads, hidden, grad_middle, place[0], *others)

time: 540 us -> 542 us (level)
  transfers between devices with their start and end apart: 16 -> 16, of which waited for: 5 -> 6; matrix products, arithmetic and copies ran while one was open for 2% -> 2% of each run, Pallas kernels for 45% -> 44%
where the time goes in v6:
time: 542 us; the launch traced here: 538 us
  Pallas kernels  290 us (54%)
  waiting for transfers between devices  197 us (36%)
  starting transfers between devices  16.1 us (3%)
  between operations  14.8 us (3%)
  local copies, waits for them, and re-layouts  14.5 us (3%)
    all_gather x2, waiting for transfers between devices, gather_weights(): lax.all_gather(rows, ('dp', 'section'), axis=0).reshape(SHARDS, 2, -1, D)  189 us
    pallas_call x2, Pallas kernels, attend_back(): pl.pallas_call(attend_back_kernel, grid_spec=pltpu.PrefetchScalarGridSpec...  60.9 us
    pallas_call x1, Pallas kernels, turn_block(): pl.pallas_call(functools.partial(turn_kernel, (attention[1], up[1], down[...  48.7 us
    pallas_call x2, Pallas kernels, attend(): pl.pallas_call(attend_kernel, grid_spec=pltpu.PrefetchScalarGridSpec(num_...  47.7 us
    pallas_call x1, Pallas kernels, backward_block(): pl.pallas_call(functools.partial(backward_kernel, (attention[1], up[1], d...  28.2 us
    pallas_call x1, Pallas kernels, forward_block(): pl.pallas_call(functools.partial(forward_kernel, (up[1], down[1])), grid=...  27.1 us
    pallas_call x2, Pallas kernels, unproject(): pl.pallas_call(functools.partial(unproject_kernel, place[1], which), in_s...  26.3 us
    pallas_call x2, Pallas kernels, project(): pl.pallas_call(functools.partial(qkv_kernel, place[1]), grid_spec=pltpu.P...  25.5 us
  transfers between devices with their start and end apart: 16, of which 6 were waited for; matrix products, arithmetic and copies ran while one was open for 2% of the time, Pallas kernels for 44%

profile of v6, /device:TPU:0, one launch (start us, length us, event | category | flops | bytes accessed | tf_op | source)
XLA Modules:
  0.0 538.4 jit_solution(5783729771298670147)
XLA Ops:
  12.2 1.9 collective-permute-done.1
  16.4 2.0 slice.61
  25.2 188.5 %all-gather.6.cloned.1.call-done = bf16[16384,1024]{1,0:T(8,128)(2,1)} async-done(((bf16[512,1024]{1,0:T(8,128)(2,1)}), bf16[16384,1024]{1,0:T(8,128)(2,1)}) %all-gather.6.cloned.1.call-update) | async-done | bytes 33554448 | tf_op jit(solution)/shard_map/all_gather | solution.py:1346
  213.7 12.5 %norm_project.2.q_ref.k_ref.v_ref = bf16[24,1024,128]{2,1,0:T(8,128)(2,1)} custom-call(s32[2]{0:T(128)} %pad_add_fusion.spot_ref, bf16[2,1024,1024]{2,1,0:T(8,128)(2,1)} %hidden_ref.5, f32[8,1024]{1,0:T(8,128)} %slice_convert_fusion.1.norm_ref, bf16[16,2,512,1024]{3,2,1,0:T(8,128)(2,1)} %bitcast.71), custom_call_target="tpu_custom_call" | custom-call | flops 13799999488 | bytes 1048576 | tf_op jit(solution)/shard_map/norm_project/pallas_call | solution.py:204
  226.2 23.9 %attend.2 = (bf16[8,1024,128]{2,1,0:T(8,128)(2,1)}, bf16[8,1040,2048]{2,1,0:T(8,128)(2,1)}, f32[8,1024,128]{2,1,0:T(8,128)}) custom-call(s32[1]{0:T(128)} %dynamic_slice.3.seq_ref, bf16[24,1024,128]{2,1,0:T(8,128)(2,1)} %norm_project.2.q_ref.k_ref.v_ref, bf16[24,1024,128]{2,1,0:T(8,128)(2,1)} %norm_project.2.q_ref.k_ref.v_ref, ...), custom_call_target="tpu_custom_call" | custom-call | flops 34500001792 | bytes 1048576 | tf_op jit(solution)/shard_map/attend/pallas_call | solution.py:355
  250.1 9.0 %middle_block.2 = (f32[1024,1024]{1,0:T(8,128)}, bf16[1024,1024]{1,0:T(8,128)(2,1)}) custom-call(s32[2]{0:T(128)} %pad_add_fusion.spot_ref, f32[8,1024]{1,0:T(8,128)} %slice_convert_fusion.1.norm_ref, bf16[8,1024,128]{2,1,0:T(8,128)(2,1)} %get-tuple-element.39.attended_ref.out_ref, bf16[2,1024,1024]{2,1,0:T(8,128)(2,1)} %hidden_ref.5, ...), custom_call_target="tpu_custom_call" | custom-call | flops 5750000128 | bytes 1048576 | tf_op jit(solution)/shard_map/middle_block/pallas_call | solution.py:576
  259.1 27.1 %forward_block.1 = (bf16[1024,4096]{1,0:T(8,128)(2,1)}, bf16[1,1024,1024]{2,1,0:T(8,128)(2,1)}) custom-call(bf16[1024,1024]{1,0:T(8,128)(2,1)} %get-tuple-element.40.normed_ref, f32[1024,1024]{1,0:T(8,128)} %get-tuple-element.41.middle_ref, bf16[16,2,512,1024]{3,2,1,0:T(8,128)(2,1)} %bitcast.73, bf16[16,2,512,1024]{3,2,1,0:T(8,128)(2,1)} %bitcast.74), custom_call_target="tpu_custom_call" | custom-call | flops 28750000128 | bytes 1048576 | tf_op jit(solution)/shard_map/forward_block/pallas_call | solution.py:679
  286.2 13.0 %norm_project.3.q_ref.k_ref.v_ref = bf16[24,1024,128]{2,1,0:T(8,128)(2,1)} custom-call(s32[2]{0:T(128)} %pad_add_fusion.spot_ref, bf16[1,1024,1024]{2,1,0:T(8,128)(2,1)} %get-tuple-element.43.hidden_ref.first_ref, f32[8,1024]{1,0:T(8,128)} %slice_convert_fusion.norm_ref, bf16[16,2,512,1024]{3,2,1,0:T(8,128)(2,1)} %bitcast.75), custom_call_target="tpu_custom_call" | custom-call | flops 13799999488 | bytes 1048576 | tf_op jit(solution)/shard_map/norm_project/pallas_call | solution.py:204
  299.2 23.8 %attend.3 = (bf16[8,1024,128]{2,1,0:T(8,128)(2,1)}, bf16[8,1040,2048]{2,1,0:T(8,128)(2,1)}, f32[8,1024,128]{2,1,0:T(8,128)}) custom-call(s32[1]{0:T(128)} %dynamic_slice.3.seq_ref, bf16[24,1024,128]{2,1,0:T(8,128)(2,1)} %norm_project.3.q_ref.k_ref.v_ref, bf16[24,1024,128]{2,1,0:T(8,128)(2,1)} %norm_project.3.q_ref.k_ref.v_ref, ...), custom_call_target="tpu_custom_call" | custom-call | flops 34500001792 | bytes 1048576 | tf_op jit(solution)/shard_map/attend/pallas_call | solution.py:355
  323.0 9.2 %middle_block.3 = (f32[1024,1024]{1,0:T(8,128)}, bf16[1024,1024]{1,0:T(8,128)(2,1)}) custom-call(s32[2]{0:T(128)} %pad_add_fusion.spot_ref, f32[8,1024]{1,0:T(8,128)} %slice_convert_fusion.norm_ref, bf16[8,1024,128]{2,1,0:T(8,128)(2,1)} %get-tuple-element.44.attended_ref.out_ref, bf16[1,1024,1024]{2,1,0:T(8,128)(2,1)} %get-tuple-element.43.hidden_ref.first_ref, ...), custom_call_target="tpu_custom_call" | custom-call | flops 5750000128 | bytes 1048576 | tf_op jit(solution)/shard_map/middle_block/pallas_call | solution.py:576
  332.3 48.7 %turn_block.1 = (bf16[1,1024,1024]{2,1,0:T(8,128)(2,1)}, bf16[1,1024,1024]{2,1,0:T(8,128)(2,1)}, bf16[1024,1024]{1,0:T(8,128)(2,1)}, bf16[8,1024,128]{2,1,0:T(8,128)(2,1)}) custom-call(s32[2]{0:T(128)} %pad_add_fusion.spot_ref, f32[8,1024]{1,0:T(8,128)} %slice_convert_fusion.norm_ref, bf16[1024,1024]{1,0:T(8,128)(2,1)} %get-tuple-element.45.normed_ref, ...), custom_call_target="tpu_custom_call" | custom-call | flops 48299999232 | bytes 1048576 | tf_op jit(solution)/shard_map/turn_block/pallas_call | solution.py:828
  381.1 30.4 %attend_back.2 = (bf16[3,8,1024,128]{3,2,1,0:T(8,128)(2,1)}, f32[8,24,128]{2,1,0:T(8,128)}) custom-call(s32[1]{0:T(128)} %dynamic_slice.3.seq_ref, bf16[24,1024,128]{2,1,0:T(8,128)(2,1)} %norm_project.3.q_ref.k_ref.v_ref, bf16[24,1024,128]{2,1,0:T(8,128)(2,1)} %norm_project.3.q_ref.k_ref.v_ref, bf16[24,1024,128]{2,1,0:T(8,128)(2,1)} %norm_project.3.q_ref.k_ref.v_ref, ...), custom_call_target="tpu_custom_call" | custom-call | flops 34500001792 | bytes 1048576 | tf_op jit(solution)/shard_map/attend_back/pallas_call | solution.py:465
  414.6 12.7 %unproject.2.upstream_ref.refs_0_ = bf16[1,1024,1024]{2,1,0:T(8,128)(2,1)} custom-call(s32[2]{0:T(128)S(1)} %copy-done.10, f32[8,1024]{1,0:T(8,128)S(1)} %copy-done.8, bf16[3,8,1024,128]{3,2,1,0:T(8,128)(2,1)} %get-tuple-element.50.grads_ref, bf16[1,1024,1024]{2,1,0:T(8,128)(2,1)S(1)} %copy-done, bf16[1024,1024]{1,0:T(8,128)(2,1)S(1)} %copy-done.12, ...), custom_call_target="tpu_custom_call" | custom-call | flops 12650000384 | bytes 1048576 | tf_op jit(solution)/shard_map/unproject/pallas_call | solution.py:1134
  427.4 2.7 collective-permute-start.11
  430.1 28.2 %backward_block.1 = (bf16[2,1024,1024]{2,1,0:T(8,128)(2,1)}, bf16[1024,1024]{1,0:T(8,128)(2,1)}, bf16[8,1024,128]{2,1,0:T(8,128)(2,1)}) custom-call(s32[2]{0:T(128)} %pad_add_fusion.spot_ref, f32[8,1024]{1,0:T(8,128)} %slice_convert_fusion.1.norm_ref, bf16[1024,4096]{1,0:T(8,128)(2,1)} %get-tuple-element.42.slope_ref, ...), custom_call_target="tpu_custom_call" | custom-call | flops 28750000128 | bytes 1048576 | tf_op jit(solution)/shard_map/backward_block/pallas_call | solution.py:975
  458.3 30.6 %attend_back.3 = (bf16[3,8,1024,128]{3,2,1,0:T(8,128)(2,1)}, f32[8,24,128]{2,1,0:T(8,128)}) custom-call(s32[1]{0:T(128)} %dynamic_slice.3.seq_ref, bf16[24,1024,128]{2,1,0:T(8,128)(2,1)} %norm_project.2.q_ref.k_ref.v_ref, bf16[24,1024,128]{2,1,0:T(8,128)(2,1)} %norm_project.2.q_ref.k_ref.v_ref, bf16[24,1024,128]{2,1,0:T(8,128)(2,1)} %norm_project.2.q_ref.k_ref.v_ref, ...), custom_call_target="tpu_custom_call" | custom-call | flops 34500001792 | bytes 1048576 | tf_op jit(solution)/shard_map/attend_back/pallas_call | solution.py:465
  492.6 2.2 collective-permute-start.5
  497.3 13.6 %unproject.3 = (bf16[2,1024,1024]{2,1,0:T(8,128)(2,1)}, bf16[1,512,1024]{2,1,0:T(8,128)(2,1)S(1)}, bf16[1,512,1024]{2,1,0:T(8,128)(2,1)S(1)}) custom-call(s32[2]{0:T(128)S(1)} %copy-done.11, f32[8,1024]{1,0:T(8,128)S(1)} %copy-done.5, bf16[3,8,1024,128]{3,2,1,0:T(8,128)(2,1)} %get-tuple-element.60.grads_ref, bf16[2,1024,1024]{2,1,0:T(8,128)(2,1)} %hidden_ref.5, ...), custom_call_target="tpu_custom_call" | custom-call | flops 12650000384 | bytes 1048576 | tf_op jit(solution)/shard_map/unproject/pallas_call | solution.py:1134
  513.5 2.1 collective-permute-start.9
  515.6 2.9 collective-permute-start.8
  519.9 2.2 collective-permute-done.8
  522.1 1.8 collective-permute-done.7
  524.7 2.8 second_back.1
  527.5 3.8 last_block.1
  (105 shorter events, 28.0 us)
Async XLA Ops:
  7.2 3.6 copy-start.14
  7.2 206.5 %all-gather.6.cloned.1.call-start = ((), (), s32[]{:S(2)}) async-start(), calls=%async_computation.1 | async-start | bytes 34603008 | tf_op jit(solution)/shard_map/all_gather | solution.py:1346
  11.6 2.4 collective-permute-start.1
  15.1 3.4 copy-start.9
  16.2 316.1 %all-gather.4.cloned.1.call-start = ((), (), s32[]{:S(2)}) async-start(), calls=%async_computation | async-start | bytes 17301504 | tf_op jit(solution)/shard_map/all_gather | solution.py:1346
  19.8 1.7 collective-permute-start
  381.0 49.1 %collective-permute-start.2 = (bf16[1,1024,1024]{2,1,0:T(8,128)(2,1)}, bf16[1,1024,1024]{2,1,0:T(8,128)(2,1)}, u32[]{:S(2)}, u32[]{:S(2)}) collective-permute-start(bf16[1,1024,1024]{2,1,0:T(8,128)(2,1)} %get-tuple-element.53), channel_id=1, source_target_pairs={{0,1},{1,0},{2,3},{3,2},{4,5},{5,4},{6,7},{7,6},{8,9},{9,8},{10,11... | collective-permute-start | bytes 6291464 | tf_op jit(solution)/shard_map/ppermute | solution.py:1322
  381.1 30.4 %copy-start.8 = (f32[8,1024]{1,0:T(8,128)S(1)}, f32[8,1024]{1,0:T(8,128)}, u32[]{:S(2)}) copy-start(f32[8,1024]{1,0:T(8,128)} %slice_convert_fusion.norm_ref) | copy-start | bytes 98308
  381.1 30.4 %copy-start.10 = (s32[2]{0:T(128)S(1)}, s32[2]{0:T(128)}, u32[]{:S(2)}) copy-start(s32[2]{0:T(128)} %pad_add_fusion.spot_ref) | copy-start | bytes 28
  427.4 68.3 %collective-permute-start.11 = (bf16[1,1024,1024]{2,1,0:T(8,128)(2,1)}, bf16[1,1024,1024]{2,1,0:T(8,128)(2,1)}, u32[]{:S(2)}, u32[]{:S(2)}) collective-permute-start(bf16[1,1024,1024]{2,1,0:T(8,128)(2,1)} %unproject.2.upstream_ref.refs_0_), channel_id=1, source_target_pairs={{0,1},{2,3},{4,5},{6,7},{8,9},{10,11},{12,13},{14,15},{16,17},{18,... | collective-permute-start | bytes 6291464 | tf_op jit(solution)/shard_map/ppermute | solution.py:1451
  458.3 30.6 %copy-start.16 = (f32[8,24,128]{2,1,0:T(8,128)S(1)}, f32[8,24,128]{2,1,0:T(8,128)}, u32[]{:S(2)}) copy-start(f32[8,24,128]{2,1,0:T(8,128)} %get-tuple-element.59) | copy-start | bytes 294916
  458.3 37.4 %copy-start.5 = (f32[8,1024]{1,0:T(8,128)S(1)}, f32[8,1024]{1,0:T(8,128)}, u32[]{:S(2)}) copy-start(f32[8,1024]{1,0:T(8,128)} %slice_convert_fusion.1.norm_ref) | copy-start | bytes 98308
  458.3 37.4 %copy-start.11 = (s32[2]{0:T(128)S(1)}, s32[2]{0:T(128)}, u32[]{:S(2)}) copy-start(s32[2]{0:T(128)} %pad_add_fusion.spot_ref) | copy-start | bytes 28
  489.0 1.4 collective-permute-start.3
  491.3 22.2 %collective-permute-start.6 = (f32[8,24,128]{2,1,0:T(8,128)S(1)}, f32[8,24,128]{2,1,0:T(8,128)S(1)}, u32[]{:S(2)}, u32[]{:S(2)}) collective-permute-start(f32[8,24,128]{2,1,0:T(8,128)S(1)} %select_add_fusion), channel_id=1, source_target_pairs={{0,24},{2,26},{4,28},{6,30},{8,16},{10,18},{12,20},{14,22},{16,8},... | collective-permute-start | bytes 294920 | tf_op jit(solution)/shard_map/ppermute | solution.py:1376
  492.6 20.8 %collective-permute-start.5 = (f32[8,24,128]{2,1,0:T(8,128)S(1)}, f32[8,24,128]{2,1,0:T(8,128)S(1)}, u32[]{:S(2)}, u32[]{:S(2)}) collective-permute-start(f32[8,24,128]{2,1,0:T(8,128)S(1)} %select_add_fusion), channel_id=1, source_target_pairs={{0,16},{2,18},{4,20},{6,22},{8,24},{10,26},{12,28},{14,30},{16,0},... | collective-permute-start | bytes 294920 | tf_op jit(solution)/shard_map/ppermute | solution.py:1376
  494.9 18.6 %collective-permute-start.4 = (f32[8,24,128]{2,1,0:T(8,128)S(1)}, f32[8,24,128]{2,1,0:T(8,128)S(1)}, u32[]{:S(2)}, u32[]{:S(2)}) collective-permute-start(f32[8,24,128]{2,1,0:T(8,128)S(1)} %select_add_fusion), channel_id=1, source_target_pairs={{0,8},{2,10},{4,12},{6,14},{8,0},{10,2},{12,4},{14,6},{16,24},{18,... | collective-permute-start | bytes 294920 | tf_op jit(solution)/shard_map/ppermute | solution.py:1376
  497.3 26.6 %copy-start.3 = (bf16[1,512,2048]{2,1,0:T(8,128)(2,1)S(1)}, bf16[1,512,2048]{2,1,0:T(8,128)(2,1)}, u32[]{:S(2)}) copy-start(bf16[1,512,2048]{2,1,0:T(8,128)(2,1)} %w2_ref.1) | copy-start | bytes 6291460
  510.9 16.6 %collective-permute-start.12 = (bf16[1,512,1024]{2,1,0:T(8,128)(2,1)S(1)}, bf16[1,512,1024]{2,1,0:T(8,128)(2,1)S(1)}, u32[]{:S(2)}, u32[]{:S(2)}) collective-permute-start(bf16[1,512,1024]{2,1,0:T(8,128)(2,1)S(1)} %get-tuple-element.63), channel_id=1, source_target_pairs={{1,0},{3,2},{5,4},{7,6},{9,8},{11,10},{13,12},{15,14},{17,16},{19,... | collective-permute-start | bytes 3145736 | tf_op jit(solution)/shard_map/ppermute | solution.py:1473
  512.2 15.3 %collective-permute-start.13 = (bf16[1,512,1024]{2,1,0:T(8,128)(2,1)S(1)}, bf16[1,512,1024]{2,1,0:T(8,128)(2,1)S(1)}, u32[]{:S(2)}, u32[]{:S(2)}) collective-permute-start(bf16[1,512,1024]{2,1,0:T(8,128)(2,1)S(1)} %get-tuple-element.64), channel_id=1, source_target_pairs={{1,0},{3,2},{5,4},{7,6},{9,8},{11,10},{13,12},{15,14},{17,16},{19,... | collective-permute-start | bytes 3145736 | tf_op jit(solution)/shard_map/ppermute | solution.py:1473
  513.5 6.3 %collective-permute-start.9 = (f32[8,24,128]{2,1,0:T(8,128)S(1)}, f32[8,24,128]{2,1,0:T(8,128)S(1)}, u32[]{:S(2)}, u32[]{:S(2)}) collective-permute-start(f32[8,24,128]{2,1,0:T(8,128)S(1)} %add_add_fusion.1), channel_id=1, source_target_pairs={{0,6},{2,4},{4,2},{6,0},{8,14},{10,12},{12,10},{14,8},{16,22},{18,... | collective-permute-start | bytes 294920 | tf_op jit(solution)/shard_map/ppermute | solution.py:1376
  515.6 6.5 %collective-permute-start.8 = (f32[8,24,128]{2,1,0:T(8,128)S(1)}, f32[8,24,128]{2,1,0:T(8,128)S(1)}, u32[]{:S(2)}, u32[]{:S(2)}) collective-permute-start(f32[8,24,128]{2,1,0:T(8,128)S(1)} %add_add_fusion.1), channel_id=1, source_target_pairs={{0,4},{2,6},{4,0},{6,2},{8,12},{10,14},{12,8},{14,10},{16,20},{18,... | collective-permute-start | bytes 294920 | tf_op jit(solution)/shard_map/ppermute | solution.py:1376
  518.5 5.4 %collective-permute-start.7 = (f32[8,24,128]{2,1,0:T(8,128)S(1)}, f32[8,24,128]{2,1,0:T(8,128)S(1)}, u32[]{:S(2)}, u32[]{:S(2)}) collective-permute-start(f32[8,24,128]{2,1,0:T(8,128)S(1)} %add_add_fusion.1), channel_id=1, source_target_pairs={{0,2},{2,0},{4,6},{6,4},{8,10},{10,8},{12,14},{14,12},{16,18},{18,... | collective-permute-start | bytes 294920 | tf_op jit(solution)/shard_map/ppermute | solution.py:1376
  524.7 2.8 collective-permute-start.10
  (14 other events, 26.1 us)
Sparse Core Ops, SparseCore 0:
  16.3 197.3 all-gather.5
  216.6 113.0 all-gather.3
